TPU v7x, 32 devices: a whole 2x2x4 slice. The times are simulated.
32 devices in a mesh: gx: 2 (over x), gy: 16 (over z, y, core).
Axes of the slice: x: 2, y: 2, z: 4, core: 2. Of those that a mesh axis runs over, the one named last changes fastest.
Arguments:
- pressure: float32 [8, 8, 2048], P('gx', None, 'gy'), may hold values from -6 to 6
- saturation: float32 [2, 8, 8, 2048], P(None, 'gx', None, 'gy'), may hold values from 0.05 to 0.45
- saturation_old: float32 [2, 8, 8, 2048], P(None, 'gx', None, 'gy'), may hold values from 0.05 to 0.45
- pore_volume: float32 [8, 8, 2048], P('gx', None, 'gy'), may hold values from 0.4 to 25.6
- permeability: float32 [8, 8, 2048], P('gx', None, 'gy'), may hold values from 0.1 to 10
- jac_diag: float32 [3, 3, 8, 8, 2048], P(None, None, 'gx', None, 'gy'), may hold values from -0.2 to 1, as said below
- jac_off: float32 [6, 3, 3, 8, 8, 2048], P(None, None, None, 'gx', None, 'gy'), may hold values from -0.05 to 0.05
- perf_cell: int32 [2, 2048], P('gx', 'gy'), may hold values from 0 to 4095
- perf_well: int32 [2, 2048], P('gx', 'gy'), may hold values from 0 to 127, as said below
- perf_index: float32 [2, 2048], P('gx', 'gy'), may hold values from 0.5 to 4
- well_rate: float32 [2, 128], P('gx', 'gy'), may hold values from 1 to 8
Outputs:
- residual: float32 [3, 8, 8, 2048], P(None, 'gx', None, 'gy')
- update: float32 [3, 8, 8, 2048], P(None, 'gx', None, 'gy')
Inputs may be any that keep to these rules, and one draw needn't show every extreme that they name: `perf_well`: every one of the 128 wells of a row (one index of gx) has at least one perforation in that row. `jac_diag`: in every 3 x 3 block each diagonal entry exceeds the sum of the magnitudes of the other entries of its row.
All inputs are finite; a program needn't handle non-finite values.
Results may differ from a plain program's by a relative error of at most 0.0003.
Values sent between devices are 32-bit elements; how exact they have to be, the bound alone decides.
No kernel may reach another device: no remote copies, remote signals or barrier semaphores. Data moves between devices by JAX's collectives and lax.ppermute only.
A program may use at most 64 MiB of HBM per device.

v0:
```python
import jax
import jax.numpy as jnp
from jax import lax
from jax.sharding import PartitionSpec as P

SWEEPS = 4


viscosity = (1.0, 2.0, 0.2)
vertical_ratio = 0.1
highest = lax.Precision.HIGHEST


def padded_2(cells, sides, width):
    for axis, dim in sides:
        count = lax.axis_size(axis)
        ends = count - 1
        head = lax.slice_in_dim(cells, 0, width, axis=dim)
        tail = lax.slice_in_dim(cells, cells.shape[dim] - width, cells.shape[dim], axis=dim)
        cells = jnp.concatenate(
            [
                lax.ppermute(tail, axis, [(i, (i + 1) % count) for i in range(ends)]),
                cells,
                lax.ppermute(head, axis, [((i + 1) % count, i) for i in range(ends)]),
            ],
            axis=dim,
        )
    return cells


def beside_all(padded):
    return [
        padded[..., :-2, 1:-1, 1:-1],
        padded[..., 2:, 1:-1, 1:-1],
        padded[..., 1:-1, 1:-1, :-2],
        padded[..., 1:-1, 1:-1, 2:],
        padded[..., 1:-1, :-2, 1:-1],
        padded[..., 1:-1, 2:, 1:-1],
    ]


def phases(sat):
    return jnp.stack([sat[0], 1.0 - sat[0] - sat[1], sat[1]])


def mobilities(water_sat, gas_sat):
    oil_sat = 1.0 - water_sat - gas_sat
    return jnp.stack(
        [
            water_sat * water_sat / viscosity[0],
            oil_sat * oil_sat / viscosity[1],
            gas_sat * gas_sat / viscosity[2],
        ]
    )


def flux_terms(center, padded):
    nearby = beside_all(padded)
    pressure_here = center[0]
    mobile = center[1:4]
    perm_here = center[4]
    summed = jnp.zeros_like(mobile)
    for facing in range(6):
        beyond = nearby[facing]
        conduct = 2.0 * perm_here * beyond[4] / (perm_here + beyond[4])
        if facing >= 4:
            conduct = vertical_ratio * conduct
        pressure_drop = pressure_here - beyond[0]
        upwind = jnp.where(pressure_drop >= 0.0, mobile, beyond[1:4])
        summed = summed + conduct * upwind * pressure_drop
    return summed


def block_solve(matrix, target):

    def cofactor(row_at, col_at):
        return (
            matrix[(row_at + 1) % 3, (col_at + 1) % 3] * matrix[(row_at + 2) % 3, (col_at + 2) % 3]
            - matrix[(row_at + 1) % 3, (col_at + 2) % 3]
            * matrix[(row_at + 2) % 3, (col_at + 1) % 3]
        )

    cofactors = [[cofactor(row_at, col_at) for col_at in range(3)] for row_at in range(3)]
    determinant = (
        matrix[0, 0] * cofactors[0][0]
        + matrix[0, 1] * cofactors[0][1]
        + matrix[0, 2] * cofactors[0][2]
    )
    solved = [
        (
            cofactors[0][col_at] * target[0]
            + cofactors[1][col_at] * target[1]
            + cofactors[2][col_at] * target[2]
        )
        / determinant
        for col_at in range(3)
    ]
    return jnp.stack(solved)


def jacobian_times(jac_diag, jac_off, values, nearby):
    local_part = jnp.einsum("abxzy,bxzy->axzy", jac_diag, values, precision=highest)
    return local_part + jnp.einsum("qabxzy,qbxzy->axzy", jac_off, nearby, precision=highest)


def edge_cells(stack):
    return padded_2(stack, (("gx", 1), ("gy", 3)), 1)


def pad_layers(stack):
    return jnp.pad(stack, ((0, 0), (0, 0), (1, 1), (0, 0)))


def near_field(stack):
    return jnp.stack(beside_all(pad_layers(edge_cells(stack))))


def precondition(vector, jac_diag, jac_off, near_fn):
    press_diag = jac_diag[0, 0] + jac_diag[1, 0] + jac_diag[2, 0]
    press_off = jac_off[:, 0, 0] + jac_off[:, 1, 0] + jac_off[:, 2, 0]
    restricted = vector[0] + vector[1] + vector[2]
    pressure_part = restricted / press_diag
    for sweep_index in range(1, SWEEPS):
        nearby = near_fn(pressure_part[None])[:, 0]
        pressure_part = (restricted - jnp.sum(press_off * nearby, axis=0)) / press_diag
    nearby = near_fn(pressure_part[None])[:, 0]
    coupled = jac_diag[:, 0] * pressure_part + jnp.sum(jac_off[:, :, 0] * nearby[:, None], axis=0)
    correction = block_solve(jac_diag, vector - coupled)
    empty = jnp.zeros_like(pressure_part)
    return correction + jnp.stack([pressure_part, empty, empty])


def global_sum(values):
    return lax.psum((values[0], values[1]), ("gx", "gy"))


def body(
    pressure,
    saturation,
    saturation_old,
    pore_volume,
    permeability,
    jac_diag,
    jac_off,
    perf_cell,
    perf_well,
    perf_index,
    well_rate,
):
    mobile = mobilities(saturation[0], saturation[1])
    center = jnp.concatenate([pressure[None], mobile, permeability[None]])
    padded = pad_layers(edge_cells(center))
    residual = pore_volume * (phases(saturation) - phases(saturation_old)) + flux_terms(
        center, padded
    )
    cells_hit = perf_cell[0]
    well_slot = perf_well[0]
    index_vals = perf_index[0]
    owned_count = well_rate.shape[1]
    row_wells = owned_count * lax.axis_size("gy")
    pressure_at = pressure.reshape(-1)[cells_hit]
    mobile_at = mobile.reshape(3, -1)[:, cells_hit]
    strength = index_vals * jnp.sum(mobile_at, axis=0)
    weighted = strength * pressure_at
    member = (well_slot[:, None] == jnp.arange(row_wells, dtype=jnp.int32)[None, :]).astype(
        jnp.float32
    )
    partial_sums = jnp.dot(jnp.stack([strength, weighted]), member, precision=highest)
    owned_sums = lax.psum_scatter(partial_sums, "gy", scatter_dimension=1, tiled=True)
    bottom = (owned_sums[1] - well_rate[0]) / owned_sums[0]
    bottom_all = lax.all_gather(bottom, "gy", axis=0, tiled=True)
    bottom_at = jnp.dot(member, bottom_all, precision=highest)
    perf_rates = index_vals * mobile_at * (pressure_at - bottom_at)
    residual = residual.reshape(3, -1).at[:, cells_hit].add(perf_rates).reshape(residual.shape)
    initial = -residual
    direction = precondition(initial, jac_diag, jac_off, near_field)
    mapped = jacobian_times(jac_diag, jac_off, direction, near_field(direction))
    along_sum, square_sum = global_sum((jnp.sum(mapped * initial), jnp.sum(mapped * mapped)))
    update = along_sum / square_sum * direction
    return (residual, update)


def solution(mesh):
    placed = (
        P("gx", None, "gy"),
        P(None, "gx", None, "gy"),
        P(None, "gx", None, "gy"),
        P("gx", None, "gy"),
        P("gx", None, "gy"),
        P(None, None, "gx", None, "gy"),
        P(None, None, None, "gx", None, "gy"),
        P("gx", "gy"),
        P("gx", "gy"),
        P("gx", "gy"),
        P("gx", "gy"),
    )
    return jax.shard_map(
        body,
        mesh=mesh,
        in_specs=placed,
        out_specs=(P(None, "gx", None, "gy"), P(None, "gx", None, "gy")),
        check_vma=False,
    )
```

profile of v0, /device:TPU:0, one launch (start us, length us, event | category | flops | bytes accessed | tf_op | source)
XLA Modules:
  0.0 210.3 jit_solution(1334989806861261582)
XLA Ops:
  0.7 0.8 constant_dynamic-update-slice_fusion.4
  1.4 0.7 slice_multiply_fusion
  2.2 0.7 constant_dynamic-update-slice_fusion.1
  2.9 0.7 constant_dynamic-update-slice_fusion
  3.6 4.8 %collective-permute-start = (f32[5,1,8,128]{3,2,1,0:T(8,128)S(1)}, f32[5,1,8,128]{3,2,1,0:T(8,128)S(1)}, u32[]{:S(2)}, u32[]{:S(2)}) collective-permute-start(f32[5,1,8,128]{3,2,1,0:T(8,128)S(1)} %get-tuple-element.50), channel_id=1, source_target_pairs={{0,16},{1,17},{2,18},{3,19},{4,20},{5,21},{6,22},{7,23},{8,24},{9,... | collective-permute-start | bytes 61448 | tf_op jit(solution)/shard_map/ppermute | solution.py:22
  8.5 1.3 collective-permute-start.1
  9.8 0.7 fusion.107
  10.5 0.7 fusion.119
  11.3 0.6 copy.41
  11.9 1.1 gather_fusion.1
  13.1 0.6 gather_fusion
  13.7 0.1 reduce_sum.71
  13.9 0.2 fusion.12
  14.1 33.2 %all-reduce.8 = f32[2,128]{1,0:T(2,128)S(1)} all-reduce(f32[2,128]{1,0:T(2,128)S(1)} %fusion.12), channel_id=3, replica_groups=mesh['gx'=2,'gy'=16] {'gy'}, use_global_device_ids=true, to_apply=%region_1.2.clone | all-reduce | flops 256 | bytes 2048
  47.3 0.6 fusion.128
  49.3 29.5 %all-reduce.7 = f32[128]{0:T(128)S(1)} all-reduce(f32[128]{0:T(128)S(1)} %bitcast_dynamic-update-slice_fusion), channel_id=2, replica_groups=mesh['gx'=2,'gy'=16] {'gy'}, use_global_device_ids=true, to_apply=%add.7 | all-reduce | flops 128 | bytes 1024 | tf_op jit(solution)/shard_map/all_gather | solution.py:171
  78.8 0.2 fusion
  79.2 1.8 collective-permute-start.2
  81.0 1.3 collective-permute-start.3
  82.3 1.9 collective-permute-done.3
  84.2 0.3 select_maximum_fusion
  84.8 0.2 fusion.20
  85.0 0.6 copy.40
  85.6 2.1 %scatter_custom_fusion = f32[3,4096]{0,1:T(8,128)S(1)} fusion(f32[3,4096]{0,1:T(8,128)S(1)} %bitcast.501, s32[128]{0:T(128)S(1)} %fusion.107, f32[128,3]{1,0:T(8,128)S(1)} %gather_fusion, f32[128]{0:T(128)S(1)} %fusion, f32[128]{0:T(128)S(1)} %bitcast.509), kind=kCustom, calls=%fused_computation.89 | custom fusion | flops 1152 | bytes 115712 | tf_op jit(solution)/shard_map/scatter-add | solution.py:174
  87.7 0.6 copy.52
  88.4 1.3 collective-permute-start.5
  89.7 4.5 %collective-permute-start.4 = (f32[1,1,8,128]{3,2,1,0:T(8,128)S(1)}, f32[1,1,8,128]{3,2,1,0:T(8,128)S(1)}, u32[]{:S(2)}, u32[]{:S(2)}) collective-permute-start(f32[1,1,8,128]{3,2,1,0:T(8,128)S(1)} %get-tuple-element.91), channel_id=1, source_target_pairs={{0,16},{1,17},{2,18},{3,19},{4,20},{5,21},{6,22},{7,23},{8,24},{9,... | collective-permute-start | bytes 12296 | tf_op jit(solution)/shard_map/ppermute | solution.py:22
  94.3 1.3 collective-permute-done.4
  95.7 1.3 collective-permute-start.7
  97.0 4.4 %collective-permute-start.6 = (f32[1,6,8,1]{3,2,1,0:T(8,128)S(1)}, f32[1,6,8,1]{3,2,1,0:T(8,128)S(1)}, u32[]{:S(2)}, u32[]{:S(2)}) collective-permute-start(f32[1,6,8,1]{3,2,1,0:T(8,128)S(1)} %get-tuple-element.81), channel_id=1, source_target_pairs={{0,1},{1,2},{2,3},{3,4},{4,5},{5,6},{6,7},{7,8},{8,9},{9,10},{10,1... | collective-permute-start | bytes 584 | tf_op jit(solution)/shard_map/ppermute | solution.py:22
  101.4 0.8 collective-permute-done.6
  102.2 0.1 select_maximum_fusion.20
  102.7 1.3 collective-permute-start.9
  104.0 4.5 %collective-permute-start.8 = (f32[1,1,8,128]{3,2,1,0:T(8,128)S(1)}, f32[1,1,8,128]{3,2,1,0:T(8,128)S(1)}, u32[]{:S(2)}, u32[]{:S(2)}) collective-permute-start(f32[1,1,8,128]{3,2,1,0:T(8,128)S(1)} %get-tuple-element.89), channel_id=1, source_target_pairs={{0,16},{1,17},{2,18},{3,19},{4,20},{5,21},{6,22},{7,23},{8,24},{9,... | collective-permute-start | bytes 12296 | tf_op jit(solution)/shard_map/ppermute | solution.py:22
  108.5 1.3 collective-permute-done.8
  109.9 1.3 collective-permute-start.11
  111.2 3.2 %collective-permute-start.10 = (f32[1,6,8,1]{3,2,1,0:T(8,128)S(1)}, f32[1,6,8,1]{3,2,1,0:T(8,128)S(1)}, u32[]{:S(2)}, u32[]{:S(2)}) collective-permute-start(f32[1,6,8,1]{3,2,1,0:T(8,128)S(1)} %get-tuple-element.79), channel_id=1, source_target_pairs={{0,1},{1,2},{2,3},{3,4},{4,5},{5,6},{6,7},{7,8},{8,9},{9,10},{10,1... | collective-permute-start | bytes 584 | tf_op jit(solution)/shard_map/ppermute | solution.py:22
  114.5 0.8 collective-permute-done.10
  115.3 0.1 select_maximum_fusion.16
  115.7 1.3 collective-permute-start.13
  117.0 4.5 %collective-permute-start.12 = (f32[1,1,8,128]{3,2,1,0:T(8,128)S(1)}, f32[1,1,8,128]{3,2,1,0:T(8,128)S(1)}, u32[]{:S(2)}, u32[]{:S(2)}) collective-permute-start(f32[1,1,8,128]{3,2,1,0:T(8,128)S(1)} %get-tuple-element.87), channel_id=1, source_target_pairs={{0,16},{1,17},{2,18},{3,19},{4,20},{5,21},{6,22},{7,23},{8,24},{9,... | collective-permute-start | bytes 12296 | tf_op jit(solution)/shard_map/ppermute | solution.py:22
  121.6 1.3 collective-permute-done.12
  123.0 1.3 collective-permute-start.15
  124.3 4.9 %collective-permute-start.14 = (f32[1,6,8,1]{3,2,1,0:T(8,128)S(1)}, f32[1,6,8,1]{3,2,1,0:T(8,128)S(1)}, u32[]{:S(2)}, u32[]{:S(2)}) collective-permute-start(f32[1,6,8,1]{3,2,1,0:T(8,128)S(1)} %get-tuple-element.77), channel_id=1, source_target_pairs={{0,1},{1,2},{2,3},{3,4},{4,5},{5,6},{6,7},{7,8},{8,9},{9,10},{10,1... | collective-permute-start | bytes 584 | tf_op jit(solution)/shard_map/ppermute | solution.py:22
  129.2 0.8 collective-permute-done.14
  130.0 0.1 select_maximum_fusion.12
  130.5 1.3 collective-permute-start.17
  131.8 4.5 %collective-permute-start.16 = (f32[1,1,8,128]{3,2,1,0:T(8,128)S(1)}, f32[1,1,8,128]{3,2,1,0:T(8,128)S(1)}, u32[]{:S(2)}, u32[]{:S(2)}) collective-permute-start(f32[1,1,8,128]{3,2,1,0:T(8,128)S(1)} %get-tuple-element.85), channel_id=1, source_target_pairs={{0,16},{1,17},{2,18},{3,19},{4,20},{5,21},{6,22},{7,23},{8,24},{9,... | collective-permute-start | bytes 12296 | tf_op jit(solution)/shard_map/ppermute | solution.py:22
  136.4 1.3 collective-permute-done.16
  137.7 1.3 collective-permute-start.19
  139.0 4.9 %collective-permute-start.18 = (f32[1,6,8,1]{3,2,1,0:T(8,128)S(1)}, f32[1,6,8,1]{3,2,1,0:T(8,128)S(1)}, u32[]{:S(2)}, u32[]{:S(2)}) collective-permute-start(f32[1,6,8,1]{3,2,1,0:T(8,128)S(1)} %get-tuple-element.75), channel_id=1, source_target_pairs={{0,1},{1,2},{2,3},{3,4},{4,5},{5,6},{6,7},{7,8},{8,9},{9,10},{10,1... | collective-permute-start | bytes 584 | tf_op jit(solution)/shard_map/ppermute | solution.py:22
  144.0 0.8 collective-permute-done.18
  144.8 0.1 select_maximum_fusion.8
  145.4 1.3 collective-permute-start.21
  146.7 4.5 %collective-permute-start.20 = (f32[3,1,8,128]{3,2,1,0:T(8,128)S(1)}, f32[3,1,8,128]{3,2,1,0:T(8,128)S(1)}, u32[]{:S(2)}, u32[]{:S(2)}) collective-permute-start(f32[3,1,8,128]{3,2,1,0:T(8,128)S(1)} %get-tuple-element.55), channel_id=1, source_target_pairs={{0,16},{1,17},{2,18},{3,19},{4,20},{5,21},{6,22},{7,23},{8,24},{9,... | collective-permute-start | bytes 36872 | tf_op jit(solution)/shard_map/ppermute | solution.py:22
  151.3 1.4 collective-permute-done.20
  152.7 1.3 collective-permute-start.23
  154.0 4.9 %collective-permute-start.22 = (f32[3,6,8,1]{3,2,1,0:T(8,128)S(1)}, f32[3,6,8,1]{3,2,1,0:T(8,128)S(1)}, u32[]{:S(2)}, u32[]{:S(2)}) collective-permute-start(f32[3,6,8,1]{3,2,1,0:T(8,128)S(1)} %get-tuple-element.53), channel_id=1, source_target_pairs={{0,1},{1,2},{2,3},{3,4},{4,5},{5,6},{6,7},{7,8},{8,9},{9,10},{10,1... | collective-permute-start | bytes 1736 | tf_op jit(solution)/shard_map/ppermute | solution.py:22
  159.0 0.9 collective-permute-done.22
  159.9 0.2 select_maximum_fusion.4
  160.4 0.1 multiply_reduce_fusion
  160.5 0.7 fusion.43
  161.2 47.2 %all-reduce.9 = (f32[]{:T(128)}, f32[]{:T(128)}) all-reduce(f32[]{:T(128)} %get-tuple-element.9, f32[]{:T(128)} %get-tuple-element.8), channel_id=1, replica_groups=mesh['gx'=2,'gy'=16] {'gx','gy'}, use_global_device_ids=true, to_apply=%region_8.9 | all-reduce | flops 2 | bytes 16 | tf_op jit(solution)/shard_map/psum | solution.py:134
  209.7 0.6 broadcast_multiply_fusion
  (108 shorter events, 3.0 us)
Async XLA Ops:
  0.6 46.6 %copy-start.6 = (u32[32]{0:T(128)S(1)}, u32[32]{0:T(128)}, u32[]{:S(2)}) copy-start(u32[32]{0:T(128)} %constant.41) | copy-start | bytes 388
  0.6 11.3 %copy-start = (f32[4,8,128]{2,1,0:T(8,128)S(1)}, f32[4,8,128]{2,1,0:T(8,128)}, u32[]{:S(2)}) copy-start(f32[4,8,128]{2,1,0:T(8,128)} %param.11) | copy-start | bytes 49156
  0.7 13.2 %copy-start.7 = (f32[1,128]{1,0:T(1,128)S(1)}, f32[1,128]{1,0:T(1,128)}, u32[]{:S(2)}) copy-start(f32[1,128]{1,0:T(1,128)} %param.20) | copy-start | bytes 1540
  0.7 13.2 %copy-start.9 = (s32[1,128]{1,0:T(1,128)S(1)}, s32[1,128]{1,0:T(1,128)}, u32[]{:S(2)}) copy-start(s32[1,128]{1,0:T(1,128)} %param.19) | copy-start | bytes 1540
  0.7 48.6 %copy-start.8 = (f32[1,8]{1,0:T(1,128)S(1)}, f32[1,8]{1,0:T(1,128)}, u32[]{:S(2)}) copy-start(f32[1,8]{1,0:T(1,128)} %param.21) | copy-start | bytes 100
  3.6 75.4 %collective-permute-start = (f32[5,1,8,128]{3,2,1,0:T(8,128)S(1)}, f32[5,1,8,128]{3,2,1,0:T(8,128)S(1)}, u32[]{:S(2)}, u32[]{:S(2)}) collective-permute-start(f32[5,1,8,128]{3,2,1,0:T(8,128)S(1)} %get-tuple-element.50), channel_id=1, source_target_pairs={{0,16},{1,17},{2,18},{3,19},{4,20},{5,21},{6,22},{7,23},{8,24},{9,... | collective-permute-start | bytes 61448 | tf_op jit(solution)/shard_map/ppermute | solution.py:22
  8.5 70.6 %collective-permute-start.1 = (f32[5,1,8,128]{3,2,1,0:T(8,128)S(1)}, f32[5,1,8,128]{3,2,1,0:T(8,128)S(1)}, u32[]{:S(2)}, u32[]{:S(2)}) collective-permute-start(f32[5,1,8,128]{3,2,1,0:T(8,128)S(1)} %get-tuple-element.51), channel_id=1, source_target_pairs={{16,0},{17,1},{18,2},{19,3},{20,4},{21,5},{22,6},{23,7},{24,8},{25... | collective-permute-start | bytes 61448 | tf_op jit(solution)/shard_map/ppermute | solution.py:24
  11.9 72.7 %copy-start.4 = (f32[4,8,128]{2,1,0:T(8,128)S(1)}, f32[4,8,128]{2,1,0:T(8,128)}, u32[]{:S(2)}) copy-start(f32[4,8,128]{2,1,0:T(8,128)} %param.15) | copy-start | bytes 49156
  11.9 72.9 %copy-start.5 = (f32[4,8,128]{2,1,0:T(8,128)S(1)}, f32[4,8,128]{2,1,0:T(8,128)}, u32[]{:S(2)}) copy-start(f32[4,8,128]{2,1,0:T(8,128)} %param.14) | copy-start | bytes 49156
  79.2 3.1 %collective-permute-start.2 = (f32[5,6,8,1]{3,2,1,0:T(8,128)S(1)}, f32[5,6,8,1]{3,2,1,0:T(8,128)S(1)}, u32[]{:S(2)}, u32[]{:S(2)}) collective-permute-start(f32[5,6,8,1]{3,2,1,0:T(8,128)S(1)} %get-tuple-element.44), channel_id=1, source_target_pairs={{0,1},{1,2},{2,3},{3,4},{4,5},{5,6},{6,7},{7,8},{8,9},{9,10},{10,1... | collective-permute-start | bytes 2888 | tf_op jit(solution)/shard_map/ppermute | solution.py:22
  81.0 3.2 %collective-permute-start.3 = (f32[5,6,8,1]{3,2,1,0:T(8,128)S(1)}, f32[5,6,8,1]{3,2,1,0:T(8,128)S(1)}, u32[]{:S(2)}, u32[]{:S(2)}) collective-permute-start(f32[5,6,8,1]{3,2,1,0:T(8,128)S(1)} %get-tuple-element.45), channel_id=1, source_target_pairs={{1,0},{2,1},{3,2},{4,3},{5,4},{6,5},{7,6},{8,7},{9,8},{10,9},{11,1... | collective-permute-start | bytes 2888 | tf_op jit(solution)/shard_map/ppermute | solution.py:24
  85.6 2.8 %copy-start.1 = (f32[3,3,4,8,128]{4,3,2,1,0:T(8,128)S(1)}, f32[3,3,4,8,128]{4,3,2,1,0:T(8,128)}, u32[]{:S(2)}) copy-start(f32[3,3,4,8,128]{4,3,2,1,0:T(8,128)} %param.16) | copy-start | bytes 442372
  85.6 17.0 %copy-start.2 = (f32[6,3,3,4,8,128]{5,4,3,2,1,0:T(8,128)S(1)}, f32[6,3,3,4,8,128]{5,4,3,2,1,0:T(8,128)}, u32[]{:S(2)}) copy-start(f32[6,3,3,4,8,128]{5,4,3,2,1,0:T(8,128)} %param.17) | copy-start | bytes 2654212
  88.4 72.2 %copy-start.3 = (f32[3,4,8,128]{3,2,1,0:T(8,128)}, f32[3,4,8,128]{3,2,1,0:T(8,128)S(1)}, u32[]{:S(2)}) copy-start(f32[3,4,8,128]{3,2,1,0:T(8,128)S(1)} %copy.52) | copy-start | bytes 147460
  88.4 5.9 %collective-permute-start.5 = (f32[1,1,8,128]{3,2,1,0:T(8,128)S(1)}, f32[1,1,8,128]{3,2,1,0:T(8,128)S(1)}, u32[]{:S(2)}, u32[]{:S(2)}) collective-permute-start(f32[1,1,8,128]{3,2,1,0:T(8,128)S(1)} %get-tuple-element.90), channel_id=1, source_target_pairs={{16,0},{17,1},{18,2},{19,3},{20,4},{21,5},{22,6},{23,7},{24,8},{25... | collective-permute-start | bytes 12296 | tf_op jit(solution)/shard_map/ppermute | solution.py:24
  89.7 5.9 %collective-permute-start.4 = (f32[1,1,8,128]{3,2,1,0:T(8,128)S(1)}, f32[1,1,8,128]{3,2,1,0:T(8,128)S(1)}, u32[]{:S(2)}, u32[]{:S(2)}) collective-permute-start(f32[1,1,8,128]{3,2,1,0:T(8,128)S(1)} %get-tuple-element.91), channel_id=1, source_target_pairs={{0,16},{1,17},{2,18},{3,19},{4,20},{5,21},{6,22},{7,23},{8,24},{9,... | collective-permute-start | bytes 12296 | tf_op jit(solution)/shard_map/ppermute | solution.py:22
  95.7 5.7 %collective-permute-start.7 = (f32[1,6,8,1]{3,2,1,0:T(8,128)S(1)}, f32[1,6,8,1]{3,2,1,0:T(8,128)S(1)}, u32[]{:S(2)}, u32[]{:S(2)}) collective-permute-start(f32[1,6,8,1]{3,2,1,0:T(8,128)S(1)} %get-tuple-element.80), channel_id=1, source_target_pairs={{1,0},{2,1},{3,2},{4,3},{5,4},{6,5},{7,6},{8,7},{9,8},{10,9},{11,1... | collective-permute-start | bytes 584 | tf_op jit(solution)/shard_map/ppermute | solution.py:24
  97.0 5.2 %collective-permute-start.6 = (f32[1,6,8,1]{3,2,1,0:T(8,128)S(1)}, f32[1,6,8,1]{3,2,1,0:T(8,128)S(1)}, u32[]{:S(2)}, u32[]{:S(2)}) collective-permute-start(f32[1,6,8,1]{3,2,1,0:T(8,128)S(1)} %get-tuple-element.81), channel_id=1, source_target_pairs={{0,1},{1,2},{2,3},{3,4},{4,5},{5,6},{6,7},{7,8},{8,9},{9,10},{10,1... | collective-permute-start | bytes 584 | tf_op jit(solution)/shard_map/ppermute | solution.py:22
  102.7 5.9 %collective-permute-start.9 = (f32[1,1,8,128]{3,2,1,0:T(8,128)S(1)}, f32[1,1,8,128]{3,2,1,0:T(8,128)S(1)}, u32[]{:S(2)}, u32[]{:S(2)}) collective-permute-start(f32[1,1,8,128]{3,2,1,0:T(8,128)S(1)} %get-tuple-element.88), channel_id=1, source_target_pairs={{16,0},{17,1},{18,2},{19,3},{20,4},{21,5},{22,6},{23,7},{24,8},{25... | collective-permute-start | bytes 12296 | tf_op jit(solution)/shard_map/ppermute | solution.py:24
  104.0 5.9 %collective-permute-start.8 = (f32[1,1,8,128]{3,2,1,0:T(8,128)S(1)}, f32[1,1,8,128]{3,2,1,0:T(8,128)S(1)}, u32[]{:S(2)}, u32[]{:S(2)}) collective-permute-start(f32[1,1,8,128]{3,2,1,0:T(8,128)S(1)} %get-tuple-element.89), channel_id=1, source_target_pairs={{0,16},{1,17},{2,18},{3,19},{4,20},{5,21},{6,22},{7,23},{8,24},{9,... | collective-permute-start | bytes 12296 | tf_op jit(solution)/shard_map/ppermute | solution.py:22
  109.9 4.6 %collective-permute-start.11 = (f32[1,6,8,1]{3,2,1,0:T(8,128)S(1)}, f32[1,6,8,1]{3,2,1,0:T(8,128)S(1)}, u32[]{:S(2)}, u32[]{:S(2)}) collective-permute-start(f32[1,6,8,1]{3,2,1,0:T(8,128)S(1)} %get-tuple-element.78), channel_id=1, source_target_pairs={{1,0},{2,1},{3,2},{4,3},{5,4},{6,5},{7,6},{8,7},{9,8},{10,9},{11,1... | collective-permute-start | bytes 584 | tf_op jit(solution)/shard_map/ppermute | solution.py:24
  111.2 4.1 %collective-permute-start.10 = (f32[1,6,8,1]{3,2,1,0:T(8,128)S(1)}, f32[1,6,8,1]{3,2,1,0:T(8,128)S(1)}, u32[]{:S(2)}, u32[]{:S(2)}) collective-permute-start(f32[1,6,8,1]{3,2,1,0:T(8,128)S(1)} %get-tuple-element.79), channel_id=1, source_target_pairs={{0,1},{1,2},{2,3},{3,4},{4,5},{5,6},{6,7},{7,8},{8,9},{9,10},{10,1... | collective-permute-start | bytes 584 | tf_op jit(solution)/shard_map/ppermute | solution.py:22
  115.7 5.9 %collective-permute-start.13 = (f32[1,1,8,128]{3,2,1,0:T(8,128)S(1)}, f32[1,1,8,128]{3,2,1,0:T(8,128)S(1)}, u32[]{:S(2)}, u32[]{:S(2)}) collective-permute-start(f32[1,1,8,128]{3,2,1,0:T(8,128)S(1)} %get-tuple-element.86), channel_id=1, source_target_pairs={{16,0},{17,1},{18,2},{19,3},{20,4},{21,5},{22,6},{23,7},{24,8},{25... | collective-permute-start | bytes 12296 | tf_op jit(solution)/shard_map/ppermute | solution.py:24
  117.0 5.9 %collective-permute-start.12 = (f32[1,1,8,128]{3,2,1,0:T(8,128)S(1)}, f32[1,1,8,128]{3,2,1,0:T(8,128)S(1)}, u32[]{:S(2)}, u32[]{:S(2)}) collective-permute-start(f32[1,1,8,128]{3,2,1,0:T(8,128)S(1)} %get-tuple-element.87), channel_id=1, source_target_pairs={{0,16},{1,17},{2,18},{3,19},{4,20},{5,21},{6,22},{7,23},{8,24},{9,... | collective-permute-start | bytes 12296 | tf_op jit(solution)/shard_map/ppermute | solution.py:22
  123.0 6.3 %collective-permute-start.15 = (f32[1,6,8,1]{3,2,1,0:T(8,128)S(1)}, f32[1,6,8,1]{3,2,1,0:T(8,128)S(1)}, u32[]{:S(2)}, u32[]{:S(2)}) collective-permute-start(f32[1,6,8,1]{3,2,1,0:T(8,128)S(1)} %get-tuple-element.76), channel_id=1, source_target_pairs={{1,0},{2,1},{3,2},{4,3},{5,4},{6,5},{7,6},{8,7},{9,8},{10,9},{11,1... | collective-permute-start | bytes 584 | tf_op jit(solution)/shard_map/ppermute | solution.py:24
  124.3 5.8 %collective-permute-start.14 = (f32[1,6,8,1]{3,2,1,0:T(8,128)S(1)}, f32[1,6,8,1]{3,2,1,0:T(8,128)S(1)}, u32[]{:S(2)}, u32[]{:S(2)}) collective-permute-start(f32[1,6,8,1]{3,2,1,0:T(8,128)S(1)} %get-tuple-element.77), channel_id=1, source_target_pairs={{0,1},{1,2},{2,3},{3,4},{4,5},{5,6},{6,7},{7,8},{8,9},{9,10},{10,1... | collective-permute-start | bytes 584 | tf_op jit(solution)/shard_map/ppermute | solution.py:22
  130.5 5.9 %collective-permute-start.17 = (f32[1,1,8,128]{3,2,1,0:T(8,128)S(1)}, f32[1,1,8,128]{3,2,1,0:T(8,128)S(1)}, u32[]{:S(2)}, u32[]{:S(2)}) collective-permute-start(f32[1,1,8,128]{3,2,1,0:T(8,128)S(1)} %get-tuple-element.84), channel_id=1, source_target_pairs={{16,0},{17,1},{18,2},{19,3},{20,4},{21,5},{22,6},{23,7},{24,8},{25... | collective-permute-start | bytes 12296 | tf_op jit(solution)/shard_map/ppermute | solution.py:24
  131.8 5.9 %collective-permute-start.16 = (f32[1,1,8,128]{3,2,1,0:T(8,128)S(1)}, f32[1,1,8,128]{3,2,1,0:T(8,128)S(1)}, u32[]{:S(2)}, u32[]{:S(2)}) collective-permute-start(f32[1,1,8,128]{3,2,1,0:T(8,128)S(1)} %get-tuple-element.85), channel_id=1, source_target_pairs={{0,16},{1,17},{2,18},{3,19},{4,20},{5,21},{6,22},{7,23},{8,24},{9,... | collective-permute-start | bytes 12296 | tf_op jit(solution)/shard_map/ppermute | solution.py:22
  137.7 6.3 %collective-permute-start.19 = (f32[1,6,8,1]{3,2,1,0:T(8,128)S(1)}, f32[1,6,8,1]{3,2,1,0:T(8,128)S(1)}, u32[]{:S(2)}, u32[]{:S(2)}) collective-permute-start(f32[1,6,8,1]{3,2,1,0:T(8,128)S(1)} %get-tuple-element.74), channel_id=1, source_target_pairs={{1,0},{2,1},{3,2},{4,3},{5,4},{6,5},{7,6},{8,7},{9,8},{10,9},{11,1... | collective-permute-start | bytes 584 | tf_op jit(solution)/shard_map/ppermute | solution.py:24
  139.0 5.8 %collective-permute-start.18 = (f32[1,6,8,1]{3,2,1,0:T(8,128)S(1)}, f32[1,6,8,1]{3,2,1,0:T(8,128)S(1)}, u32[]{:S(2)}, u32[]{:S(2)}) collective-permute-start(f32[1,6,8,1]{3,2,1,0:T(8,128)S(1)} %get-tuple-element.75), channel_id=1, source_target_pairs={{0,1},{1,2},{2,3},{3,4},{4,5},{5,6},{6,7},{7,8},{8,9},{9,10},{10,1... | collective-permute-start | bytes 584 | tf_op jit(solution)/shard_map/ppermute | solution.py:22
  145.4 5.9 %collective-permute-start.21 = (f32[3,1,8,128]{3,2,1,0:T(8,128)S(1)}, f32[3,1,8,128]{3,2,1,0:T(8,128)S(1)}, u32[]{:S(2)}, u32[]{:S(2)}) collective-permute-start(f32[3,1,8,128]{3,2,1,0:T(8,128)S(1)} %get-tuple-element.54), channel_id=1, source_target_pairs={{16,0},{17,1},{18,2},{19,3},{20,4},{21,5},{22,6},{23,7},{24,8},{25... | collective-permute-start | bytes 36872 | tf_op jit(solution)/shard_map/ppermute | solution.py:24
  146.7 5.9 %collective-permute-start.20 = (f32[3,1,8,128]{3,2,1,0:T(8,128)S(1)}, f32[3,1,8,128]{3,2,1,0:T(8,128)S(1)}, u32[]{:S(2)}, u32[]{:S(2)}) collective-permute-start(f32[3,1,8,128]{3,2,1,0:T(8,128)S(1)} %get-tuple-element.55), channel_id=1, source_target_pairs={{0,16},{1,17},{2,18},{3,19},{4,20},{5,21},{6,22},{7,23},{8,24},{9,... | collective-permute-start | bytes 36872 | tf_op jit(solution)/shard_map/ppermute | solution.py:22
  152.7 6.3 %collective-permute-start.23 = (f32[3,6,8,1]{3,2,1,0:T(8,128)S(1)}, f32[3,6,8,1]{3,2,1,0:T(8,128)S(1)}, u32[]{:S(2)}, u32[]{:S(2)}) collective-permute-start(f32[3,6,8,1]{3,2,1,0:T(8,128)S(1)} %get-tuple-element.52), channel_id=1, source_target_pairs={{1,0},{2,1},{3,2},{4,3},{5,4},{6,5},{7,6},{8,7},{9,8},{10,9},{11,1... | collective-permute-start | bytes 1736 | tf_op jit(solution)/shard_map/ppermute | solution.py:24
  154.0 5.8 %collective-permute-start.22 = (f32[3,6,8,1]{3,2,1,0:T(8,128)S(1)}, f32[3,6,8,1]{3,2,1,0:T(8,128)S(1)}, u32[]{:S(2)}, u32[]{:S(2)}) collective-permute-start(f32[3,6,8,1]{3,2,1,0:T(8,128)S(1)} %get-tuple-element.53), channel_id=1, source_target_pairs={{0,1},{1,2},{2,3},{3,4},{4,5},{5,6},{6,7},{7,8},{8,9},{9,10},{10,1... | collective-permute-start | bytes 1736 | tf_op jit(solution)/shard_map/ppermute | solution.py:22
where the time goes:
time: 212 us; the launch traced here: 210 us
  blocking collectives  110 us (52%)
  starting transfers between devices  67.2 us (32%)
  waiting for transfers between devices  12.6 us (6%)
  other arithmetic  9.13 us (4%)
  local copies, waits for them, and re-layouts  7.14 us (3%)
  between operations  4.03 us (2%)
    ppermute x12, starting transfers between devices, padded_2(): lax.ppermute(tail, axis, [(i, (i + 1) % count) for i in range(ends)])  51.7 us
    psum x1, blocking collectives, global_sum(): return lax.psum((values[0], values[1]), ('gx', 'gy'))  47.2 us
    unnamed x1, blocking collectives  33.2 us
    all_gather x1, blocking collectives, body(): bottom_all = lax.all_gather(bottom, 'gy', axis=0, tiled=True)  29.5 us
    ppermute x12, starting transfers between devices, padded_2(): lax.ppermute(head, axis, [((i + 1) % count, i) for i in range(ends)])  15.5 us
    ppermute x12, waiting for transfers between devices, padded_2(): lax.ppermute(tail, axis, [(i, (i + 1) % count) for i in range(ends)])  10.6 us
  transfers between devices with their start and end apart: 24, of which 11 were waited for; matrix products, arithmetic and copies ran while one was open for 2% of the time, Pallas kernels for 0%

commit v1 on v0

v1 whole, which is shorter than its diff:
```python
import functools

import jax
import jax.numpy as jnp
from jax import lax
from jax.experimental import pallas as pl
from jax.experimental.pallas import tpu as pltpu
from jax.sharding import PartitionSpec as P

SWEEPS = 4
WIDE = SWEEPS + 2

viscosity = (1.0, 2.0, 0.2)
vertical_ratio = 0.1
highest = lax.Precision.HIGHEST
f32 = jnp.float32

PRESS, MOB, PERM, ACC, INV, COEF = 0, 1, 4, 5, 8, 9
BULK = 15
DINV, DCOL, OFFC = 0, 9, 12
EDGE = 30
EDGE_AT = BULK * WIDE
NT = (((1,), (1,)), ((), ()))
NN = (((1,), (0,)), ((), ()))


def iota(shape, axis):
    return lax.broadcasted_iota(jnp.int32, shape, axis)


def split_dot(values, hot, dims):
    rows = values.shape[0]
    high = values.astype(jnp.bfloat16)
    rest = values - high.astype(f32)
    mid = rest.astype(jnp.bfloat16)
    low = (rest - mid.astype(f32)).astype(jnp.bfloat16)
    parts = jnp.concatenate([high, mid, low], axis=0)
    out = lax.dot_general(parts, hot, dims, preferred_element_type=f32)
    return out[:rows] + (out[rows : 2 * rows] + out[2 * rows :])


def hot_of(condition):
    return jnp.where(condition, 1.0, 0.0).astype(jnp.bfloat16)


def window(count, cx):
    reach = -(-WIDE // cx)
    if count <= 2 * reach + 1:
        return list(range(count))
    return list(range(reach + 1)) + list(range(-reach, 0))


def before_kernel(
    count_x,
    count_y,
    press_ref,
    sat_ref,
    old_ref,
    pore_ref,
    perm_ref,
    diag_ref,
    off_ref,
    cell_ref,
    well_ref,
    index_ref,
    rate_ref,
    wells_out,
    block_out,
    ya_out,
    yb_out,
    dinv_out,
):
    cx, nz, cy = press_ref.shape
    at_x = lax.axis_index("gx")
    at_y = lax.axis_index("gy")
    layers = 1 if count_x == 2 else 2
    last = block_out.shape[0] - 1

    press = press_ref[...]
    water, gas = sat_ref[0], sat_ref[1]
    oil = 1.0 - water - gas
    mobile = [
        water * water / viscosity[0],
        oil * oil / viscosity[1],
        gas * gas / viscosity[2],
    ]

    cells = cell_ref[...]
    perfs = cells.shape[1]
    spot_xz = lax.div(cells, cy)
    spot_y = lax.rem(cells, cy)
    stacked = jnp.concatenate([m.reshape(cx * nz, cy) for m in mobile + [press]], axis=0)
    hot_y = hot_of(iota((cy, perfs), 0) == spot_y)
    picked = split_dot(stacked, hot_y, NN).reshape(4, cx * nz, perfs)
    on_xz = iota((cx * nz, perfs), 0) == spot_xz
    at_perf = [
        jnp.sum(jnp.where(on_xz, picked[i], 0.0), axis=0, keepdims=True) for i in range(4)
    ]
    index_vals = index_ref[...]
    parts = [index_vals * at_perf[i] for i in range(3)]
    strength = index_vals * (at_perf[0] + at_perf[1] + at_perf[2])
    weighted = strength * at_perf[3]
    row = iota((8, perfs), 0)
    both = jnp.where(row == 0, strength, jnp.where(row == 1, weighted, 0.0))
    wells = wells_out.shape[2]
    member = jnp.where(iota((wells, perfs), 0) == well_ref[...], 1.0, 0.0)
    sums = lax.dot_general(both, member, NT, precision=highest, preferred_element_type=f32)
    owned = rate_ref.shape[1]
    square = jnp.broadcast_to(rate_ref[...], (owned, owned))
    column = jnp.sum(
        jnp.where(iota((owned, owned), 0) == iota((owned, owned), 1), square, 0.0),
        axis=1,
        keepdims=True,
    )
    mine = iota((owned, wells), 1) == at_y * owned + iota((owned, wells), 0)
    rates = jnp.sum(jnp.where(mine, column, 0.0), axis=0, keepdims=True)
    pair = sums[:2] - jnp.where(iota((2, wells), 0) == 1, rates, 0.0)
    wells_out[...] = jnp.broadcast_to(pair[None], wells_out.shape)

    perf_rows = [
        spot_xz.astype(f32),
        spot_y.astype(f32),
        well_ref[...].astype(f32),
        *parts,
        at_perf[3],
        jnp.zeros_like(at_perf[3]),
    ]
    for r, values in enumerate(perf_rows):
        block_out[last, r : r + 1, :] = values
        ya_out[cx, r : r + 1, :] = values
        yb_out[cx, r : r + 1, :] = values

    old_water, old_gas = old_ref[0], old_ref[1]
    old_oil = 1.0 - old_water - old_gas
    pore = pore_ref[...]
    accumulated = [pore * (water - old_water), pore * (oil - old_oil), pore * (gas - old_gas)]
    layer_at = iota((cx, nz, cy), 1)
    columns = [[off_ref[q, c, 0] for c in range(3)] for q in range(6)]
    columns[4] = [jnp.where(layer_at > 0, v, 0.0) for v in columns[4]]
    columns[5] = [jnp.where(layer_at < nz - 1, v, 0.0) for v in columns[5]]
    diag = [[diag_ref[a, b] for b in range(3)] for a in range(3)]
    inverse = 1.0 / (diag[0][0] + diag[1][0] + diag[2][0])
    coefs = [(columns[q][0] + columns[q][1] + columns[q][2]) * inverse for q in range(6)]
    bulk = [press, *mobile, perm_ref[...], *accumulated, inverse, *coefs]

    def cofactor(a, b):
        return (
            diag[(a + 1) % 3][(b + 1) % 3] * diag[(a + 2) % 3][(b + 2) % 3]
            - diag[(a + 1) % 3][(b + 2) % 3] * diag[(a + 2) % 3][(b + 1) % 3]
        )

    cofactors = [[cofactor(a, b) for b in range(3)] for a in range(3)]
    over = 1.0 / (
        diag[0][0] * cofactors[0][0] + diag[0][1] * cofactors[0][1] + diag[0][2] * cofactors[0][2]
    )
    solve = [cofactors[b][a] * over for a in range(3) for b in range(3)]
    for i in range(9):
        dinv_out[i] = solve[i]
    edge = solve + [diag[c][0] for c in range(3)] + [columns[q][c] for q in range(6) for c in range(3)]

    for f in range(BULK):
        block_out[f * cx : (f + 1) * cx] = bulk[f]
    base = BULK * cx
    for e in range(EDGE):
        if layers == 1:
            block_out[base + e] = jnp.where(at_x == 0, edge[e][cx - 1], edge[e][0])
        else:
            block_out[base + e] = edge[e][0]
            block_out[base + EDGE + e] = edge[e][cx - 1]

    lane = iota((nz, cy), 1)
    to_left = [jnp.zeros((nz, cy), f32) for _ in range(cx)]
    to_right = [jnp.zeros((nz, cy), f32) for _ in range(cx)]
    for f in range(BULK + EDGE):
        wide = WIDE if f < BULK else 1
        shift = f * WIDE if f < BULK else EDGE_AT + f - BULK
        on_left = (lane >= shift) & (lane < shift + wide)
        start = (shift - wide) % cy
        on_right = (lane >= start) & (lane < start + wide)
        values = bulk[f] if f < BULK else edge[f - BULK]
        for x in range(cx):
            turned = pltpu.roll(values[x], shift, 1) if shift else values[x]
            to_left[x] = jnp.where(on_left, turned, to_left[x])
            to_right[x] = jnp.where(on_right, turned, to_right[x])
    even = lax.rem(at_y, 2) == 0
    for x in range(cx):
        ya_out[x] = jnp.where(even, to_right[x], to_left[x])
        yb_out[x] = jnp.where(even, to_left[x], to_right[x])


def main_kernel(count_x, count_y, offsets, *refs):
    width = len(offsets)
    (wells_ref, diag_ref, off_ref, dinv_ref), refs = refs[:4], refs[4:]
    blocks, refs = refs[:width], refs[width:]
    ya_refs, refs = refs[:width], refs[width:]
    yb_refs, refs = refs[:width], refs[width:]
    residual_out, z_out, sums_out = refs

    cx, nz, cy = residual_out.shape[1:]
    total = width * cx
    at_x = lax.axis_index("gx")
    at_y = lax.axis_index("gy")
    even = lax.rem(at_y, 2) == 0
    has_left = jnp.where(at_y > 0, 1.0, 0.0).astype(f32)
    has_right = jnp.where(at_y < count_y - 1, 1.0, 0.0).astype(f32)
    layers = 1 if count_x == 2 else 2
    last = BULK * cx + layers * EDGE
    index_x = [lax.rem(at_x + (o % count_x), count_x) for o in offsets]
    joined = [
        jnp.where(index_x[(j + 1) % width] == index_x[j] + 1, 1.0, 0.0).astype(f32)
        for j in range(width)
    ]

    from_left, from_right = [], []
    for j in range(width):
        first, second = ya_refs[j][...], yb_refs[j][...]
        from_right.append(jnp.where(even, first, second) * has_right)
        from_left.append(jnp.where(even, second, first) * has_left)
    lane = iota((nz, cy), 1)

    def halo(tiles_l, tiles_r, x, shift, wide):
        back = (cy - shift) % cy
        left, right = tiles_l[x], tiles_r[x]
        if back:
            left, right = pltpu.roll(left, back, 1), pltpu.roll(right, back, 1)
        return jnp.where(lane < wide, right, jnp.where(lane >= cy - wide, left, 0.0))

    def extended(f):
        own = jnp.concatenate([blocks[j][f * cx : (f + 1) * cx] for j in range(width)], axis=0)
        side = jnp.stack(
            [
                halo(from_left[j], from_right[j], x, f * WIDE, WIDE)
                for j in range(width)
                for x in range(cx)
            ]
        )
        return jnp.concatenate([own, side], axis=2)

    lanes = 2 * cy
    level = iota((total, nz, lanes), 1)

    def next_x(v):
        return jnp.concatenate([v[1:], v[:1]], axis=0)

    def last_x(v):
        return jnp.concatenate([v[-1:], v[:-1]], axis=0)

    def next_y(v):
        return pltpu.roll(v, v.shape[2] - 1, 2)

    def last_y(v):
        return pltpu.roll(v, 1, 2)

    def next_z(v):
        return pltpu.roll(v, nz - 1, 1)

    def last_z(v):
        return pltpu.roll(v, 1, 1)

    def seam_after(v):
        rows = [v[i] for i in range(total)]
        for j in range(width):
            rows[j * cx + cx - 1] = rows[j * cx + cx - 1] * joined[j]
        return jnp.stack(rows)

    def seam_before(v):
        rows = [v[i] for i in range(total)]
        for j in range(width):
            at = ((j + 1) % width) * cx
            rows[at] = rows[at] * joined[j]
        return jnp.stack(rows)

    press = extended(PRESS)
    mobile = [extended(MOB + c) for c in range(3)]
    perm = extended(PERM)
    resid = [extended(ACC + c) for c in range(3)]

    for forward, backward, kind in ((next_x, last_x, 0), (next_y, last_y, 1), (next_z, last_z, 2)):
        beyond = forward(perm)
        bottom = perm + beyond
        conduct = 2.0 * perm * beyond / jnp.where(bottom > 0.0, bottom, 1.0)
        if kind == 0:
            conduct = seam_after(conduct)
        if kind == 2:
            conduct = jnp.where(level < nz - 1, vertical_ratio * conduct, 0.0)
        drop = press - forward(press)
        flow = conduct * drop
        for c in range(3):
            passing = flow * jnp.where(drop >= 0.0, mobile[c], forward(mobile[c]))
            resid[c] = resid[c] + passing - backward(passing)

    wells = wells_ref.shape[2]
    perfs = blocks[0].shape[2]
    added = [[] for _ in range(3)]
    for j in range(width):
        pair = jnp.sum(wells_ref[pl.ds(index_x[j] * count_y, count_y)], axis=0)
        hole = pair[1:2] / pair[0:1]
        tiles = jnp.concatenate(
            [blocks[j][last], from_left[j][cx], from_right[j][cx]], axis=1
        )
        spot_xz, spot_y, well = tiles[0:1], tiles[1:2], tiles[2:3]
        member = jnp.where(iota((wells, 3 * perfs), 0).astype(f32) == well, 1.0, 0.0)
        hole_at = lax.dot_general(
            jnp.broadcast_to(hole, (8, wells)),
            member,
            NN,
            precision=highest,
            preferred_element_type=f32,
        )[0:1]
        fall = tiles[6:7] - hole_at
        on_xz = iota((cx * nz, 3 * perfs), 0).astype(f32) == spot_xz
        spread = jnp.concatenate(
            [jnp.where(on_xz, tiles[3 + c : 4 + c] * fall, 0.0) for c in range(3)], axis=0
        )
        hot_y = iota((cy, 3 * perfs), 0).astype(f32) == spot_y
        nearby = iota((cy, 3 * perfs), 0)
        source = iota((cy, 3 * perfs), 1)
        kept = jnp.where(
            source < 2 * perfs, jnp.where(nearby >= cy - WIDE, 1, 0), jnp.where(nearby < WIDE, 1, 0)
        )
        hot_side = hot_of(hot_y & (kept == 1))
        inner = split_dot(spread[:, :perfs], hot_of(hot_y[:, :perfs]), NT)
        outer = split_dot(spread[:, perfs:], hot_side[:, perfs:], NT)
        both = jnp.concatenate([inner, outer], axis=1).reshape(3, cx, nz, lanes)
        for c in range(3):
            added[c].append(both[c])
    start = [-(resid[c] + jnp.concatenate(added[c], axis=0)) for c in range(3)]
    for c in range(3):
        residual_out[c] = -start[c][:cx, :, :cy]

    coefs = [extended(COEF + q) for q in range(6)]
    coefs[0] = seam_before(coefs[0])
    coefs[1] = seam_after(coefs[1])
    scaled = (start[0] + start[1] + start[2]) * extended(INV)
    steps = (last_x, next_x, last_y, next_y, last_z, next_z)
    part = scaled
    for _ in range(1, SWEEPS):
        gathered = coefs[0] * steps[0](part)
        for q in range(1, 6):
            gathered = gathered + coefs[q] * steps[q](part)
        part = scaled - gathered

    near = [step(part) for step in steps]
    near[0] = seam_before(near[0])
    near[1] = seam_after(near[1])
    near[4] = jnp.where(level > 0, near[4], 0.0)
    near[5] = jnp.where(level < nz - 1, near[5], 0.0)

    def direction(edge_of, where):
        here = where(part)
        rest = []
        for c in range(3):
            coupled = edge_of(DCOL + c) * here
            for q in range(6):
                coupled = coupled + edge_of(OFFC + 3 * q + c) * where(near[q])
            rest.append(where(start[c]) - coupled)
        solved = []
        for a in range(3):
            value = edge_of(DINV + 3 * a) * rest[0]
            value = value + edge_of(DINV + 3 * a + 1) * rest[1]
            solved.append(value + edge_of(DINV + 3 * a + 2) * rest[2])
        solved[0] = solved[0] + here
        return solved

    def edge_own(e):
        if e < DCOL:
            return dinv_ref[e]
        if e < OFFC:
            return diag_ref[e - DCOL, 0]
        return off_ref[(e - OFFC) // 3, (e - OFFC) % 3, 0]

    def edge_side(e):
        return jnp.stack(
            [halo(from_left[0], from_right[0], x, EDGE_AT + e, 1) for x in range(cx)]
        )

    base = BULK * cx
    after, before = 1 % width, width - 1
    z_own = direction(edge_own, lambda v: v[:cx, :, :cy])
    z_side = direction(edge_side, lambda v: v[:cx, :, cy:])
    z_next = direction(
        lambda e: blocks[after][base + e], lambda v: v[after * cx, :, :cy]
    )
    z_last = direction(
        lambda e: blocks[before][base + (layers - 1) * EDGE + e],
        lambda v: v[before * cx + cx - 1, :, :cy],
    )
    level_own = iota((cx, nz, cy), 1)
    around = []
    for k in range(3):
        z_out[k] = z_own[k]
        ext = jnp.concatenate([z_own[k], z_side[k]], axis=2)
        around.append(
            [
                jnp.concatenate([(z_last[k] * joined[width - 1])[None], z_own[k][:-1]], axis=0),
                jnp.concatenate([z_own[k][1:], (z_next[k] * joined[0])[None]], axis=0),
                last_y(ext)[:, :, :cy],
                next_y(ext)[:, :, :cy],
                jnp.where(level_own > 0, last_z(z_own[k]), 0.0),
                jnp.where(level_own < nz - 1, next_z(z_own[k]), 0.0),
            ]
        )
    along = jnp.zeros((nz, cy), f32)
    square = jnp.zeros((nz, cy), f32)
    for c in range(3):
        mapped = diag_ref[c, 0] * z_own[0]
        for k in range(1, 3):
            mapped = mapped + diag_ref[c, k] * z_own[k]
        for q in range(6):
            for k in range(3):
                mapped = mapped + off_ref[q, c, k] * around[k][q]
        along = along + jnp.sum(mapped * start[c][:cx, :, :cy], axis=0)
        square = square + jnp.sum(mapped * mapped, axis=0)
    along = jnp.sum(along, axis=0, keepdims=True)
    square = jnp.sum(square, axis=0, keepdims=True)
    pair = jnp.where(iota((2, cy), 0) == 0, along, square)
    sums_out[...] = jnp.broadcast_to(pair[None], sums_out.shape)


def after_kernel(sums_ref, z_ref, update_out):
    pair = jnp.sum(sums_ref[...], axis=0)
    both = jnp.sum(pair, axis=1, keepdims=True)
    step = both[0:1] / both[1:2]
    update_out[...] = z_ref[...] * step[None, None]


def body(
    pressure,
    saturation,
    saturation_old,
    pore_volume,
    permeability,
    jac_diag,
    jac_off,
    perf_cell,
    perf_well,
    perf_index,
    well_rate,
):
    count_x, count_y = lax.axis_size("gx"), lax.axis_size("gy")
    devices = count_x * count_y
    cx, nz, cy = pressure.shape
    wells = well_rate.shape[1] * count_y
    layers = 1 if count_x == 2 else 2
    tiles = BULK * cx + layers * EDGE + 1
    offsets = window(count_x, cx)
    width = len(offsets)
    shape = jax.ShapeDtypeStruct
    whole = pl.BlockSpec(memory_space=pltpu.VMEM)
    params = pltpu.CompilerParams(vmem_limit_bytes=40 * 1024 * 1024)

    wells_part, block, ya, yb, dinv = pl.pallas_call(
        functools.partial(before_kernel, count_x, count_y),
        grid=(1,),
        in_specs=[
            *[whole] * 6,
            pl.BlockSpec((6, 3, 1, cx, nz, cy), lambda i: (0, 0, 0, 0, 0, 0)),
            *[whole] * 4,
        ],
        out_specs=[whole] * 5,
        out_shape=[
            shape((devices, 2, wells), f32),
            shape((tiles, nz, cy), f32),
            shape((cx + 1, nz, cy), f32),
            shape((cx + 1, nz, cy), f32),
            shape((9, cx, nz, cy), f32),
        ],
        compiler_params=params,
        name="before",
    )(
        pressure,
        saturation,
        saturation_old,
        pore_volume,
        permeability,
        jac_diag,
        jac_off,
        perf_cell,
        perf_well,
        perf_index,
        well_rate,
    )

    pairs = [(i, i ^ 1) for i in range(count_y)]
    others = [(i, (i + 1) % count_y if i % 2 else (i - 1) % count_y) for i in range(count_y)]

    def from_x(values, offset):
        return lax.ppermute(
            values, "gx", [((i + offset) % count_x, i) for i in range(count_x)]
        )

    ya_got = lax.ppermute(ya, "gy", pairs)
    yb_got = lax.ppermute(yb, "gy", others)
    blocks = [block] + [from_x(block, o) for o in offsets[1:]]
    wells_all = lax.all_to_all(wells_part, ("gx", "gy"), 0, 0)
    forward = jnp.stack([ya_got, yb_got])
    passed = [from_x(forward, o) for o in offsets[1:]]
    ya_all = [ya_got] + [p[0] for p in passed]
    yb_all = [yb_got] + [p[1] for p in passed]

    residual, direction, sums = pl.pallas_call(
        functools.partial(main_kernel, count_x, count_y, tuple(offsets)),
        in_specs=[whole] * (4 + 3 * width),
        out_specs=[whole] * 3,
        out_shape=[
            shape((3, cx, nz, cy), f32),
            shape((3, cx, nz, cy), f32),
            shape((devices, 2, cy), f32),
        ],
        compiler_params=params,
        name="main",
    )(wells_all, jac_diag, jac_off, dinv, *blocks, *ya_all, *yb_all)

    sums_all = lax.all_to_all(sums, ("gx", "gy"), 0, 0)
    update = pl.pallas_call(
        after_kernel,
        in_specs=[whole] * 2,
        out_specs=whole,
        out_shape=shape((3, cx, nz, cy), f32),
        compiler_params=params,
        name="after",
    )(sums_all, direction)
    return (residual, update)


def solution(mesh):
    placed = (
        P("gx", None, "gy"),
        P(None, "gx", None, "gy"),
        P(None, "gx", None, "gy"),
        P("gx", None, "gy"),
        P("gx", None, "gy"),
        P(None, None, "gx", None, "gy"),
        P(None, None, None, "gx", None, "gy"),
        P("gx", "gy"),
        P("gx", "gy"),
        P("gx", "gy"),
        P("gx", "gy"),
    )
    return jax.shard_map(
        body,
        mesh=mesh,
        in_specs=placed,
        out_specs=(P(None, "gx", None, "gy"), P(None, "gx", None, "gy")),
        check_vma=False,
    )
```

time: 212 us -> 43 us (0.20)
  blocking collectives: 110 us -> 8.93 us
  starting transfers between devices: 67.2 us -> 13.6 us
  other arithmetic: 9.13 us -> 0.01 us
  waiting for transfers between devices: 12.6 us -> 7.25 us
  Pallas kernels: 0 us -> 3.67 us
  between operations: 4.03 us -> 0.67 us
    ppermute x24 -> x4, starting transfers between devices: 67.2 us -> 9.08 us  [the longest x1 5.67 us: body(): yb_got = lax.ppermute(yb, 'gy', others)]
    psum x1 -> x0, blocking collectives: 47.2 us -> none  [global_sum(): return lax.psum((values[0], values[1]), ('gx', 'gy'))]
    unnamed x1 -> x0, blocking collectives: 33.2 us -> none
    all_gather x1 -> x0, blocking collectives: 29.5 us -> none  [body(): bottom_all = lax.all_gather(bottom, 'gy', axis=0, tiled=True)]
    ppermute x24 -> x4, waiting for transfers between devices: 12.6 us -> 0.94 us  [the longest x2 0.93 us: from_x(): lax.ppermute(values, 'gx', [((i + offset) % count_x, i) for i in range(co...]
    all_to_all x0 -> x1, blocking collectives: none -> 8.93 us  [body(): sums_all = lax.all_to_all(sums, ('gx', 'gy'), 0, 0)]
    all_to_all x0 -> x1, waiting for transfers between devices: none -> 6.31 us  [body(): wells_all = lax.all_to_all(wells_part, ('gx', 'gy'), 0, 0)]
    unnamed x31 -> x26, local copies, waits for them, and re-layouts: 2.48 us -> 8.36 us
  transfers between devices with their start and end apart: 24 -> 5, of which waited for: 11 -> 2; matrix products, arithmetic and copies ran while one was open for 2% -> 0% of each run, Pallas kernels for 0% -> 0%
where the time goes in v1:
time: 43 us; the launch traced here: 42.5 us
  starting transfers between devices  13.6 us (32%)
  blocking collectives  8.93 us (21%)
  local copies, waits for them, and re-layouts  8.37 us (19%)
  waiting for transfers between devices  7.25 us (17%)
  Pallas kernels  3.67 us (9%)
  between operations  0.67 us (2%)
    all_to_all x1, blocking collectives, body(): sums_all = lax.all_to_all(sums, ('gx', 'gy'), 0, 0)  8.93 us
    unnamed x26, local copies, waits for them, and re-layouts  8.36 us
    all_to_all x1, waiting for transfers between devices, body(): wells_all = lax.all_to_all(wells_part, ('gx', 'gy'), 0, 0)  6.31 us
    ppermute x1, starting transfers between devices, body(): yb_got = lax.ppermute(yb, 'gy', others)  5.67 us
    all_to_all x1, starting transfers between devices, body(): wells_all = lax.all_to_all(wells_part, ('gx', 'gy'), 0, 0)  4.51 us
    ppermute x2, starting transfers between devices, from_x(): lax.ppermute(values, 'gx', [((i + offset) % count_x, i) for i in range(co...  2.97 us
    pallas_call x1, Pallas kernels, body(): pl.pallas_call(functools.partial(main_kernel, count_x, count_y, tuple(off...  1.84 us
    pallas_call x1, Pallas kernels, body(): pl.pallas_call(functools.partial(before_kernel, count_x, count_y), grid=(...  1.05 us
  transfers between devices with their start and end apart: 5, of which 2 were waited for; matrix products, arithmetic and copies ran while one was open for 0% of the time, Pallas kernels for 0%

profile of v1, /device:TPU:0, one launch (start us, length us, event | category | flops | bytes accessed | tf_op | source)
XLA Modules:
  0.0 42.5 jit_solution(7269396309117079072)
XLA Ops:
  0.6 0.0 copy-start
  0.6 1.2 %copy-done = f32[6,3,3,4,8,128]{5,4,3,2,1,0:T(8,128)S(1)} copy-done((f32[6,3,3,4,8,128]{5,4,3,2,1,0:T(8,128)S(1)}, f32[6,3,3,4,8,128]{5,4,3,2,1,0:T(8,128)}, u32[]{:S(2)}) %copy-start) | copy-done | bytes 884760
  1.8 0.0 copy-start.2
  1.8 0.9 %copy-done.2 = f32[3,3,4,8,128]{4,3,2,1,0:T(8,128)S(1)} copy-done((f32[3,3,4,8,128]{4,3,2,1,0:T(8,128)S(1)}, f32[3,3,4,8,128]{4,3,2,1,0:T(8,128)}, u32[]{:S(2)}) %copy-start.2) | copy-done | bytes 147480
  2.7 0.0 copy-start.4
  2.7 0.8 %copy-done.4 = f32[2,4,8,128]{3,2,1,0:T(8,128)S(1)} copy-done((f32[2,4,8,128]{3,2,1,0:T(8,128)S(1)}, f32[2,4,8,128]{3,2,1,0:T(8,128)}, u32[]{:S(2)}) %copy-start.4) | copy-done | bytes 32792
  3.5 0.0 copy-start.5
  3.5 0.8 %copy-done.5 = f32[2,4,8,128]{3,2,1,0:T(8,128)S(1)} copy-done((f32[2,4,8,128]{3,2,1,0:T(8,128)S(1)}, f32[2,4,8,128]{3,2,1,0:T(8,128)}, u32[]{:S(2)}) %copy-start.5) | copy-done | bytes 32792
  4.2 0.0 copy-start.6
  4.2 0.7 %copy-done.6 = f32[4,8,128]{2,1,0:T(8,128)S(1)} copy-done((f32[4,8,128]{2,1,0:T(8,128)S(1)}, f32[4,8,128]{2,1,0:T(8,128)}, u32[]{:S(2)}) %copy-start.6) | copy-done | bytes 16408
  4.9 0.0 copy-start.7
  4.9 0.7 %copy-done.7 = f32[4,8,128]{2,1,0:T(8,128)S(1)} copy-done((f32[4,8,128]{2,1,0:T(8,128)S(1)}, f32[4,8,128]{2,1,0:T(8,128)}, u32[]{:S(2)}) %copy-start.7) | copy-done | bytes 16408
  5.7 0.0 copy-start.8
  5.7 0.7 %copy-done.8 = f32[4,8,128]{2,1,0:T(8,128)S(1)} copy-done((f32[4,8,128]{2,1,0:T(8,128)S(1)}, f32[4,8,128]{2,1,0:T(8,128)}, u32[]{:S(2)}) %copy-start.8) | copy-done | bytes 16408
  6.4 0.0 copy-start.9
  6.4 0.7 %copy-done.9 = s32[1,128]{1,0:T(1,128)S(1)} copy-done((s32[1,128]{1,0:T(1,128)S(1)}, s32[1,128]{1,0:T(1,128)}, u32[]{:S(2)}) %copy-start.9) | copy-done | bytes 536
  7.0 0.0 copy-start.10
  7.0 0.7 %copy-done.10 = s32[1,128]{1,0:T(1,128)S(1)} copy-done((s32[1,128]{1,0:T(1,128)S(1)}, s32[1,128]{1,0:T(1,128)}, u32[]{:S(2)}) %copy-start.10) | copy-done | bytes 536
  7.7 0.0 copy-start.11
  7.7 0.7 %copy-done.11 = f32[1,128]{1,0:T(1,128)S(1)} copy-done((f32[1,128]{1,0:T(1,128)S(1)}, f32[1,128]{1,0:T(1,128)}, u32[]{:S(2)}) %copy-start.11) | copy-done | bytes 536
  8.4 0.0 copy-start.12
  8.4 0.7 %copy-done.12 = f32[1,8]{1,0:T(1,128)S(1)} copy-done((f32[1,8]{1,0:T(1,128)S(1)}, f32[1,8]{1,0:T(1,128)}, u32[]{:S(2)}) %copy-start.12) | copy-done | bytes 56
  9.0 0.0 copy-start.1
  9.0 1.1 %before.1 = (f32[32,2,128]{2,1,0:T(2,128)}, f32[91,8,128]{2,1,0:T(8,128)S(1)}, f32[5,8,128]{2,1,0:T(8,128)S(1)}, f32[5,8,128]{2,1,0:T(8,128)S(1)}, f32[9,4,8,128]{3,2,1,0:T(8,128)S(1)}) custom-call(f32[4,8,128]{2,1,0:T(8,128)S(1)} %copy-done.6, f32[2,4,8,128]{3,2,1,0:T(8,128)S(1)} %copy-done.4, f32[2,4,8,128]{3,2,1,0:T(8,128)S(1)} %copy-done.5, ...), custom_call_target="tpu_custom_call" | custom-call | tf_op jit(solution)/shard_map/before/pallas_call | solution.py:452
  10.1 0.0 copy-start.3
  10.1 0.5 %collective-permute-start.1 = (f32[5,8,128]{2,1,0:T(8,128)S(1)}, f32[5,8,128]{2,1,0:T(8,128)S(1)}, u32[]{:S(2)}, u32[]{:S(2)}) collective-permute-start(f32[5,8,128]{2,1,0:T(8,128)S(1)} %get-tuple-element.13), channel_id=1, source_target_pairs={{0,1},{1,0},{2,3},{3,2},{4,5},{5,4},{6,7},{7,6},{8,9},{9,8},{10,11... | collective-permute-start | bytes 61448 | tf_op jit(solution)/shard_map/ppermute | solution.py:492
  10.5 5.7 %collective-permute-start.2 = (f32[5,8,128]{2,1,0:T(8,128)S(1)}, f32[5,8,128]{2,1,0:T(8,128)S(1)}, u32[]{:S(2)}, u32[]{:S(2)}) collective-permute-start(f32[5,8,128]{2,1,0:T(8,128)S(1)} %get-tuple-element.14), channel_id=1, source_target_pairs={{0,15},{1,2},{2,1},{3,4},{4,3},{5,6},{6,5},{7,8},{8,7},{9,10},{10,... | collective-permute-start | bytes 61448 | tf_op jit(solution)/shard_map/ppermute | solution.py:493
  16.2 1.5 %collective-permute-start = (f32[91,8,128]{2,1,0:T(8,128)S(1)}, f32[91,8,128]{2,1,0:T(8,128)S(1)}, u32[]{:S(2)}, u32[]{:S(2)}) collective-permute-start(f32[91,8,128]{2,1,0:T(8,128)S(1)} %get-tuple-element.12.refs_4_), channel_id=1, source_target_pairs={{16,0},{0,16},{17,1},{1,17},{18,2},{2,18},{19,3},{3,19},{20,4},{4,... | collective-permute-start | bytes 1118216 | tf_op jit(solution)/shard_map/ppermute | solution.py:488
  17.7 0.0 collective-permute-done.1.refs_6_
  17.7 0.0 collective-permute-done.2.refs_8_
  17.7 1.5 %collective-permute-start.3 = (f32[2,5,8,128]{3,2,1,0:T(8,128)S(1)}, f32[2,5,8,128]{3,2,1,0:T(8,128)S(1)}, u32[]{:S(2)}, u32[]{:S(2)}) collective-permute-start(f32[2,5,8,128]{3,2,1,0:T(8,128)S(1)} %pad_maximum_fusion), channel_id=1, source_target_pairs={{16,0},{0,16},{17,1},{1,17},{18,2},{2,18},{19,3},{3,19},{20,4},{4,... | collective-permute-start | bytes 122888 | tf_op jit(solution)/shard_map/ppermute | solution.py:488
  19.2 4.5 %all-to-all-start = ((f32[32,2,128]{2,1,0:T(2,128)}), f32[32,2,128]{2,1,0:T(2,128)S(1)}, u32[]{:S(2)}, u32[]{:S(2)}) async-start(f32[32,2,128]{2,1,0:T(2,128)} %get-tuple-element.10), calls=%async_computation | async-start | bytes 65536 | tf_op jit(solution)/shard_map/all_to_all | solution.py:495
  23.7 0.9 %collective-permute-done.3 = f32[2,5,8,128]{3,2,1,0:T(8,128)S(1)} collective-permute-done((f32[2,5,8,128]{3,2,1,0:T(8,128)S(1)}, f32[2,5,8,128]{3,2,1,0:T(8,128)S(1)}, u32[]{:S(2)}, u32[]{:S(2)}) %collective-permute-start.3) | collective-permute-done | bytes 40992 | tf_op jit(solution)/shard_map/ppermute | solution.py:488
  24.6 6.3 %all-to-all-done.refs_0_ = f32[32,2,128]{2,1,0:T(2,128)S(1)} async-done(((f32[32,2,128]{2,1,0:T(2,128)}), f32[32,2,128]{2,1,0:T(2,128)S(1)}, u32[]{:S(2)}, u32[]{:S(2)}) %all-to-all-start) | async-done | bytes 32800 | tf_op jit(solution)/shard_map/all_to_all | solution.py:495
  30.9 0.0 collective-permute-done.refs_5_
  30.9 0.0 copy-done.1
  30.9 0.0 copy-done.3
  30.9 1.8 %main.1 = (f32[3,4,8,128]{3,2,1,0:T(8,128)}, f32[3,4,8,128]{3,2,1,0:T(8,128)S(1)}, f32[32,2,128]{2,1,0:T(2,128)S(1)}) custom-call(f32[32,2,128]{2,1,0:T(2,128)S(1)} %all-to-all-done.refs_0_, f32[3,3,4,8,128]{4,3,2,1,0:T(8,128)S(1)} %copy-done.3, f32[6,3,3,4,8,128]{5,4,3,2,1,0:T(8,128)S(1)} %copy-done.1, f32[9,4,8,128]{3,2,1,0:T(8,128)S(1)} %get-tuple-element.11.refs_3_, ...), custom_call_target="tpu_custom_call" | custom-call | tf_op jit(solution)/shard_map/main/pallas_call | solution.py:501
  32.8 8.9 %all_to_all.10.sums_ref = f32[32,2,128]{2,1,0:T(2,128)S(1)} all-to-all(f32[32,2,128]{2,1,0:T(2,128)S(1)} %get-tuple-element.16), channel_id=1, replica_groups=mesh['gx'=2,'gy'=16] {'gx','gy'}, dimensions={0} | all-to-all | bytes 65536 | tf_op jit(solution)/shard_map/all_to_all | solution.py:514
  41.7 0.8 %after.1 = f32[3,4,8,128]{3,2,1,0:T(8,128)} custom-call(f32[32,2,128]{2,1,0:T(2,128)S(1)} %all_to_all.10.sums_ref, f32[3,4,8,128]{3,2,1,0:T(8,128)S(1)} %get-tuple-element.17.z_ref), custom_call_target="tpu_custom_call" | custom-call | tf_op jit(solution)/shard_map/after/pallas_call | solution.py:515
  (2 shorter events, 0.0 us)
Async XLA Ops:
  0.6 1.2 %copy-start = (f32[6,3,3,4,8,128]{5,4,3,2,1,0:T(8,128)S(1)}, f32[6,3,3,4,8,128]{5,4,3,2,1,0:T(8,128)}, u32[]{:S(2)}) copy-start(f32[6,3,3,4,8,128]{5,4,3,2,1,0:T(8,128)} %refs_2_.1) | copy-start | bytes 2654212
  1.8 0.9 %copy-start.2 = (f32[3,3,4,8,128]{4,3,2,1,0:T(8,128)S(1)}, f32[3,3,4,8,128]{4,3,2,1,0:T(8,128)}, u32[]{:S(2)}) copy-start(f32[3,3,4,8,128]{4,3,2,1,0:T(8,128)} %refs_1_.1) | copy-start | bytes 442372
  2.7 0.8 %copy-start.4 = (f32[2,4,8,128]{3,2,1,0:T(8,128)S(1)}, f32[2,4,8,128]{3,2,1,0:T(8,128)}, u32[]{:S(2)}) copy-start(f32[2,4,8,128]{3,2,1,0:T(8,128)} %sat_ref.1) | copy-start | bytes 98308
  3.5 0.8 %copy-start.5 = (f32[2,4,8,128]{3,2,1,0:T(8,128)S(1)}, f32[2,4,8,128]{3,2,1,0:T(8,128)}, u32[]{:S(2)}) copy-start(f32[2,4,8,128]{3,2,1,0:T(8,128)} %old_ref.1) | copy-start | bytes 98308
  4.2 0.7 %copy-start.6 = (f32[4,8,128]{2,1,0:T(8,128)S(1)}, f32[4,8,128]{2,1,0:T(8,128)}, u32[]{:S(2)}) copy-start(f32[4,8,128]{2,1,0:T(8,128)} %press_ref.1) | copy-start | bytes 49156
  4.9 0.7 %copy-start.7 = (f32[4,8,128]{2,1,0:T(8,128)S(1)}, f32[4,8,128]{2,1,0:T(8,128)}, u32[]{:S(2)}) copy-start(f32[4,8,128]{2,1,0:T(8,128)} %pore_ref.1) | copy-start | bytes 49156
  5.7 0.7 %copy-start.8 = (f32[4,8,128]{2,1,0:T(8,128)S(1)}, f32[4,8,128]{2,1,0:T(8,128)}, u32[]{:S(2)}) copy-start(f32[4,8,128]{2,1,0:T(8,128)} %perm_ref.1) | copy-start | bytes 49156
  6.4 0.7 %copy-start.9 = (s32[1,128]{1,0:T(1,128)S(1)}, s32[1,128]{1,0:T(1,128)}, u32[]{:S(2)}) copy-start(s32[1,128]{1,0:T(1,128)} %cell_ref.1) | copy-start | bytes 1540
  7.0 0.7 %copy-start.10 = (s32[1,128]{1,0:T(1,128)S(1)}, s32[1,128]{1,0:T(1,128)}, u32[]{:S(2)}) copy-start(s32[1,128]{1,0:T(1,128)} %well_ref.1) | copy-start | bytes 1540
  7.7 0.7 %copy-start.11 = (f32[1,128]{1,0:T(1,128)S(1)}, f32[1,128]{1,0:T(1,128)}, u32[]{:S(2)}) copy-start(f32[1,128]{1,0:T(1,128)} %index_ref.1) | copy-start | bytes 1540
  8.4 0.7 %copy-start.12 = (f32[1,8]{1,0:T(1,128)S(1)}, f32[1,8]{1,0:T(1,128)}, u32[]{:S(2)}) copy-start(f32[1,8]{1,0:T(1,128)} %rate_ref.1) | copy-start | bytes 100
  9.0 21.9 %copy-start.1 = (f32[6,3,3,4,8,128]{5,4,3,2,1,0:T(8,128)S(1)}, f32[6,3,3,4,8,128]{5,4,3,2,1,0:T(8,128)}, u32[]{:S(2)}) copy-start(f32[6,3,3,4,8,128]{5,4,3,2,1,0:T(8,128)} %refs_2_.1) | copy-start | bytes 2654212
  10.1 20.9 %copy-start.3 = (f32[3,3,4,8,128]{4,3,2,1,0:T(8,128)S(1)}, f32[3,3,4,8,128]{4,3,2,1,0:T(8,128)}, u32[]{:S(2)}) copy-start(f32[3,3,4,8,128]{4,3,2,1,0:T(8,128)} %refs_1_.1) | copy-start | bytes 442372
  10.1 7.6 %collective-permute-start.1 = (f32[5,8,128]{2,1,0:T(8,128)S(1)}, f32[5,8,128]{2,1,0:T(8,128)S(1)}, u32[]{:S(2)}, u32[]{:S(2)}) collective-permute-start(f32[5,8,128]{2,1,0:T(8,128)S(1)} %get-tuple-element.13), channel_id=1, source_target_pairs={{0,1},{1,0},{2,3},{3,2},{4,5},{5,4},{6,7},{7,6},{8,9},{9,8},{10,11... | collective-permute-start | bytes 61448 | tf_op jit(solution)/shard_map/ppermute | solution.py:492
  10.5 7.2 %collective-permute-start.2 = (f32[5,8,128]{2,1,0:T(8,128)S(1)}, f32[5,8,128]{2,1,0:T(8,128)S(1)}, u32[]{:S(2)}, u32[]{:S(2)}) collective-permute-start(f32[5,8,128]{2,1,0:T(8,128)S(1)} %get-tuple-element.14), channel_id=1, source_target_pairs={{0,15},{1,2},{2,1},{3,4},{4,3},{5,6},{6,5},{7,8},{8,7},{9,10},{10,... | collective-permute-start | bytes 61448 | tf_op jit(solution)/shard_map/ppermute | solution.py:493
  16.2 14.7 %collective-permute-start = (f32[91,8,128]{2,1,0:T(8,128)S(1)}, f32[91,8,128]{2,1,0:T(8,128)S(1)}, u32[]{:S(2)}, u32[]{:S(2)}) collective-permute-start(f32[91,8,128]{2,1,0:T(8,128)S(1)} %get-tuple-element.12.refs_4_), channel_id=1, source_target_pairs={{16,0},{0,16},{17,1},{1,17},{18,2},{2,18},{19,3},{3,19},{20,4},{4,... | collective-permute-start | bytes 1118216 | tf_op jit(solution)/shard_map/ppermute | solution.py:488
  17.7 6.9 %collective-permute-start.3 = (f32[2,5,8,128]{3,2,1,0:T(8,128)S(1)}, f32[2,5,8,128]{3,2,1,0:T(8,128)S(1)}, u32[]{:S(2)}, u32[]{:S(2)}) collective-permute-start(f32[2,5,8,128]{3,2,1,0:T(8,128)S(1)} %pad_maximum_fusion), channel_id=1, source_target_pairs={{16,0},{0,16},{17,1},{1,17},{18,2},{2,18},{19,3},{3,19},{20,4},{4,... | collective-permute-start | bytes 122888 | tf_op jit(solution)/shard_map/ppermute | solution.py:488
  19.2 11.8 %all-to-all-start = ((f32[32,2,128]{2,1,0:T(2,128)}), f32[32,2,128]{2,1,0:T(2,128)S(1)}, u32[]{:S(2)}, u32[]{:S(2)}) async-start(f32[32,2,128]{2,1,0:T(2,128)} %get-tuple-element.10), calls=%async_computation | async-start | bytes 65536 | tf_op jit(solution)/shard_map/all_to_all | solution.py:495

commit v2 on v1

--- a/solution.py
+++ b/solution.py
@@ -53,23 +53,19 @@
 def before_kernel(
     count_x,
     count_y,
-    press_ref,
-    sat_ref,
-    old_ref,
-    pore_ref,
-    perm_ref,
-    diag_ref,
-    off_ref,
-    cell_ref,
-    well_ref,
-    index_ref,
-    rate_ref,
-    wells_out,
-    block_out,
-    ya_out,
-    yb_out,
-    dinv_out,
+    *refs,
 ):
+    sources, (wells_out, block_out, ya_out, yb_out, dinv_out) = refs[:11], refs[11:16]
+    diag_ref, off_ref = refs[16:18]
+    press_ref, sat_ref, old_ref, pore_ref, perm_ref = refs[18:23]
+    cell_ref, well_ref, index_ref, rate_ref, sems = refs[23:]
+    targets = (*refs[18:23], diag_ref, off_ref, *refs[23:27])
+    copies = []
+    for i in (7, 8, 9, 10, 0, 1, 4, 2, 3, 5, 6):
+        copies.append(pltpu.make_async_copy(sources[i], targets[i], sems.at[i]))
+        copies[-1].start()
+    for copy in copies[:6]:
+        copy.wait()
     cx, nz, cy = press_ref.shape
     at_x = lax.axis_index("gx")
     at_y = lax.axis_index("gy")
@@ -130,6 +126,8 @@
         ya_out[cx, r : r + 1, :] = values
         yb_out[cx, r : r + 1, :] = values
 
+    for copy in copies[6:]:
+        copy.wait()
     old_water, old_gas = old_ref[0], old_ref[1]
     old_oil = 1.0 - old_water - old_gas
     pore = pore_ref[...]
@@ -182,6 +180,9 @@
             turned = pltpu.roll(values[x], shift, 1) if shift else values[x]
             to_left[x] = jnp.where(on_left, turned, to_left[x])
             to_right[x] = jnp.where(on_right, turned, to_right[x])
+    for spare in range(cx + 1, 2 * cx):
+        ya_out[spare] = jnp.zeros((nz, cy), f32)
+        yb_out[spare] = jnp.zeros((nz, cy), f32)
     even = lax.rem(at_y, 2) == 0
     for x in range(cx):
         ya_out[x] = jnp.where(even, to_right[x], to_left[x])
@@ -447,42 +448,35 @@
     width = len(offsets)
     shape = jax.ShapeDtypeStruct
     whole = pl.BlockSpec(memory_space=pltpu.VMEM)
-    params = pltpu.CompilerParams(vmem_limit_bytes=40 * 1024 * 1024)
-
-    wells_part, block, ya, yb, dinv = pl.pallas_call(
+    anywhere = pl.BlockSpec(memory_space=pltpu.HBM)
+    params = pltpu.CompilerParams(vmem_limit_bytes=32 * 1024 * 1024)
+
+    fields = (pressure, saturation, saturation_old, pore_volume, permeability, jac_diag)
+    perforations = (perf_cell, perf_well, perf_index, well_rate)
+    wells_part, block, ya, yb, dinv, diag, off = pl.pallas_call(
         functools.partial(before_kernel, count_x, count_y),
-        grid=(1,),
-        in_specs=[
-            *[whole] * 6,
-            pl.BlockSpec((6, 3, 1, cx, nz, cy), lambda i: (0, 0, 0, 0, 0, 0)),
-            *[whole] * 4,
-        ],
-        out_specs=[whole] * 5,
+        in_specs=[anywhere] * 11,
+        out_specs=[whole] * 7,
         out_shape=[
             shape((devices, 2, wells), f32),
             shape((tiles, nz, cy), f32),
-            shape((cx + 1, nz, cy), f32),
-            shape((cx + 1, nz, cy), f32),
+            shape((2 * cx, nz, cy), f32),
+            shape((2 * cx, nz, cy), f32),
             shape((9, cx, nz, cy), f32),
+            shape(jac_diag.shape, f32),
+            shape(jac_off.shape, f32),
+        ],
+        scratch_shapes=[
+            *[pltpu.VMEM(v.shape, v.dtype) for v in fields[:5]],
+            *[pltpu.VMEM(v.shape, v.dtype) for v in perforations],
+            pltpu.SemaphoreType.DMA((11,)),
         ],
         compiler_params=params,
         name="before",
-    )(
-        pressure,
-        saturation,
-        saturation_old,
-        pore_volume,
-        permeability,
-        jac_diag,
-        jac_off,
-        perf_cell,
-        perf_well,
-        perf_index,
-        well_rate,
-    )
+    )(*[pltpu.with_memory_space_constraint(v, pltpu.HBM) for v in (*fields, jac_off, *perforations)])
 
     pairs = [(i, i ^ 1) for i in range(count_y)]
-    others = [(i, (i + 1) % count_y if i % 2 else (i - 1) % count_y) for i in range(count_y)]
+    others = [(i, min(i + 1, count_y - 1) if i % 2 else max(i - 1, 0)) for i in range(count_y)]
 
     def from_x(values, offset):
         return lax.ppermute(
@@ -493,10 +487,8 @@
     yb_got = lax.ppermute(yb, "gy", others)
     blocks = [block] + [from_x(block, o) for o in offsets[1:]]
     wells_all = lax.all_to_all(wells_part, ("gx", "gy"), 0, 0)
-    forward = jnp.stack([ya_got, yb_got])
-    passed = [from_x(forward, o) for o in offsets[1:]]
-    ya_all = [ya_got] + [p[0] for p in passed]
-    yb_all = [yb_got] + [p[1] for p in passed]
+    ya_all = [ya_got] + [from_x(ya_got, o) for o in offsets[1:]]
+    yb_all = [yb_got] + [from_x(yb_got, o) for o in offsets[1:]]
 
     residual, direction, sums = pl.pallas_call(
         functools.partial(main_kernel, count_x, count_y, tuple(offsets)),
@@ -509,7 +501,7 @@
         ],
         compiler_params=params,
         name="main",
-    )(wells_all, jac_diag, jac_off, dinv, *blocks, *ya_all, *yb_all)
+    )(wells_all, diag, off, dinv, *blocks, *ya_all, *yb_all)
 
     sums_all = lax.all_to_all(sums, ("gx", "gy"), 0, 0)
     update = pl.pallas_call(

time: 43 us -> 33.6 us (0.78)
  local copies, waits for them, and re-layouts: 8.37 us -> 0 us
  waiting for transfers between devices: 7.25 us -> 5.16 us
  blocking collectives: 8.93 us -> 10.2 us
  Pallas kernels: 3.67 us -> 4.86 us
  starting transfers between devices: 13.6 us -> 12.5 us
    unnamed x26 -> x0, local copies, waits for them, and re-layouts: 8.36 us -> none
    ppermute x1, starting transfers between devices: 5.67 us -> 0.65 us  [body(): yb_got = lax.ppermute(yb, 'gy', others)]
    all_to_all x1, starting transfers between devices: 4.51 us -> 6.79 us  [body(): wells_all = lax.all_to_all(wells_part, ('gx', 'gy'), 0, 0)]
    ppermute x2 -> x3, starting transfers between devices: 2.97 us -> 5.1 us  [from_x(): lax.ppermute(values, 'gx', [((i + offset) % count_x, i) for i in range(co...]
    all_to_all x1, blocking collectives: 8.93 us -> 10.2 us  [body(): sums_all = lax.all_to_all(sums, ('gx', 'gy'), 0, 0)]
    pallas_call x1, Pallas kernels: 1.05 us -> 2.23 us  [body(): pl.pallas_call(functools.partial(before_kernel, count_x, count_y), in_spe...]
    all_to_all x1, waiting for transfers between devices: 6.31 us -> 5.14 us  [body(): wells_all = lax.all_to_all(wells_part, ('gx', 'gy'), 0, 0)]
    ppermute x2 -> x3, waiting for transfers between devices: 0.93 us -> 0.01 us  [from_x(): lax.ppermute(values, 'gx', [((i + offset) % count_x, i) for i in range(co...]
  transfers between devices with their start and end apart: 5 -> 6, of which waited for: 2 -> 1; matrix products, arithmetic and copies ran while one was open for 0% -> 0% of each run, Pallas kernels for 0% -> 0%
where the time goes in v2:
time: 33.6 us; the launch traced here: 33.4 us
  starting transfers between devices  12.5 us (37%)
  blocking collectives  10.2 us (30%)
  waiting for transfers between devices  5.16 us (15%)
  Pallas kernels  4.86 us (14%)
  between operations  0.67 us (2%)
    all_to_all x1, blocking collectives, body(): sums_all = lax.all_to_all(sums, ('gx', 'gy'), 0, 0)  10.2 us
    all_to_all x1, starting transfers between devices, body(): wells_all = lax.all_to_all(wells_part, ('gx', 'gy'), 0, 0)  6.79 us
    all_to_all x1, waiting for transfers between devices, body(): wells_all = lax.all_to_all(wells_part, ('gx', 'gy'), 0, 0)  5.14 us
    ppermute x3, starting transfers between devices, from_x(): lax.ppermute(values, 'gx', [((i + offset) % count_x, i) for i in range(co...  5.1 us
    pallas_call x1, Pallas kernels, body(): pl.pallas_call(functools.partial(before_kernel, count_x, count_y), in_spe...  2.23 us
    pallas_call x1, Pallas kernels, body(): pl.pallas_call(functools.partial(main_kernel, count_x, count_y, tuple(off...  1.85 us
    pallas_call x1, Pallas kernels, body(): pl.pallas_call(after_kernel, in_specs=[whole] * 2, out_specs=whole, out_s...  0.78 us
  transfers between devices with their start and end apart: 6, of which 1 were waited for; matrix products, arithmetic and copies ran while one was open for 0% of the time, Pallas kernels for 0%

profile of v2, /device:TPU:0, one launch (start us, length us, event | category | flops | bytes accessed | tf_op | source)
XLA Modules:
  0.0 33.4 jit_solution(2871766501112717139)
XLA Ops:
  0.6 2.2 %before.1 = (f32[32,2,128]{2,1,0:T(2,128)}, f32[91,8,128]{2,1,0:T(8,128)S(1)}, f32[8,8,128]{2,1,0:T(8,128)S(1)}, f32[8,8,128]{2,1,0:T(8,128)S(1)}, f32[9,4,8,128...) custom-call(f32[4,8,128]{2,1,0:T(8,128)} %refs_0_.1, ...), custom_call_target="tpu_custom_call" | custom-call | tf_op jit(solution)/shard_map/before/pallas_call | solution.py:456
  2.9 3.0 %collective-permute-start = (f32[91,8,128]{2,1,0:T(8,128)S(1)}, f32[91,8,128]{2,1,0:T(8,128)S(1)}, u32[]{:S(2)}, u32[]{:S(2)}) collective-permute-start(f32[91,8,128]{2,1,0:T(8,128)S(1)} %get-tuple-element.16.refs_4_), channel_id=1, source_target_pairs={{16,0},{0,16},{17,1},{1,17},{18,2},{2,18},{19,3},{3,19},{20,4},{4,... | collective-permute-start | bytes 1118216 | tf_op jit(solution)/shard_map/ppermute | solution.py:482
  5.9 0.0 collective-permute-start.1
  5.9 0.7 %collective-permute-start.3 = (f32[8,8,128]{2,1,0:T(8,128)S(1)}, f32[8,8,128]{2,1,0:T(8,128)S(1)}, u32[]{:S(2)}, u32[]{:S(2)}) collective-permute-start(f32[8,8,128]{2,1,0:T(8,128)S(1)} %get-tuple-element.18), channel_id=1, source_target_pairs={{0,0},{1,2},{2,1},{3,4},{4,3},{5,6},{6,5},{7,8},{8,7},{9,10},{10,9... | collective-permute-start | bytes 98312 | tf_op jit(solution)/shard_map/ppermute | solution.py:487
  6.5 6.8 %all-to-all-start = ((f32[32,2,128]{2,1,0:T(2,128)}), f32[32,2,128]{2,1,0:T(2,128)S(1)}, u32[]{:S(2)}, u32[]{:S(2)}) async-start(f32[32,2,128]{2,1,0:T(2,128)} %get-tuple-element.12), calls=%async_computation | async-start | bytes 65536 | tf_op jit(solution)/shard_map/all_to_all | solution.py:489
  13.3 0.0 collective-permute-done.1.refs_6_
  13.4 1.8 %collective-permute-start.2 = (f32[8,8,128]{2,1,0:T(8,128)S(1)}, f32[8,8,128]{2,1,0:T(8,128)S(1)}, u32[]{:S(2)}, u32[]{:S(2)}) collective-permute-start(f32[8,8,128]{2,1,0:T(8,128)S(1)} %collective-permute-done.1.refs_6_), channel_id=1, source_target_pairs={{16,0},{0,16},{17,1},{1,17},{18,2},{2,18},{19,3},{3,19},{20,4},{4,... | collective-permute-start | bytes 98312 | tf_op jit(solution)/shard_map/ppermute | solution.py:482
  15.2 0.0 collective-permute-done.3.refs_8_
  15.2 0.3 collective-permute-start.4
  15.4 5.1 %all-to-all-done.refs_0_ = f32[32,2,128]{2,1,0:T(2,128)S(1)} async-done(((f32[32,2,128]{2,1,0:T(2,128)}), f32[32,2,128]{2,1,0:T(2,128)S(1)}, u32[]{:S(2)}, u32[]{:S(2)}) %all-to-all-start) | async-done | bytes 32800 | tf_op jit(solution)/shard_map/all_to_all | solution.py:489
  20.6 0.0 collective-permute-done.2.refs_7_
  20.6 0.0 collective-permute-done.4.refs_9_
  20.6 0.0 collective-permute-done.refs_5_
  20.6 1.9 %main.1 = (f32[3,4,8,128]{3,2,1,0:T(8,128)}, f32[3,4,8,128]{3,2,1,0:T(8,128)S(1)}, f32[32,2,128]{2,1,0:T(2,128)S(1)}) custom-call(f32[32,2,128]{2,1,0:T(2,128)S(1)} %all-to-all-done.refs_0_, f32[3,3,4,8,128]{4,3,2,1,0:T(8,128)S(1)} %get-tuple-element.13.refs_1_, f32[6,3,3,4,8,128]{5,4,3,2,1,0:T(8,128)S(1)} %get-tuple-element.14.refs_2_, ...), custom_call_target="tpu_custom_call" | custom-call | tf_op jit(solution)/shard_map/main/pallas_call | solution.py:493
  22.5 10.2 %all_to_all.10.sums_ref = f32[32,2,128]{2,1,0:T(2,128)S(1)} all-to-all(f32[32,2,128]{2,1,0:T(2,128)S(1)} %get-tuple-element.20), channel_id=1, replica_groups=mesh['gx'=2,'gy'=16] {'gx','gy'}, dimensions={0} | all-to-all | bytes 65536 | tf_op jit(solution)/shard_map/all_to_all | solution.py:506
  32.6 0.8 %after.1 = f32[3,4,8,128]{3,2,1,0:T(8,128)} custom-call(f32[32,2,128]{2,1,0:T(2,128)S(1)} %all_to_all.10.sums_ref, f32[3,4,8,128]{3,2,1,0:T(8,128)S(1)} %get-tuple-element.21.z_ref), custom_call_target="tpu_custom_call" | custom-call | tf_op jit(solution)/shard_map/after/pallas_call | solution.py:507
Async XLA Ops:
  2.9 17.7 %collective-permute-start = (f32[91,8,128]{2,1,0:T(8,128)S(1)}, f32[91,8,128]{2,1,0:T(8,128)S(1)}, u32[]{:S(2)}, u32[]{:S(2)}) collective-permute-start(f32[91,8,128]{2,1,0:T(8,128)S(1)} %get-tuple-element.16.refs_4_), channel_id=1, source_target_pairs={{16,0},{0,16},{17,1},{1,17},{18,2},{2,18},{19,3},{3,19},{20,4},{4,... | collective-permute-start | bytes 1118216 | tf_op jit(solution)/shard_map/ppermute | solution.py:482
  5.9 7.5 %collective-permute-start.1 = (f32[8,8,128]{2,1,0:T(8,128)S(1)}, f32[8,8,128]{2,1,0:T(8,128)S(1)}, u32[]{:S(2)}, u32[]{:S(2)}) collective-permute-start(f32[8,8,128]{2,1,0:T(8,128)S(1)} %get-tuple-element.17), channel_id=1, source_target_pairs={{0,1},{1,0},{2,3},{3,2},{4,5},{5,4},{6,7},{7,6},{8,9},{9,8},{10,11... | collective-permute-start | bytes 98312 | tf_op jit(solution)/shard_map/ppermute | solution.py:486
  5.9 9.3 %collective-permute-start.3 = (f32[8,8,128]{2,1,0:T(8,128)S(1)}, f32[8,8,128]{2,1,0:T(8,128)S(1)}, u32[]{:S(2)}, u32[]{:S(2)}) collective-permute-start(f32[8,8,128]{2,1,0:T(8,128)S(1)} %get-tuple-element.18), channel_id=1, source_target_pairs={{0,0},{1,2},{2,1},{3,4},{4,3},{5,6},{6,5},{7,8},{8,7},{9,10},{10,9... | collective-permute-start | bytes 98312 | tf_op jit(solution)/shard_map/ppermute | solution.py:487
  6.5 14.0 %all-to-all-start = ((f32[32,2,128]{2,1,0:T(2,128)}), f32[32,2,128]{2,1,0:T(2,128)S(1)}, u32[]{:S(2)}, u32[]{:S(2)}) async-start(f32[32,2,128]{2,1,0:T(2,128)} %get-tuple-element.12), calls=%async_computation | async-start | bytes 65536 | tf_op jit(solution)/shard_map/all_to_all | solution.py:489
  13.4 7.2 %collective-permute-start.2 = (f32[8,8,128]{2,1,0:T(8,128)S(1)}, f32[8,8,128]{2,1,0:T(8,128)S(1)}, u32[]{:S(2)}, u32[]{:S(2)}) collective-permute-start(f32[8,8,128]{2,1,0:T(8,128)S(1)} %collective-permute-done.1.refs_6_), channel_id=1, source_target_pairs={{16,0},{0,16},{17,1},{1,17},{18,2},{2,18},{19,3},{3,19},{20,4},{4,... | collective-permute-start | bytes 98312 | tf_op jit(solution)/shard_map/ppermute | solution.py:482
  15.2 5.4 %collective-permute-start.4 = (f32[8,8,128]{2,1,0:T(8,128)S(1)}, f32[8,8,128]{2,1,0:T(8,128)S(1)}, u32[]{:S(2)}, u32[]{:S(2)}) collective-permute-start(f32[8,8,128]{2,1,0:T(8,128)S(1)} %collective-permute-done.3.refs_8_), channel_id=1, source_target_pairs={{16,0},{0,16},{17,1},{1,17},{18,2},{2,18},{19,3},{3,19},{20,4},{4,... | collective-permute-start | bytes 98312 | tf_op jit(solution)/shard_map/ppermute | solution.py:482

commit v3 on v2

--- a/solution.py
+++ b/solution.py
@@ -17,9 +17,11 @@
 
 PRESS, MOB, PERM, ACC, INV, COEF = 0, 1, 4, 5, 8, 9
 BULK = 15
-DINV, DCOL, OFFC = 0, 9, 12
-EDGE = 30
+DINV, DCOL, OFFC, EACC = 0, 9, 12, 30
+EDGE = 33
 EDGE_AT = BULK * WIDE
+WATER, GAS, SENT = 2, 3, 4
+SUM, INNER = 7, 8
 NT = (((1,), (1,)), ((), ()))
 NN = (((1,), (0,)), ((), ()))
 
@@ -43,6 +45,12 @@
     return jnp.where(condition, 1.0, 0.0).astype(jnp.bfloat16)
 
 
+def sent_tiles(cx, layers):
+    inner = SENT * cx
+    edges = inner + INNER * (cx - layers)
+    return inner, edges, edges + EDGE * layers, edges + EDGE * layers + 1
+
+
 def window(count, cx):
     reach = -(-WIDE // cx)
     if count <= 2 * reach + 1:
@@ -55,11 +63,11 @@
     count_y,
     *refs,
 ):
-    sources, (wells_out, block_out, ya_out, yb_out, dinv_out) = refs[:11], refs[11:16]
-    diag_ref, off_ref = refs[16:18]
-    press_ref, sat_ref, old_ref, pore_ref, perm_ref = refs[18:23]
-    cell_ref, well_ref, index_ref, rate_ref, sems = refs[23:]
-    targets = (*refs[18:23], diag_ref, off_ref, *refs[23:27])
+    sources, (wells_hbm, block_out, own_out, ya_out, yb_out, dinv_out) = refs[:11], refs[11:17]
+    diag_ref, off_ref = refs[17:19]
+    press_ref, sat_ref, old_ref, pore_ref, perm_ref = refs[19:24]
+    cell_ref, well_ref, index_ref, rate_ref, wells_out, sems = refs[24:]
+    targets = (*refs[19:24], diag_ref, off_ref, *refs[24:28])
     copies = []
     for i in (7, 8, 9, 10, 0, 1, 4, 2, 3, 5, 6):
         copies.append(pltpu.make_async_copy(sources[i], targets[i], sems.at[i]))
@@ -70,7 +78,7 @@
     at_x = lax.axis_index("gx")
     at_y = lax.axis_index("gy")
     layers = 1 if count_x == 2 else 2
-    last = block_out.shape[0] - 1
+    inner_at, edge_at, last, _ = sent_tiles(cx, layers)
 
     press = press_ref[...]
     water, gas = sat_ref[0], sat_ref[1]
@@ -112,6 +120,8 @@
     rates = jnp.sum(jnp.where(mine, column, 0.0), axis=0, keepdims=True)
     pair = sums[:2] - jnp.where(iota((2, wells), 0) == 1, rates, 0.0)
     wells_out[...] = jnp.broadcast_to(pair[None], wells_out.shape)
+    wells_copy = pltpu.make_async_copy(wells_out, wells_hbm, sems.at[11])
+    wells_copy.start()
 
     perf_rows = [
         spot_xz.astype(f32),
@@ -123,6 +133,7 @@
     ]
     for r, values in enumerate(perf_rows):
         block_out[last, r : r + 1, :] = values
+        own_out[BULK * cx, r : r + 1, :] = values
         ya_out[cx, r : r + 1, :] = values
         yb_out[cx, r : r + 1, :] = values
 
@@ -157,19 +168,28 @@
     edge = solve + [diag[c][0] for c in range(3)] + [columns[q][c] for q in range(6) for c in range(3)]
 
     for f in range(BULK):
-        block_out[f * cx : (f + 1) * cx] = bulk[f]
-    base = BULK * cx
-    for e in range(EDGE):
+        own_out[f * cx : (f + 1) * cx] = bulk[f]
+    for i, values in enumerate((press, perm_ref[...], water, gas)):
+        block_out[i * cx : (i + 1) * cx] = values
+    inner = [*coefs, inverse, accumulated[0] + accumulated[1] + accumulated[2]]
+    for i in range(INNER):
+        for x in range(cx - layers):
+            at = inner_at + i * (cx - layers) + x
+            if layers == 1:
+                block_out[at] = jnp.where(at_x == 0, inner[i][x], inner[i][x + 1])
+            else:
+                block_out[at] = inner[i][x + 1]
+    for e, values in enumerate(edge + accumulated):
         if layers == 1:
-            block_out[base + e] = jnp.where(at_x == 0, edge[e][cx - 1], edge[e][0])
+            block_out[edge_at + e] = jnp.where(at_x == 0, values[cx - 1], values[0])
         else:
-            block_out[base + e] = edge[e][0]
-            block_out[base + EDGE + e] = edge[e][cx - 1]
+            block_out[edge_at + e] = values[0]
+            block_out[edge_at + EDGE + e] = values[cx - 1]
 
     lane = iota((nz, cy), 1)
     to_left = [jnp.zeros((nz, cy), f32) for _ in range(cx)]
     to_right = [jnp.zeros((nz, cy), f32) for _ in range(cx)]
-    for f in range(BULK + EDGE):
+    for f in range(BULK + EACC):
         wide = WIDE if f < BULK else 1
         shift = f * WIDE if f < BULK else EDGE_AT + f - BULK
         on_left = (lane >= shift) & (lane < shift + wide)
@@ -181,21 +201,21 @@
             to_left[x] = jnp.where(on_left, turned, to_left[x])
             to_right[x] = jnp.where(on_right, turned, to_right[x])
     for spare in range(cx + 1, 2 * cx):
-        ya_out[spare] = jnp.zeros((nz, cy), f32)
         yb_out[spare] = jnp.zeros((nz, cy), f32)
     even = lax.rem(at_y, 2) == 0
     for x in range(cx):
         ya_out[x] = jnp.where(even, to_right[x], to_left[x])
         yb_out[x] = jnp.where(even, to_left[x], to_right[x])
+    wells_copy.wait()
 
 
 def main_kernel(count_x, count_y, offsets, *refs):
     width = len(offsets)
-    (wells_ref, diag_ref, off_ref, dinv_ref), refs = refs[:4], refs[4:]
-    blocks, refs = refs[:width], refs[width:]
+    (wells_ref, diag_ref, off_ref, dinv_ref, own_ref), refs = refs[:5], refs[5:]
+    blocks, refs = (None, *refs[: width - 1]), refs[width - 1 :]
     ya_refs, refs = refs[:width], refs[width:]
     yb_refs, refs = refs[:width], refs[width:]
-    residual_out, z_out, sums_out = refs
+    residual_hbm, z_out, sums_out, residual_out, sem = refs
 
     cx, nz, cy = residual_out.shape[1:]
     total = width * cx
@@ -205,7 +225,7 @@
     has_left = jnp.where(at_y > 0, 1.0, 0.0).astype(f32)
     has_right = jnp.where(at_y < count_y - 1, 1.0, 0.0).astype(f32)
     layers = 1 if count_x == 2 else 2
-    last = BULK * cx + layers * EDGE
+    inner_at, edge_at, last, _ = sent_tiles(cx, layers)
     index_x = [lax.rem(at_x + (o % count_x), count_x) for o in offsets]
     joined = [
         jnp.where(index_x[(j + 1) % width] == index_x[j] + 1, 1.0, 0.0).astype(f32)
@@ -214,7 +234,7 @@
 
     from_left, from_right = [], []
     for j in range(width):
-        first, second = ya_refs[j][...], yb_refs[j][...]
+        first, second = ya_refs[j][: cx + 1], yb_refs[j][: cx + 1]
         from_right.append(jnp.where(even, first, second) * has_right)
         from_left.append(jnp.where(even, second, first) * has_left)
     lane = iota((nz, cy), 1)
@@ -226,8 +246,55 @@
             left, right = pltpu.roll(left, back, 1), pltpu.roll(right, back, 1)
         return jnp.where(lane < wide, right, jnp.where(lane >= cy - wide, left, 0.0))
 
+    def arranged(edges, inner):
+        if layers == 2:
+            return jnp.stack([edges[0], *inner, edges[1]])
+        first = [edges[0], *inner]
+        second = [*inner, edges[0]]
+        return jnp.stack([jnp.where(at_x == 0, a, b) for a, b in zip(first, second)])
+
+    def received(j):
+        block = blocks[j]
+        press, perm, water, gas = (block[i * cx : (i + 1) * cx] for i in range(SENT))
+        oil = 1.0 - water - gas
+        edges = [
+            [block[edge_at + side * EDGE + e] for e in range(EDGE)] for side in range(layers)
+        ]
+        inner = [
+            [block[inner_at + i * (cx - layers) + x] for x in range(cx - layers)]
+            for i in range(INNER)
+        ]
+        zero = jnp.zeros((nz, cy), f32)
+        acc = [
+            arranged(
+                [edge[EACC + c] for edge in edges], inner[SUM] if c == 0 else [zero] * (cx - layers)
+            )
+            for c in range(3)
+        ]
+        scale = [1.0 / (edge[DCOL] + edge[DCOL + 1] + edge[DCOL + 2]) for edge in edges]
+        coefs = [
+            arranged(
+                [
+                    (edge[OFFC + 3 * q] + edge[OFFC + 3 * q + 1] + edge[OFFC + 3 * q + 2]) * by
+                    for edge, by in zip(edges, scale)
+                ],
+                inner[q],
+            )
+            for q in range(6)
+        ]
+        mobile = [
+            water * water / viscosity[0],
+            oil * oil / viscosity[1],
+            gas * gas / viscosity[2],
+        ]
+        return [press, *mobile, perm, *acc, arranged(scale, inner[6]), *coefs]
+
+    others = [received(j) for j in range(1, width)]
+
     def extended(f):
-        own = jnp.concatenate([blocks[j][f * cx : (f + 1) * cx] for j in range(width)], axis=0)
+        own = jnp.concatenate(
+            [own_ref[f * cx : (f + 1) * cx], *[other[f] for other in others]], axis=0
+        )
         side = jnp.stack(
             [
                 halo(from_left[j], from_right[j], x, f * WIDE, WIDE)
@@ -291,13 +358,18 @@
             resid[c] = resid[c] + passing - backward(passing)
 
     wells = wells_ref.shape[2]
-    perfs = blocks[0].shape[2]
+    perfs = own_ref.shape[2]
     added = [[] for _ in range(3)]
     for j in range(width):
         pair = jnp.sum(wells_ref[pl.ds(index_x[j] * count_y, count_y)], axis=0)
         hole = pair[1:2] / pair[0:1]
         tiles = jnp.concatenate(
-            [blocks[j][last], from_left[j][cx], from_right[j][cx]], axis=1
+            [
+                blocks[j][last] if j else own_ref[BULK * cx],
+                from_left[j][cx],
+                from_right[j][cx],
+            ],
+            axis=1,
         )
         spot_xz, spot_y, well = tiles[0:1], tiles[1:2], tiles[2:3]
         member = jnp.where(iota((wells, 3 * perfs), 0).astype(f32) == well, 1.0, 0.0)
@@ -328,6 +400,8 @@
     start = [-(resid[c] + jnp.concatenate(added[c], axis=0)) for c in range(3)]
     for c in range(3):
         residual_out[c] = -start[c][:cx, :, :cy]
+    residual_copy = pltpu.make_async_copy(residual_out, residual_hbm, sem)
+    residual_copy.start()
 
     coefs = [extended(COEF + q) for q in range(6)]
     coefs[0] = seam_before(coefs[0])
@@ -375,15 +449,14 @@
             [halo(from_left[0], from_right[0], x, EDGE_AT + e, 1) for x in range(cx)]
         )
 
-    base = BULK * cx
     after, before = 1 % width, width - 1
     z_own = direction(edge_own, lambda v: v[:cx, :, :cy])
     z_side = direction(edge_side, lambda v: v[:cx, :, cy:])
     z_next = direction(
-        lambda e: blocks[after][base + e], lambda v: v[after * cx, :, :cy]
+        lambda e: blocks[after][edge_at + e], lambda v: v[after * cx, :, :cy]
     )
     z_last = direction(
-        lambda e: blocks[before][base + (layers - 1) * EDGE + e],
+        lambda e: blocks[before][edge_at + (layers - 1) * EDGE + e],
         lambda v: v[before * cx + cx - 1, :, :cy],
     )
     level_own = iota((cx, nz, cy), 1)
@@ -416,6 +489,7 @@
     square = jnp.sum(square, axis=0, keepdims=True)
     pair = jnp.where(iota((2, cy), 0) == 0, along, square)
     sums_out[...] = jnp.broadcast_to(pair[None], sums_out.shape)
+    residual_copy.wait()
 
 
 def after_kernel(sums_ref, z_ref, update_out):
@@ -423,6 +497,14 @@
     both = jnp.sum(pair, axis=1, keepdims=True)
     step = both[0:1] / both[1:2]
     update_out[...] = z_ref[...] * step[None, None]
+
+
+def other_pair(device, count_x, count_y):
+    x, y = divmod(device, count_y)
+    near = y + 1 if y % 2 else y - 1
+    if 0 <= near < count_y:
+        return x * count_y + near
+    return (x ^ 1) * count_y + y if count_x % 2 == 0 else device
 
 
 def body(
@@ -443,7 +525,7 @@
     cx, nz, cy = pressure.shape
     wells = well_rate.shape[1] * count_y
     layers = 1 if count_x == 2 else 2
-    tiles = BULK * cx + layers * EDGE + 1
+    tiles = sent_tiles(cx, layers)[-1]
     offsets = window(count_x, cx)
     width = len(offsets)
     shape = jax.ShapeDtypeStruct
@@ -453,14 +535,15 @@
 
     fields = (pressure, saturation, saturation_old, pore_volume, permeability, jac_diag)
     perforations = (perf_cell, perf_well, perf_index, well_rate)
-    wells_part, block, ya, yb, dinv, diag, off = pl.pallas_call(
+    wells_part, block, own, ya, yb, dinv, diag, off = pl.pallas_call(
         functools.partial(before_kernel, count_x, count_y),
         in_specs=[anywhere] * 11,
-        out_specs=[whole] * 7,
+        out_specs=[anywhere, *[whole] * 7],
         out_shape=[
-            shape((devices, 2, wells), f32),
+            pltpu.HBM((devices, 2, wells), f32),
             shape((tiles, nz, cy), f32),
-            shape((2 * cx, nz, cy), f32),
+            shape((BULK * cx + 1, nz, cy), f32),
+            shape((cx + 1, nz, cy), f32),
             shape((2 * cx, nz, cy), f32),
             shape((9, cx, nz, cy), f32),
             shape(jac_diag.shape, f32),
@@ -469,14 +552,15 @@
         scratch_shapes=[
             *[pltpu.VMEM(v.shape, v.dtype) for v in fields[:5]],
             *[pltpu.VMEM(v.shape, v.dtype) for v in perforations],
-            pltpu.SemaphoreType.DMA((11,)),
+            pltpu.VMEM((devices, 2, wells), f32),
+            pltpu.SemaphoreType.DMA((12,)),
         ],
         compiler_params=params,
         name="before",
     )(*[pltpu.with_memory_space_constraint(v, pltpu.HBM) for v in (*fields, jac_off, *perforations)])
 
     pairs = [(i, i ^ 1) for i in range(count_y)]
-    others = [(i, min(i + 1, count_y - 1) if i % 2 else max(i - 1, 0)) for i in range(count_y)]
+    others = [(i, other_pair(i, count_x, count_y)) for i in range(devices)]
 
     def from_x(values, offset):
         return lax.ppermute(
@@ -484,8 +568,8 @@
         )
 
     ya_got = lax.ppermute(ya, "gy", pairs)
-    yb_got = lax.ppermute(yb, "gy", others)
-    blocks = [block] + [from_x(block, o) for o in offsets[1:]]
+    yb_got = lax.ppermute(yb, ("gx", "gy"), others)
+    blocks = [from_x(block, o) for o in offsets[1:]]
     wells_all = lax.all_to_all(wells_part, ("gx", "gy"), 0, 0)
     ya_all = [ya_got] + [from_x(ya_got, o) for o in offsets[1:]]
     yb_all = [yb_got] + [from_x(yb_got, o) for o in offsets[1:]]
@@ -493,15 +577,16 @@
     residual, direction, sums = pl.pallas_call(
         functools.partial(main_kernel, count_x, count_y, tuple(offsets)),
         in_specs=[whole] * (4 + 3 * width),
-        out_specs=[whole] * 3,
+        out_specs=[anywhere, whole, whole],
         out_shape=[
-            shape((3, cx, nz, cy), f32),
+            pltpu.HBM((3, cx, nz, cy), f32),
             shape((3, cx, nz, cy), f32),
             shape((devices, 2, cy), f32),
         ],
+        scratch_shapes=[pltpu.VMEM((3, cx, nz, cy), f32), pltpu.SemaphoreType.DMA],
         compiler_params=params,
         name="main",
-    )(wells_all, diag, off, dinv, *blocks, *ya_all, *yb_all)
+    )(wells_all, diag, off, dinv, own, *blocks, *ya_all, *yb_all)
 
     sums_all = lax.all_to_all(sums, ("gx", "gy"), 0, 0)
     update = pl.pallas_call(

time: 33.6 us -> 31.7 us (0.943)
  starting transfers between devices: 12.5 us -> 10.6 us
  Pallas kernels: 4.86 us -> 4.4 us
  waiting for transfers between devices: 5.16 us -> 5.5 us
    all_to_all x1, waiting for transfers between devices: 5.14 us -> 0.01 us  [body(): wells_all = lax.all_to_all(wells_part, ('gx', 'gy'), 0, 0)]
    ppermute x3, waiting for transfers between devices: 0.01 us -> 3.55 us  [from_x(): lax.ppermute(values, 'gx', [((i + offset) % count_x, i) for i in range(co...]
    ppermute x1, waiting for transfers between devices: 0.01 us -> 1.95 us  [body(): yb_got = lax.ppermute(yb, ('gx', 'gy'), others)]
    all_to_all x1, starting transfers between devices: 6.79 us -> 5.19 us  [body(): wells_all = lax.all_to_all(wells_part, ('gx', 'gy'), 0, 0)]
    ppermute x1, starting transfers between devices: 0.65 us -> 0.08 us  [body(): yb_got = lax.ppermute(yb, ('gx', 'gy'), others)]
  transfers between devices with their start and end apart: 6 -> 6, of which waited for: 1 -> 2; matrix products, arithmetic and copies ran while one was open for 0% -> 0% of each run, Pallas kernels for 0% -> 0%
where the time goes in v3:
time: 31.7 us; the launch traced here: 31.5 us
  starting transfers between devices  10.6 us (33%)
  blocking collectives  10.3 us (32%)
  waiting for transfers between devices  5.5 us (17%)
  Pallas kernels  4.4 us (14%)
  between operations  0.67 us (2%)
    all_to_all x1, blocking collectives, body(): sums_all = lax.all_to_all(sums, ('gx', 'gy'), 0, 0)  10.3 us
    all_to_all x1, starting transfers between devices, body(): wells_all = lax.all_to_all(wells_part, ('gx', 'gy'), 0, 0)  5.19 us
    ppermute x3, starting transfers between devices, from_x(): lax.ppermute(values, 'gx', [((i + offset) % count_x, i) for i in range(co...  5.03 us
    ppermute x3, waiting for transfers between devices, from_x(): lax.ppermute(values, 'gx', [((i + offset) % count_x, i) for i in range(co...  3.55 us
    pallas_call x1, Pallas kernels, body(): pl.pallas_call(functools.partial(before_kernel, count_x, count_y), in_spe...  1.99 us
    ppermute x1, waiting for transfers between devices, body(): yb_got = lax.ppermute(yb, ('gx', 'gy'), others)  1.95 us
    pallas_call x1, Pallas kernels, body(): pl.pallas_call(functools.partial(main_kernel, count_x, count_y, tuple(off...  1.64 us
    pallas_call x1, Pallas kernels, body(): pl.pallas_call(after_kernel, in_specs=[whole] * 2, out_specs=whole, out_s...  0.78 us
  transfers between devices with their start and end apart: 6, of which 2 were waited for; matrix products, arithmetic and copies ran while one was open for 0% of the time, Pallas kernels for 0%

profile of v3, /device:TPU:0, one launch (start us, length us, event | category | flops | bytes accessed | tf_op | source)
XLA Modules:
  0.0 31.5 jit_solution(17167485675932830477)
XLA Ops:
  0.6 2.0 %before.1 = (f32[32,2,128]{2,1,0:T(2,128)}, f32[74,8,128]{2,1,0:T(8,128)S(1)}, f32[61,8,128]{2,1,0:T(8,128)S(1)}, f32[5,8,128]{2,1,0:T(8,128)S(1)}, f32[8,8,128]...) custom-call(f32[4,8,128]{2,1,0:T(8,128)} %refs_0_.1, ...), custom_call_target="tpu_custom_call" | custom-call | tf_op jit(solution)/shard_map/before/pallas_call | solution.py:538
  2.6 3.0 %collective-permute-start = (f32[74,8,128]{2,1,0:T(8,128)S(1)}, f32[74,8,128]{2,1,0:T(8,128)S(1)}, u32[]{:S(2)}, u32[]{:S(2)}) collective-permute-start(f32[74,8,128]{2,1,0:T(8,128)S(1)} %get-tuple-element.18), channel_id=1, source_target_pairs={{16,0},{0,16},{17,1},{1,17},{18,2},{2,18},{19,3},{3,19},{20,4},{4,... | collective-permute-start | bytes 909320 | tf_op jit(solution)/shard_map/ppermute | solution.py:566
  5.6 0.1 collective-permute-start.3
  5.7 5.2 %all-to-all-start = ((f32[32,2,128]{2,1,0:T(2,128)}), f32[32,2,128]{2,1,0:T(2,128)S(1)}, u32[]{:S(2)}, u32[]{:S(2)}) async-start(f32[32,2,128]{2,1,0:T(2,128)} %get-tuple-element.13), calls=%async_computation | async-start | bytes 65536 | tf_op jit(solution)/shard_map/all_to_all | solution.py:573
  10.9 0.3 %collective-permute-start.1 = (f32[5,8,128]{2,1,0:T(8,128)S(1)}, f32[5,8,128]{2,1,0:T(8,128)S(1)}, u32[]{:S(2)}, u32[]{:S(2)}) collective-permute-start(f32[5,8,128]{2,1,0:T(8,128)S(1)} %get-tuple-element.19), channel_id=1, source_target_pairs={{0,1},{1,0},{2,3},{3,2},{4,5},{5,4},{6,7},{7,6},{8,9},{9,8},{10,11... | collective-permute-start | bytes 61448 | tf_op jit(solution)/shard_map/ppermute | solution.py:570
  11.2 1.9 %collective-permute-done.3.refs_8_ = f32[8,8,128]{2,1,0:T(8,128)S(1)} collective-permute-done((f32[8,8,128]{2,1,0:T(8,128)S(1)}, f32[8,8,128]{2,1,0:T(8,128)S(1)}, u32[]{:S(2)}, u32[]{:S(2)}) %collective-permute-start.3) | collective-permute-done | bytes 32800 | tf_op jit(solution)/shard_map/ppermute | solution.py:571
  13.2 1.8 %collective-permute-start.4 = (f32[8,8,128]{2,1,0:T(8,128)S(1)}, f32[8,8,128]{2,1,0:T(8,128)S(1)}, u32[]{:S(2)}, u32[]{:S(2)}) collective-permute-start(f32[8,8,128]{2,1,0:T(8,128)S(1)} %collective-permute-done.3.refs_8_), channel_id=1, source_target_pairs={{16,0},{0,16},{17,1},{1,17},{18,2},{2,18},{19,3},{3,19},{20,4},{4,... | collective-permute-start | bytes 98312 | tf_op jit(solution)/shard_map/ppermute | solution.py:566
  15.0 0.0 collective-permute-done.1.refs_6_
  15.0 0.2 collective-permute-start.2
  15.2 3.5 %collective-permute-done.2.refs_7_ = f32[5,8,128]{2,1,0:T(8,128)S(1)} collective-permute-done((f32[5,8,128]{2,1,0:T(8,128)S(1)}, f32[5,8,128]{2,1,0:T(8,128)S(1)}, u32[]{:S(2)}, u32[]{:S(2)}) %collective-permute-start.2) | collective-permute-done | bytes 20512 | tf_op jit(solution)/shard_map/ppermute | solution.py:566
  18.7 0.0 all-to-all-done.refs_0_
  18.7 0.0 collective-permute-done.4.refs_9_
  18.7 0.0 collective-permute-done.refs_5_
  18.8 1.6 %main.1 = (f32[3,4,8,128]{3,2,1,0:T(8,128)}, f32[3,4,8,128]{3,2,1,0:T(8,128)S(1)}, f32[32,2,128]{2,1,0:T(2,128)S(1)}) custom-call(f32[32,2,128]{2,1,0:T(2,128)S(1)} %all-to-all-done.refs_0_, f32[3,3,4,8,128]{4,3,2,1,0:T(8,128)S(1)} %get-tuple-element.14.refs_1_, f32[6,3,3,4,8,128]{5,4,3,2,1,0:T(8,128)S(1)} %get-tuple-element.15.refs_2_, ...), custom_call_target="tpu_custom_call" | custom-call | tf_op jit(solution)/shard_map/main/pallas_call | solution.py:577
  20.4 10.3 %all_to_all.10.sums_ref = f32[32,2,128]{2,1,0:T(2,128)S(1)} all-to-all(f32[32,2,128]{2,1,0:T(2,128)S(1)} %get-tuple-element.22), channel_id=1, replica_groups=mesh['gx'=2,'gy'=16] {'gx','gy'}, dimensions={0} | all-to-all | bytes 65536 | tf_op jit(solution)/shard_map/all_to_all | solution.py:591
  30.7 0.8 %after.1 = f32[3,4,8,128]{3,2,1,0:T(8,128)} custom-call(f32[32,2,128]{2,1,0:T(2,128)S(1)} %all_to_all.10.sums_ref, f32[3,4,8,128]{3,2,1,0:T(8,128)S(1)} %get-tuple-element.23.z_ref), custom_call_target="tpu_custom_call" | custom-call | tf_op jit(solution)/shard_map/after/pallas_call | solution.py:592
Async XLA Ops:
  2.6 16.1 %collective-permute-start = (f32[74,8,128]{2,1,0:T(8,128)S(1)}, f32[74,8,128]{2,1,0:T(8,128)S(1)}, u32[]{:S(2)}, u32[]{:S(2)}) collective-permute-start(f32[74,8,128]{2,1,0:T(8,128)S(1)} %get-tuple-element.18), channel_id=1, source_target_pairs={{16,0},{0,16},{17,1},{1,17},{18,2},{2,18},{19,3},{3,19},{20,4},{4,... | collective-permute-start | bytes 909320 | tf_op jit(solution)/shard_map/ppermute | solution.py:566
  5.6 7.5 %collective-permute-start.3 = (f32[8,8,128]{2,1,0:T(8,128)S(1)}, f32[8,8,128]{2,1,0:T(8,128)S(1)}, u32[]{:S(2)}, u32[]{:S(2)}) collective-permute-start(f32[8,8,128]{2,1,0:T(8,128)S(1)} %get-tuple-element.20), channel_id=1, source_target_pairs={{0,16},{1,2},{2,1},{3,4},{4,3},{5,6},{6,5},{7,8},{8,7},{9,10},{10,... | collective-permute-start | bytes 98312 | tf_op jit(solution)/shard_map/ppermute | solution.py:571
  5.7 13.0 %all-to-all-start = ((f32[32,2,128]{2,1,0:T(2,128)}), f32[32,2,128]{2,1,0:T(2,128)S(1)}, u32[]{:S(2)}, u32[]{:S(2)}) async-start(f32[32,2,128]{2,1,0:T(2,128)} %get-tuple-element.13), calls=%async_computation | async-start | bytes 65536 | tf_op jit(solution)/shard_map/all_to_all | solution.py:573
  10.9 4.0 %collective-permute-start.1 = (f32[5,8,128]{2,1,0:T(8,128)S(1)}, f32[5,8,128]{2,1,0:T(8,128)S(1)}, u32[]{:S(2)}, u32[]{:S(2)}) collective-permute-start(f32[5,8,128]{2,1,0:T(8,128)S(1)} %get-tuple-element.19), channel_id=1, source_target_pairs={{0,1},{1,0},{2,3},{3,2},{4,5},{5,4},{6,7},{7,6},{8,9},{9,8},{10,11... | collective-permute-start | bytes 61448 | tf_op jit(solution)/shard_map/ppermute | solution.py:570
  13.2 5.6 %collective-permute-start.4 = (f32[8,8,128]{2,1,0:T(8,128)S(1)}, f32[8,8,128]{2,1,0:T(8,128)S(1)}, u32[]{:S(2)}, u32[]{:S(2)}) collective-permute-start(f32[8,8,128]{2,1,0:T(8,128)S(1)} %collective-permute-done.3.refs_8_), channel_id=1, source_target_pairs={{16,0},{0,16},{17,1},{1,17},{18,2},{2,18},{19,3},{3,19},{20,4},{4,... | collective-permute-start | bytes 98312 | tf_op jit(solution)/shard_map/ppermute | solution.py:566
  15.0 3.8 %collective-permute-start.2 = (f32[5,8,128]{2,1,0:T(8,128)S(1)}, f32[5,8,128]{2,1,0:T(8,128)S(1)}, u32[]{:S(2)}, u32[]{:S(2)}) collective-permute-start(f32[5,8,128]{2,1,0:T(8,128)S(1)} %collective-permute-done.1.refs_6_), channel_id=1, source_target_pairs={{16,0},{0,16},{17,1},{1,17},{18,2},{2,18},{19,3},{3,19},{20,4},{4,... | collective-permute-start | bytes 61448 | tf_op jit(solution)/shard_map/ppermute | solution.py:566

commit v4 on v3

--- a/solution.py
+++ b/solution.py
@@ -8,20 +8,22 @@
 from jax.sharding import PartitionSpec as P
 
 SWEEPS = 4
-WIDE = SWEEPS + 2
+WIDE = SWEEPS + 1
 
 viscosity = (1.0, 2.0, 0.2)
 vertical_ratio = 0.1
 highest = lax.Precision.HIGHEST
 f32 = jnp.float32
 
-PRESS, MOB, PERM, ACC, INV, COEF = 0, 1, 4, 5, 8, 9
+PRESS, MOB, PERM, PART, INV, COEF = 0, 1, 4, 5, 8, 9
 BULK = 15
-DINV, DCOL, OFFC, EACC = 0, 9, 12, 30
-EDGE = 33
-EDGE_AT = BULK * WIDE
-WATER, GAS, SENT = 2, 3, 4
+FACE = 5
+DINV, DCOL, OFFC, EPART, EPRESS, EPERM, EWATER, EGAS = 0, 9, 12, 30, 33, 34, 35, 36
+EDGE = 37
+SEAM = 30
+BORDER_AT = (BULK * WIDE + 1) // 2 * 2
 SUM, INNER = 7, 8
+TINY = 1e-30
 NT = (((1,), (1,)), ((), ()))
 NN = (((1,), (0,)), ((), ()))
 
@@ -46,9 +48,27 @@
 
 
 def sent_tiles(cx, layers):
-    inner = SENT * cx
-    edges = inner + INNER * (cx - layers)
-    return inner, edges, edges + EDGE * layers, edges + EDGE * layers + 1
+    edges = INNER * (cx - layers)
+    borders = edges + EDGE * layers
+    return edges, borders, borders + 1, borders + 2, borders + 3 + cx
+
+
+def mobilities(water, gas):
+    oil = 1.0 - water - gas
+    return [
+        water * water / viscosity[0],
+        oil * oil / viscosity[1],
+        gas * gas / viscosity[2],
+    ]
+
+
+def face_flows(here, there, weight):
+    conduct = weight * here[PERM] * there[PERM] / (here[PERM] + there[PERM] + TINY)
+    drop = here[PRESS] - there[PRESS]
+    flow = conduct * drop
+    return [
+        flow * jnp.where(drop >= 0.0, here[MOB + c], there[MOB + c]) for c in range(3)
+    ]
 
 
 def window(count, cx):
@@ -78,16 +98,11 @@
     at_x = lax.axis_index("gx")
     at_y = lax.axis_index("gy")
     layers = 1 if count_x == 2 else 2
-    inner_at, edge_at, last, _ = sent_tiles(cx, layers)
+    edge_at, border_at, last, columns_at, _ = sent_tiles(cx, layers)
 
     press = press_ref[...]
     water, gas = sat_ref[0], sat_ref[1]
-    oil = 1.0 - water - gas
-    mobile = [
-        water * water / viscosity[0],
-        oil * oil / viscosity[1],
-        gas * gas / viscosity[2],
-    ]
+    mobile = mobilities(water, gas)
 
     cells = cell_ref[...]
     perfs = cells.shape[1]
@@ -133,24 +148,47 @@
     ]
     for r, values in enumerate(perf_rows):
         block_out[last, r : r + 1, :] = values
+        block_out[columns_at + cx, r : r + 1, :] = values
         own_out[BULK * cx, r : r + 1, :] = values
         ya_out[cx, r : r + 1, :] = values
         yb_out[cx, r : r + 1, :] = values
 
-    for copy in copies[6:]:
+    for copy in copies[6:9]:
         copy.wait()
+    perm = perm_ref[...]
     old_water, old_gas = old_ref[0], old_ref[1]
-    old_oil = 1.0 - old_water - old_gas
+    oil, old_oil = 1.0 - water - gas, 1.0 - old_water - old_gas
     pore = pore_ref[...]
-    accumulated = [pore * (water - old_water), pore * (oil - old_oil), pore * (gas - old_gas)]
+    part = [pore * (water - old_water), pore * (oil - old_oil), pore * (gas - old_gas)]
     layer_at = iota((cx, nz, cy), 1)
+    lane_at = iota((cx, nz, cy), 2)
+    cells_here = [press, *mobile, perm]
+    flows = face_flows([v[:-1] for v in cells_here], [v[1:] for v in cells_here], 2.0)
+    none = jnp.zeros((1, nz, cy), f32)
+    for c in range(3):
+        part[c] = part[c] + jnp.concatenate([flows[c], none], axis=0)
+        part[c] = part[c] - jnp.concatenate([none, flows[c]], axis=0)
+    for axis, weight, inside in (
+        (2, 2.0, lane_at < cy - 1),
+        (1, 2.0 * vertical_ratio, layer_at < nz - 1),
+    ):
+        size = cells_here[0].shape[axis]
+        flows = face_flows(
+            cells_here, [pltpu.roll(v, size - 1, axis) for v in cells_here], weight
+        )
+        for c in range(3):
+            flow = jnp.where(inside, flows[c], 0.0)
+            part[c] = part[c] + flow - pltpu.roll(flow, 1, axis)
+
+    for copy in copies[9:]:
+        copy.wait()
     columns = [[off_ref[q, c, 0] for c in range(3)] for q in range(6)]
     columns[4] = [jnp.where(layer_at > 0, v, 0.0) for v in columns[4]]
     columns[5] = [jnp.where(layer_at < nz - 1, v, 0.0) for v in columns[5]]
     diag = [[diag_ref[a, b] for b in range(3)] for a in range(3)]
     inverse = 1.0 / (diag[0][0] + diag[1][0] + diag[2][0])
     coefs = [(columns[q][0] + columns[q][1] + columns[q][2]) * inverse for q in range(6)]
-    bulk = [press, *mobile, perm_ref[...], *accumulated, inverse, *coefs]
+    bulk = [press, *mobile, perm, *part, inverse, *coefs]
 
     def cofactor(a, b):
         return (
@@ -169,17 +207,15 @@
 
     for f in range(BULK):
         own_out[f * cx : (f + 1) * cx] = bulk[f]
-    for i, values in enumerate((press, perm_ref[...], water, gas)):
-        block_out[i * cx : (i + 1) * cx] = values
-    inner = [*coefs, inverse, accumulated[0] + accumulated[1] + accumulated[2]]
+    inner = [*coefs, inverse, part[0] + part[1] + part[2]]
     for i in range(INNER):
         for x in range(cx - layers):
-            at = inner_at + i * (cx - layers) + x
+            at = i * (cx - layers) + x
             if layers == 1:
                 block_out[at] = jnp.where(at_x == 0, inner[i][x], inner[i][x + 1])
             else:
                 block_out[at] = inner[i][x + 1]
-    for e, values in enumerate(edge + accumulated):
+    for e, values in enumerate([*edge, *part, press, perm, water, gas]):
         if layers == 1:
             block_out[edge_at + e] = jnp.where(at_x == 0, values[cx - 1], values[0])
         else:
@@ -187,25 +223,47 @@
             block_out[edge_at + EDGE + e] = values[cx - 1]
 
     lane = iota((nz, cy), 1)
+    border = jnp.zeros((nz, cy), f32)
+    for f in range(FACE):
+        for x in range(cx):
+            at = BORDER_AT + 2 * (f * cx + x) + 1
+            first = pltpu.roll(bulk[f][x], at - 1, 1)
+            second = pltpu.roll(bulk[f][x], at + 1, 1)
+            border = jnp.where(lane == at - 1, first, jnp.where(lane == at, second, border))
+    block_out[border_at] = border
+    own_out[BULK * cx + 1] = border
+
     to_left = [jnp.zeros((nz, cy), f32) for _ in range(cx)]
     to_right = [jnp.zeros((nz, cy), f32) for _ in range(cx)]
-    for f in range(BULK + EACC):
-        wide = WIDE if f < BULK else 1
-        shift = f * WIDE if f < BULK else EDGE_AT + f - BULK
-        on_left = (lane >= shift) & (lane < shift + wide)
-        start = (shift - wide) % cy
-        on_right = (lane >= start) & (lane < start + wide)
-        values = bulk[f] if f < BULK else edge[f - BULK]
+    to_left[0] = to_right[0] = border
+    for f in range(BULK):
+        shift = f * WIDE
+        on_left = (lane >= shift) & (lane < shift + WIDE)
+        start = (shift - WIDE) % cy
+        on_right = (lane >= start) & (lane < start + WIDE)
         for x in range(cx):
-            turned = pltpu.roll(values[x], shift, 1) if shift else values[x]
+            turned = pltpu.roll(bulk[f][x], shift, 1) if shift else bulk[f][x]
             to_left[x] = jnp.where(on_left, turned, to_left[x])
             to_right[x] = jnp.where(on_right, turned, to_right[x])
-    for spare in range(cx + 1, 2 * cx):
-        yb_out[spare] = jnp.zeros((nz, cy), f32)
+    for group in range(0, SEAM, cy // (2 * cx)):
+        left, right = jnp.zeros((nz, cy), f32), jnp.zeros((nz, cy), f32)
+        for e in range(group, min(group + cy // (2 * cx), SEAM)):
+            for x in range(cx):
+                at = 2 * ((e - group) * cx + x) + 1
+                turned = pltpu.roll(edge[e][x], at, 1)
+                left = jnp.where(lane == at, turned, left)
+                right = jnp.where(lane == at - 1, turned, right)
+        to_left.append(left)
+        to_right.append(right)
     even = lax.rem(at_y, 2) == 0
     for x in range(cx):
-        ya_out[x] = jnp.where(even, to_right[x], to_left[x])
-        yb_out[x] = jnp.where(even, to_left[x], to_right[x])
+        block_out[columns_at + x] = jnp.where(even, to_right[x], to_left[x])
+    for t, (left, right) in enumerate(zip(to_left, to_right)):
+        at = t if t < cx else t + 1
+        ya_out[at] = jnp.where(even, right, left)
+        yb_out[at] = jnp.where(even, left, right)
+    for spare in range(len(to_left) + 1, yb_out.shape[0]):
+        yb_out[spare] = jnp.zeros((nz, cy), f32)
     wells_copy.wait()
 
 
@@ -225,7 +283,7 @@
     has_left = jnp.where(at_y > 0, 1.0, 0.0).astype(f32)
     has_right = jnp.where(at_y < count_y - 1, 1.0, 0.0).astype(f32)
     layers = 1 if count_x == 2 else 2
-    inner_at, edge_at, last, _ = sent_tiles(cx, layers)
+    edge_at, border_at, last, columns_at, _ = sent_tiles(cx, layers)
     index_x = [lax.rem(at_x + (o % count_x), count_x) for o in offsets]
     joined = [
         jnp.where(index_x[(j + 1) % width] == index_x[j] + 1, 1.0, 0.0).astype(f32)
@@ -255,19 +313,16 @@
 
     def received(j):
         block = blocks[j]
-        press, perm, water, gas = (block[i * cx : (i + 1) * cx] for i in range(SENT))
-        oil = 1.0 - water - gas
         edges = [
             [block[edge_at + side * EDGE + e] for e in range(EDGE)] for side in range(layers)
         ]
         inner = [
-            [block[inner_at + i * (cx - layers) + x] for x in range(cx - layers)]
-            for i in range(INNER)
+            [block[i * (cx - layers) + x] for x in range(cx - layers)] for i in range(INNER)
         ]
         zero = jnp.zeros((nz, cy), f32)
-        acc = [
+        part = [
             arranged(
-                [edge[EACC + c] for edge in edges], inner[SUM] if c == 0 else [zero] * (cx - layers)
+                [edge[EPART + c] for edge in edges], inner[SUM] if c == 0 else [zero] * (cx - layers)
             )
             for c in range(3)
         ]
@@ -282,12 +337,7 @@
             )
             for q in range(6)
         ]
-        mobile = [
-            water * water / viscosity[0],
-            oil * oil / viscosity[1],
-            gas * gas / viscosity[2],
-        ]
-        return [press, *mobile, perm, *acc, arranged(scale, inner[6]), *coefs]
+        return dict(enumerate([*part, arranged(scale, inner[6]), *coefs], start=PART))
 
     others = [received(j) for j in range(1, width)]
 
@@ -338,24 +388,63 @@
             rows[at] = rows[at] * joined[j]
         return jnp.stack(rows)
 
-    press = extended(PRESS)
-    mobile = [extended(MOB + c) for c in range(3)]
-    perm = extended(PERM)
-    resid = [extended(ACC + c) for c in range(3)]
-
-    for forward, backward, kind in ((next_x, last_x, 0), (next_y, last_y, 1), (next_z, last_z, 2)):
-        beyond = forward(perm)
-        bottom = perm + beyond
-        conduct = 2.0 * perm * beyond / jnp.where(bottom > 0.0, bottom, 1.0)
-        if kind == 0:
-            conduct = seam_after(conduct)
-        if kind == 2:
-            conduct = jnp.where(level < nz - 1, vertical_ratio * conduct, 0.0)
-        drop = press - forward(press)
-        flow = conduct * drop
+    resid = [extended(PART + c) for c in range(3)]
+    rows = [[resid[c][x] for x in range(total)] for c in range(3)]
+    sides = {}
+
+    def side_of(f, x):
+        if (f, x) not in sides:
+            j = x // cx
+            sides[f, x] = halo(from_left[j], from_right[j], x % cx, f * WIDE, WIDE)
+        return sides[f, x]
+
+    even_lane = lane % 2 == 0
+    ends = (lane == 0) | (lane == cy - 1)
+    for j in range(width):
+        border = blocks[j][border_at] if j else own_ref[BULK * cx + 1]
+        beyond = jnp.where(
+            even_lane, pltpu.roll(from_left[j][0], cy - 1, 1), pltpu.roll(from_right[j][0], 1, 1)
+        )
+        backs = [cy - BORDER_AT - 2 * f * cx for f in range(FACE)]
+        flows = face_flows(
+            [pltpu.roll(beyond, back, 1) for back in backs],
+            [pltpu.roll(border, back, 1) for back in backs],
+            2.0,
+        )
         for c in range(3):
-            passing = flow * jnp.where(drop >= 0.0, mobile[c], forward(mobile[c]))
-            resid[c] = resid[c] + passing - backward(passing)
+            flow = jnp.where(lane < 2 * cx, flows[c], 0.0)
+            swapped = jnp.where(even_lane, pltpu.roll(flow, cy - 1, 1), pltpu.roll(flow, 1, 1))
+            for x in range(cx):
+                back = cy - 2 * x - 1
+                inward = jnp.where(ends, pltpu.roll(swapped, back, 1), 0.0)
+                outward = jnp.where(ends, pltpu.roll(flow, back, 1), 0.0)
+                at = j * cx + x
+                rows[c][at] = rows[c][at] + jnp.concatenate([-inward, outward], axis=1)
+
+    def edge_cells(j, last_layer):
+        x = cx - 1 if last_layer else 0
+        if j == 0:
+            inside = [own_ref[f * cx + x] for f in range(FACE)]
+        else:
+            at = edge_at + (EDGE if last_layer and layers == 2 else 0)
+            water, gas = blocks[j][at + EWATER], blocks[j][at + EGAS]
+            inside = [
+                blocks[j][at + EPRESS],
+                *mobilities(water, gas),
+                blocks[j][at + EPERM],
+            ]
+        return [
+            jnp.concatenate([inside[f], side_of(f, j * cx + x)], axis=1) for f in range(FACE)
+        ]
+
+    for j in range(width):
+        after = (j + 1) % width
+        flows = face_flows(edge_cells(j, True), edge_cells(after, False), 2.0 * joined[j])
+        for c in range(3):
+            near_x, far_x = j * cx + cx - 1, after * cx
+            rows[c][near_x] = rows[c][near_x] + flows[c]
+            rows[c][far_x] = rows[c][far_x] - flows[c]
+    resid = [jnp.stack(rows[c]) for c in range(3)]
 
     wells = wells_ref.shape[2]
     perfs = own_ref.shape[2]
@@ -372,14 +461,8 @@
             axis=1,
         )
         spot_xz, spot_y, well = tiles[0:1], tiles[1:2], tiles[2:3]
-        member = jnp.where(iota((wells, 3 * perfs), 0).astype(f32) == well, 1.0, 0.0)
-        hole_at = lax.dot_general(
-            jnp.broadcast_to(hole, (8, wells)),
-            member,
-            NN,
-            precision=highest,
-            preferred_element_type=f32,
-        )[0:1]
+        member = hot_of(iota((wells, 3 * perfs), 0).astype(f32) == well)
+        hole_at = split_dot(jnp.broadcast_to(hole, (16, wells)), member, NN)[0:1]
         fall = tiles[6:7] - hole_at
         on_xz = iota((cx * nz, 3 * perfs), 0).astype(f32) == spot_xz
         spread = jnp.concatenate(
@@ -444,21 +527,42 @@
             return diag_ref[e - DCOL, 0]
         return off_ref[(e - OFFC) // 3, (e - OFFC) % 3, 0]
 
+    beside = []
+    for t in range(cx + 1, cx + 1 - (-SEAM * 2 * cx // cy)):
+        one, two = ya_refs[0][t], yb_refs[0][t]
+        left, right = jnp.where(even, two, one), jnp.where(even, one, two)
+        beside.append(jnp.where(even_lane, left, right))
+
     def edge_side(e):
-        return jnp.stack(
-            [halo(from_left[0], from_right[0], x, EDGE_AT + e, 1) for x in range(cx)]
-        )
+        tile, place = divmod(2 * cx * e, cy)
+        return pltpu.roll(beside[tile], cy - place, 1) if place else beside[tile]
+
+    def gathered_side(v):
+        packed = jnp.zeros((nz, cy), f32)
+        for x in range(cx):
+            turned = pltpu.roll(v[x, :, cy:], 2 * x + 1, 1)
+            packed = jnp.where((lane >= 2 * x) & (lane < 2 * x + 2), turned, packed)
+        return packed
 
     after, before = 1 % width, width - 1
     z_own = direction(edge_own, lambda v: v[:cx, :, :cy])
-    z_side = direction(edge_side, lambda v: v[:cx, :, cy:])
-    z_next = direction(
-        lambda e: blocks[after][edge_at + e], lambda v: v[after * cx, :, :cy]
-    )
-    z_last = direction(
-        lambda e: blocks[before][edge_at + (layers - 1) * EDGE + e],
-        lambda v: v[before * cx + cx - 1, :, :cy],
-    )
+    z_side = [
+        jnp.stack([pltpu.roll(v, cy - 2 * x - 1, 1) for x in range(cx)])
+        for v in direction(edge_side, gathered_side)
+    ]
+    if layers == 1:
+        z_next = z_last = direction(
+            lambda e: blocks[after][edge_at + e],
+            lambda v: jnp.where(at_x == 0, v[cx, :, :cy], v[total - 1, :, :cy]),
+        )
+    else:
+        z_next = direction(
+            lambda e: blocks[after][edge_at + e], lambda v: v[after * cx, :, :cy]
+        )
+        z_last = direction(
+            lambda e: blocks[before][edge_at + EDGE + e],
+            lambda v: v[before * cx + cx - 1, :, :cy],
+        )
     level_own = iota((cx, nz, cy), 1)
     around = []
     for k in range(3):
@@ -525,7 +629,8 @@
     cx, nz, cy = pressure.shape
     wells = well_rate.shape[1] * count_y
     layers = 1 if count_x == 2 else 2
-    tiles = sent_tiles(cx, layers)[-1]
+    columns_at, tiles = sent_tiles(cx, layers)[-2:]
+    groups = -(-SEAM * 2 * cx // cy)
     offsets = window(count_x, cx)
     width = len(offsets)
     shape = jax.ShapeDtypeStruct
@@ -542,9 +647,9 @@
         out_shape=[
             pltpu.HBM((devices, 2, wells), f32),
             shape((tiles, nz, cy), f32),
-            shape((BULK * cx + 1, nz, cy), f32),
-            shape((cx + 1, nz, cy), f32),
-            shape((2 * cx, nz, cy), f32),
+            shape((BULK * cx + 2, nz, cy), f32),
+            shape((cx + 1 + groups, nz, cy), f32),
+            shape((max(cx + 1 + groups, 2 * cx), nz, cy), f32),
             shape((9, cx, nz, cy), f32),
             shape(jac_diag.shape, f32),
             shape(jac_off.shape, f32),
@@ -571,7 +676,7 @@
     yb_got = lax.ppermute(yb, ("gx", "gy"), others)
     blocks = [from_x(block, o) for o in offsets[1:]]
     wells_all = lax.all_to_all(wells_part, ("gx", "gy"), 0, 0)
-    ya_all = [ya_got] + [from_x(ya_got, o) for o in offsets[1:]]
+    ya_all = [ya_got] + [lax.ppermute(v[columns_at:], "gy", pairs) for v in blocks]
     yb_all = [yb_got] + [from_x(yb_got, o) for o in offsets[1:]]
 
     residual, direction, sums = pl.pallas_call(

time: 31.7 us -> 30.3 us (0.956)
  blocking collectives: 10.3 us -> 9.71 us
  waiting for transfers between devices: 5.5 us -> 4.95 us
    ppermute x3 -> x2, waiting for transfers between devices: 3.55 us -> 0.01 us  [from_x(): lax.ppermute(values, 'gx', [((i + offset) % count_x, i) for i in range(co...]
    all_to_all x1, waiting for transfers between devices: 0.01 us -> 2.53 us  [body(): wells_all = lax.all_to_all(wells_part, ('gx', 'gy'), 0, 0)]
    ppermute x1, waiting for transfers between devices: 0.01 us -> 0.68 us  [body(): ya_got = lax.ppermute(ya, 'gy', pairs)]
    all_to_all x1, blocking collectives: 10.3 us -> 9.71 us  [body(): sums_all = lax.all_to_all(sums, ('gx', 'gy'), 0, 0)]
    ppermute x0 -> x1, starting transfers between devices: none -> 0.51 us  [body(): lax.ppermute(v[columns_at:], 'gy', pairs)]
    ppermute x3 -> x2, starting transfers between devices: 5.03 us -> 4.79 us  [from_x(): lax.ppermute(values, 'gx', [((i + offset) % count_x, i) for i in range(co...]
  transfers between devices with their start and end apart: 6 -> 6, of which waited for: 2 -> 3; matrix products, arithmetic and copies ran while one was open for 0% -> 0% of each run, Pallas kernels for 0% -> 0%
where the time goes in v4:
time: 30.3 us; the launch traced here: 30.1 us
  starting transfers between devices  10.6 us (35%)
  blocking collectives  9.71 us (32%)
  waiting for transfers between devices  4.95 us (16%)
  Pallas kernels  4.23 us (14%)
  between operations  0.67 us (2%)
    all_to_all x1, blocking collectives, body(): sums_all = lax.all_to_all(sums, ('gx', 'gy'), 0, 0)  9.71 us
    all_to_all x1, starting transfers between devices, body(): wells_all = lax.all_to_all(wells_part, ('gx', 'gy'), 0, 0)  5.19 us
    ppermute x2, starting transfers between devices, from_x(): lax.ppermute(values, 'gx', [((i + offset) % count_x, i) for i in range(co...  4.79 us
    all_to_all x1, waiting for transfers between devices, body(): wells_all = lax.all_to_all(wells_part, ('gx', 'gy'), 0, 0)  2.53 us
    pallas_call x1, Pallas kernels, body(): pl.pallas_call(functools.partial(before_kernel, count_x, count_y), in_spe...  1.99 us
    ppermute x1, waiting for transfers between devices, body(): yb_got = lax.ppermute(yb, ('gx', 'gy'), others)  1.74 us
    pallas_call x1, Pallas kernels, body(): pl.pallas_call(functools.partial(main_kernel, count_x, count_y, tuple(off...  1.47 us
    pallas_call x1, Pallas kernels, body(): pl.pallas_call(after_kernel, in_specs=[whole] * 2, out_specs=whole, out_s...  0.78 us
  transfers between devices with their start and end apart: 6, of which 3 were waited for; matrix products, arithmetic and copies ran while one was open for 0% of the time, Pallas kernels for 0%

profile of v4, /device:TPU:0, one launch (start us, length us, event | category | flops | bytes accessed | tf_op | source)
XLA Modules:
  0.0 30.1 jit_solution(1513946803208729850)
XLA Ops:
  0.6 2.0 %before.1 = (f32[32,2,128]{2,1,0:T(2,128)}, f32[68,8,128]{2,1,0:T(8,128)S(1)}, f32[62,8,128]{2,1,0:T(8,128)S(1)}, f32[7,8,128]{2,1,0:T(8,128)S(1)}, f32[8,8,128]...) custom-call(f32[4,8,128]{2,1,0:T(8,128)} %refs_0_.1, ...), custom_call_target="tpu_custom_call" | custom-call | tf_op jit(solution)/shard_map/before/pallas_call | solution.py:643
  2.6 3.0 %collective-permute-start = (f32[68,8,128]{2,1,0:T(8,128)S(1)}, f32[68,8,128]{2,1,0:T(8,128)S(1)}, u32[]{:S(2)}, u32[]{:S(2)}) collective-permute-start(f32[68,8,128]{2,1,0:T(8,128)S(1)} %get-tuple-element.18), channel_id=1, source_target_pairs={{16,0},{0,16},{17,1},{1,17},{18,2},{2,18},{19,3},{3,19},{20,4},{4,... | collective-permute-start | bytes 835592 | tf_op jit(solution)/shard_map/ppermute | solution.py:671
  5.6 0.1 collective-permute-start.3
  5.7 5.2 %all-to-all-start = ((f32[32,2,128]{2,1,0:T(2,128)}), f32[32,2,128]{2,1,0:T(2,128)S(1)}, u32[]{:S(2)}, u32[]{:S(2)}) async-start(f32[32,2,128]{2,1,0:T(2,128)} %get-tuple-element.13), calls=%async_computation | async-start | bytes 65536 | tf_op jit(solution)/shard_map/all_to_all | solution.py:678
  10.9 1.7 %collective-permute-done.3.refs_8_ = f32[8,8,128]{2,1,0:T(8,128)S(1)} collective-permute-done((f32[8,8,128]{2,1,0:T(8,128)S(1)}, f32[8,8,128]{2,1,0:T(8,128)S(1)}, u32[]{:S(2)}, u32[]{:S(2)}) %collective-permute-start.3) | collective-permute-done | bytes 32800 | tf_op jit(solution)/shard_map/ppermute | solution.py:676
  12.6 1.8 %collective-permute-start.4 = (f32[8,8,128]{2,1,0:T(8,128)S(1)}, f32[8,8,128]{2,1,0:T(8,128)S(1)}, u32[]{:S(2)}, u32[]{:S(2)}) collective-permute-start(f32[8,8,128]{2,1,0:T(8,128)S(1)} %collective-permute-done.3.refs_8_), channel_id=1, source_target_pairs={{16,0},{0,16},{17,1},{1,17},{18,2},{2,18},{19,3},{3,19},{20,4},{4,... | collective-permute-start | bytes 98312 | tf_op jit(solution)/shard_map/ppermute | solution.py:671
  14.4 0.0 collective-permute-start.1
  14.4 0.0 collective-permute-done.refs_5_
  14.4 0.5 %collective-permute-start.2 = (f32[5,8,128]{2,1,0:T(8,128)S(1)}, f32[5,8,128]{2,1,0:T(8,128)S(1)}, u32[]{:S(2)}, u32[]{:S(2)}) collective-permute-start(f32[5,8,128]{2,1,0:T(8,128)S(1)} %slice.4), channel_id=1, source_target_pairs={{0,1},{1,0},{2,3},{3,2},{4,5},{5,4},{6,7},{7,6},{8,9},{9,8},{10,11... | collective-permute-start | bytes 61448 | tf_op jit(solution)/shard_map/ppermute | solution.py:679
  14.9 0.7 %collective-permute-done.1.refs_6_ = f32[7,8,128]{2,1,0:T(8,128)S(1)} collective-permute-done((f32[7,8,128]{2,1,0:T(8,128)S(1)}, f32[7,8,128]{2,1,0:T(8,128)S(1)}, u32[]{:S(2)}, u32[]{:S(2)}) %collective-permute-start.1) | collective-permute-done | bytes 28704 | tf_op jit(solution)/shard_map/ppermute | solution.py:675
  15.6 2.5 %all-to-all-done.refs_0_ = f32[32,2,128]{2,1,0:T(2,128)S(1)} async-done(((f32[32,2,128]{2,1,0:T(2,128)}), f32[32,2,128]{2,1,0:T(2,128)S(1)}, u32[]{:S(2)}, u32[]{:S(2)}) %all-to-all-start) | async-done | bytes 32800 | tf_op jit(solution)/shard_map/all_to_all | solution.py:678
  18.2 0.0 collective-permute-done.4.refs_9_
  18.2 0.0 collective-permute-done.2.refs_7_
  18.2 1.5 %main.1 = (f32[3,4,8,128]{3,2,1,0:T(8,128)}, f32[3,4,8,128]{3,2,1,0:T(8,128)S(1)}, f32[32,2,128]{2,1,0:T(2,128)S(1)}) custom-call(f32[32,2,128]{2,1,0:T(2,128)S(1)} %all-to-all-done.refs_0_, f32[3,3,4,8,128]{4,3,2,1,0:T(8,128)S(1)} %get-tuple-element.14.refs_1_, f32[6,3,3,4,8,128]{5,4,3,2,1,0:T(8,128)S(1)} %get-tuple-element.15.refs_2_, ...), custom_call_target="tpu_custom_call" | custom-call | tf_op jit(solution)/shard_map/main/pallas_call | solution.py:682
  19.6 9.7 %all_to_all.10.sums_ref = f32[32,2,128]{2,1,0:T(2,128)S(1)} all-to-all(f32[32,2,128]{2,1,0:T(2,128)S(1)} %get-tuple-element.22), channel_id=1, replica_groups=mesh['gx'=2,'gy'=16] {'gx','gy'}, dimensions={0} | all-to-all | bytes 65536 | tf_op jit(solution)/shard_map/all_to_all | solution.py:696
  29.3 0.8 %after.1 = f32[3,4,8,128]{3,2,1,0:T(8,128)} custom-call(f32[32,2,128]{2,1,0:T(2,128)S(1)} %all_to_all.10.sums_ref, f32[3,4,8,128]{3,2,1,0:T(8,128)S(1)} %get-tuple-element.23.z_ref), custom_call_target="tpu_custom_call" | custom-call | tf_op jit(solution)/shard_map/after/pallas_call | solution.py:697
  (1 shorter events, 0.0 us)
Async XLA Ops:
  2.6 11.8 %collective-permute-start = (f32[68,8,128]{2,1,0:T(8,128)S(1)}, f32[68,8,128]{2,1,0:T(8,128)S(1)}, u32[]{:S(2)}, u32[]{:S(2)}) collective-permute-start(f32[68,8,128]{2,1,0:T(8,128)S(1)} %get-tuple-element.18), channel_id=1, source_target_pairs={{16,0},{0,16},{17,1},{1,17},{18,2},{2,18},{19,3},{3,19},{20,4},{4,... | collective-permute-start | bytes 835592 | tf_op jit(solution)/shard_map/ppermute | solution.py:671
  5.6 7.0 %collective-permute-start.3 = (f32[8,8,128]{2,1,0:T(8,128)S(1)}, f32[8,8,128]{2,1,0:T(8,128)S(1)}, u32[]{:S(2)}, u32[]{:S(2)}) collective-permute-start(f32[8,8,128]{2,1,0:T(8,128)S(1)} %get-tuple-element.20), channel_id=1, source_target_pairs={{0,16},{1,2},{2,1},{3,4},{4,3},{5,6},{6,5},{7,8},{8,7},{9,10},{10,... | collective-permute-start | bytes 98312 | tf_op jit(solution)/shard_map/ppermute | solution.py:676
  5.7 12.4 %all-to-all-start = ((f32[32,2,128]{2,1,0:T(2,128)}), f32[32,2,128]{2,1,0:T(2,128)S(1)}, u32[]{:S(2)}, u32[]{:S(2)}) async-start(f32[32,2,128]{2,1,0:T(2,128)} %get-tuple-element.13), calls=%async_computation | async-start | bytes 65536 | tf_op jit(solution)/shard_map/all_to_all | solution.py:678
  12.6 5.5 %collective-permute-start.4 = (f32[8,8,128]{2,1,0:T(8,128)S(1)}, f32[8,8,128]{2,1,0:T(8,128)S(1)}, u32[]{:S(2)}, u32[]{:S(2)}) collective-permute-start(f32[8,8,128]{2,1,0:T(8,128)S(1)} %collective-permute-done.3.refs_8_), channel_id=1, source_target_pairs={{16,0},{0,16},{17,1},{1,17},{18,2},{2,18},{19,3},{3,19},{20,4},{4,... | collective-permute-start | bytes 98312 | tf_op jit(solution)/shard_map/ppermute | solution.py:671
  14.4 1.2 %collective-permute-start.1 = (f32[7,8,128]{2,1,0:T(8,128)S(1)}, f32[7,8,128]{2,1,0:T(8,128)S(1)}, u32[]{:S(2)}, u32[]{:S(2)}) collective-permute-start(f32[7,8,128]{2,1,0:T(8,128)S(1)} %get-tuple-element.19), channel_id=1, source_target_pairs={{0,1},{1,0},{2,3},{3,2},{4,5},{5,4},{6,7},{7,6},{8,9},{9,8},{10,11... | collective-permute-start | bytes 86024 | tf_op jit(solution)/shard_map/ppermute | solution.py:675
  14.4 3.7 %collective-permute-start.2 = (f32[5,8,128]{2,1,0:T(8,128)S(1)}, f32[5,8,128]{2,1,0:T(8,128)S(1)}, u32[]{:S(2)}, u32[]{:S(2)}) collective-permute-start(f32[5,8,128]{2,1,0:T(8,128)S(1)} %slice.4), channel_id=1, source_target_pairs={{0,1},{1,0},{2,3},{3,2},{4,5},{5,4},{6,7},{7,6},{8,9},{9,8},{10,11... | collective-permute-start | bytes 61448 | tf_op jit(solution)/shard_map/ppermute | solution.py:679

commit v5 on v4

--- a/solution.py
+++ b/solution.py
@@ -273,7 +273,7 @@
     blocks, refs = (None, *refs[: width - 1]), refs[width - 1 :]
     ya_refs, refs = refs[:width], refs[width:]
     yb_refs, refs = refs[:width], refs[width:]
-    residual_hbm, z_out, sums_out, residual_out, sem = refs
+    residual_out, z_out, sums_out = refs
 
     cx, nz, cy = residual_out.shape[1:]
     total = width * cx
@@ -483,8 +483,6 @@
     start = [-(resid[c] + jnp.concatenate(added[c], axis=0)) for c in range(3)]
     for c in range(3):
         residual_out[c] = -start[c][:cx, :, :cy]
-    residual_copy = pltpu.make_async_copy(residual_out, residual_hbm, sem)
-    residual_copy.start()
 
     coefs = [extended(COEF + q) for q in range(6)]
     coefs[0] = seam_before(coefs[0])
@@ -593,14 +591,21 @@
     square = jnp.sum(square, axis=0, keepdims=True)
     pair = jnp.where(iota((2, cy), 0) == 0, along, square)
     sums_out[...] = jnp.broadcast_to(pair[None], sums_out.shape)
-    residual_copy.wait()
-
-
-def after_kernel(sums_ref, z_ref, update_out):
+
+
+def after_kernel(sums_ref, z_ref, residual_ref, update_hbm, residual_hbm, update_out, sem, sems):
+    copy = pltpu.make_async_copy(residual_ref, residual_hbm, sem)
+    copy.start()
     pair = jnp.sum(sums_ref[...], axis=0)
     both = jnp.sum(pair, axis=1, keepdims=True)
     step = both[0:1] / both[1:2]
-    update_out[...] = z_ref[...] * step[None, None]
+    copies = []
+    for c in range(3):
+        update_out[c] = z_ref[c] * step[None]
+        copies.append(pltpu.make_async_copy(update_out.at[c], update_hbm.at[c], sems.at[c]))
+        copies[-1].start()
+    for each in [copy, *copies]:
+        each.wait()
 
 
 def other_pair(device, count_x, count_y):
@@ -682,26 +687,30 @@
     residual, direction, sums = pl.pallas_call(
         functools.partial(main_kernel, count_x, count_y, tuple(offsets)),
         in_specs=[whole] * (4 + 3 * width),
-        out_specs=[anywhere, whole, whole],
+        out_specs=[whole] * 3,
         out_shape=[
-            pltpu.HBM((3, cx, nz, cy), f32),
+            shape((3, cx, nz, cy), f32),
             shape((3, cx, nz, cy), f32),
             shape((devices, 2, cy), f32),
         ],
-        scratch_shapes=[pltpu.VMEM((3, cx, nz, cy), f32), pltpu.SemaphoreType.DMA],
         compiler_params=params,
         name="main",
     )(wells_all, diag, off, dinv, own, *blocks, *ya_all, *yb_all)
 
     sums_all = lax.all_to_all(sums, ("gx", "gy"), 0, 0)
-    update = pl.pallas_call(
+    update, residual = pl.pallas_call(
         after_kernel,
-        in_specs=[whole] * 2,
-        out_specs=whole,
-        out_shape=shape((3, cx, nz, cy), f32),
+        in_specs=[whole] * 3,
+        out_specs=[anywhere] * 2,
+        out_shape=[pltpu.HBM((3, cx, nz, cy), f32)] * 2,
+        scratch_shapes=[
+            pltpu.VMEM((3, cx, nz, cy), f32),
+            pltpu.SemaphoreType.DMA,
+            pltpu.SemaphoreType.DMA((3,)),
+        ],
         compiler_params=params,
         name="after",
-    )(sums_all, direction)
+    )(sums_all, direction, residual)
     return (residual, update)
 
 

time: 30.3 us -> 30 us (0.990)
  Pallas kernels: 4.23 us -> 3.91 us
    pallas_call x1, Pallas kernels: 1.47 us -> 1.12 us  [body(): pl.pallas_call(functools.partial(main_kernel, count_x, count_y, tuple(off...]
where the time goes in v5:
time: 30 us; the launch traced here: 29.8 us
  starting transfers between devices  10.6 us (35%)
  blocking collectives  9.71 us (32%)
  waiting for transfers between devices  4.95 us (16%)
  Pallas kernels  3.91 us (13%)
  between operations  0.67 us (2%)
    all_to_all x1, blocking collectives, body(): sums_all = lax.all_to_all(sums, ('gx', 'gy'), 0, 0)  9.71 us
    all_to_all x1, starting transfers between devices, body(): wells_all = lax.all_to_all(wells_part, ('gx', 'gy'), 0, 0)  5.19 us
    ppermute x2, starting transfers between devices, from_x(): lax.ppermute(values, 'gx', [((i + offset) % count_x, i) for i in range(co...  4.79 us
    all_to_all x1, waiting for transfers between devices, body(): wells_all = lax.all_to_all(wells_part, ('gx', 'gy'), 0, 0)  2.53 us
    pallas_call x1, Pallas kernels, body(): pl.pallas_call(functools.partial(before_kernel, count_x, count_y), in_spe...  1.99 us
    ppermute x1, waiting for transfers between devices, body(): yb_got = lax.ppermute(yb, ('gx', 'gy'), others)  1.74 us
    pallas_call x1, Pallas kernels, body(): pl.pallas_call(functools.partial(main_kernel, count_x, count_y, tuple(off...  1.12 us
    pallas_call x1, Pallas kernels, body(): pl.pallas_call(after_kernel, in_specs=[whole] * 3, out_specs=[anywhere] *...  0.8 us
  transfers between devices with their start and end apart: 6, of which 3 were waited for; matrix products, arithmetic and copies ran while one was open for 0% of the time, Pallas kernels for 0%

profile of v5, /device:TPU:0, one launch (start us, length us, event | category | flops | bytes accessed | tf_op | source)
XLA Modules:
  0.0 29.8 jit_solution(13724169335862914881)
XLA Ops:
  0.6 2.0 %before.1 = (f32[32,2,128]{2,1,0:T(2,128)}, f32[68,8,128]{2,1,0:T(8,128)S(1)}, f32[62,8,128]{2,1,0:T(8,128)S(1)}, f32[7,8,128]{2,1,0:T(8,128)S(1)}, f32[8,8,128]...) custom-call(f32[4,8,128]{2,1,0:T(8,128)} %refs_0_.1, ...), custom_call_target="tpu_custom_call" | custom-call | tf_op jit(solution)/shard_map/before/pallas_call | solution.py:648
  2.6 3.0 %collective-permute-start = (f32[68,8,128]{2,1,0:T(8,128)S(1)}, f32[68,8,128]{2,1,0:T(8,128)S(1)}, u32[]{:S(2)}, u32[]{:S(2)}) collective-permute-start(f32[68,8,128]{2,1,0:T(8,128)S(1)} %get-tuple-element.20), channel_id=1, source_target_pairs={{16,0},{0,16},{17,1},{1,17},{18,2},{2,18},{19,3},{3,19},{20,4},{4,... | collective-permute-start | bytes 835592 | tf_op jit(solution)/shard_map/ppermute | solution.py:676
  5.6 0.1 collective-permute-start.3
  5.7 5.2 %all-to-all-start = ((f32[32,2,128]{2,1,0:T(2,128)}), f32[32,2,128]{2,1,0:T(2,128)S(1)}, u32[]{:S(2)}, u32[]{:S(2)}) async-start(f32[32,2,128]{2,1,0:T(2,128)} %get-tuple-element.15), calls=%async_computation | async-start | bytes 65536 | tf_op jit(solution)/shard_map/all_to_all | solution.py:683
  10.9 1.7 %collective-permute-done.3.refs_8_ = f32[8,8,128]{2,1,0:T(8,128)S(1)} collective-permute-done((f32[8,8,128]{2,1,0:T(8,128)S(1)}, f32[8,8,128]{2,1,0:T(8,128)S(1)}, u32[]{:S(2)}, u32[]{:S(2)}) %collective-permute-start.3) | collective-permute-done | bytes 32800 | tf_op jit(solution)/shard_map/ppermute | solution.py:681
  12.6 1.8 %collective-permute-start.4 = (f32[8,8,128]{2,1,0:T(8,128)S(1)}, f32[8,8,128]{2,1,0:T(8,128)S(1)}, u32[]{:S(2)}, u32[]{:S(2)}) collective-permute-start(f32[8,8,128]{2,1,0:T(8,128)S(1)} %collective-permute-done.3.refs_8_), channel_id=1, source_target_pairs={{16,0},{0,16},{17,1},{1,17},{18,2},{2,18},{19,3},{3,19},{20,4},{4,... | collective-permute-start | bytes 98312 | tf_op jit(solution)/shard_map/ppermute | solution.py:676
  14.4 0.0 collective-permute-start.1
  14.4 0.0 collective-permute-done.refs_5_
  14.4 0.5 %collective-permute-start.2 = (f32[5,8,128]{2,1,0:T(8,128)S(1)}, f32[5,8,128]{2,1,0:T(8,128)S(1)}, u32[]{:S(2)}, u32[]{:S(2)}) collective-permute-start(f32[5,8,128]{2,1,0:T(8,128)S(1)} %slice.4), channel_id=1, source_target_pairs={{0,1},{1,0},{2,3},{3,2},{4,5},{5,4},{6,7},{7,6},{8,9},{9,8},{10,11... | collective-permute-start | bytes 61448 | tf_op jit(solution)/shard_map/ppermute | solution.py:684
  14.9 0.7 %collective-permute-done.1.refs_6_ = f32[7,8,128]{2,1,0:T(8,128)S(1)} collective-permute-done((f32[7,8,128]{2,1,0:T(8,128)S(1)}, f32[7,8,128]{2,1,0:T(8,128)S(1)}, u32[]{:S(2)}, u32[]{:S(2)}) %collective-permute-start.1) | collective-permute-done | bytes 28704 | tf_op jit(solution)/shard_map/ppermute | solution.py:680
  15.6 2.5 %all-to-all-done.refs_0_ = f32[32,2,128]{2,1,0:T(2,128)S(1)} async-done(((f32[32,2,128]{2,1,0:T(2,128)}), f32[32,2,128]{2,1,0:T(2,128)S(1)}, u32[]{:S(2)}, u32[]{:S(2)}) %all-to-all-start) | async-done | bytes 32800 | tf_op jit(solution)/shard_map/all_to_all | solution.py:683
  18.2 0.0 collective-permute-done.4.refs_9_
  18.2 0.0 collective-permute-done.2.refs_7_
  18.2 1.1 %main.1 = (f32[3,4,8,128]{3,2,1,0:T(8,128)S(1)}, f32[3,4,8,128]{3,2,1,0:T(8,128)S(1)}, f32[32,2,128]{2,1,0:T(2,128)S(1)}) custom-call(f32[32,2,128]{2,1,0:T(2,128)S(1)} %all-to-all-done.refs_0_, f32[3,3,4,8,128]{4,3,2,1,0:T(8,128)S(1)} %get-tuple-element.16.refs_1_, f32[6,3,3,4,8,128]{5,4,3,2,1,0:T(8,128)S(1)} %get-tuple-element.17.refs_2_, ...), custom_call_target="tpu_custom_call" | custom-call | tf_op jit(solution)/shard_map/main/pallas_call | solution.py:687
  19.3 9.7 %all_to_all.10.sums_ref = f32[32,2,128]{2,1,0:T(2,128)S(1)} all-to-all(f32[32,2,128]{2,1,0:T(2,128)S(1)} %get-tuple-element.23), channel_id=1, replica_groups=mesh['gx'=2,'gy'=16] {'gx','gy'}, dimensions={0} | all-to-all | bytes 65536 | tf_op jit(solution)/shard_map/all_to_all | solution.py:700
  29.0 0.8 %after.1 = (f32[3,4,8,128]{3,2,1,0:T(8,128)}, f32[3,4,8,128]{3,2,1,0:T(8,128)}) custom-call(f32[32,2,128]{2,1,0:T(2,128)S(1)} %all_to_all.10.sums_ref, f32[3,4,8,128]{3,2,1,0:T(8,128)S(1)} %get-tuple-element.24.z_ref, f32[3,4,8,128]{3,2,1,0:T(8,128)S(1)} %get-tuple-element.25.residual_ref), custom_call_target="tpu_custom_call" | custom-call | tf_op jit(solution)/shard_map/after/pallas_call | solution.py:701
  (1 shorter events, 0.0 us)
Async XLA Ops:
  2.6 11.8 %collective-permute-start = (f32[68,8,128]{2,1,0:T(8,128)S(1)}, f32[68,8,128]{2,1,0:T(8,128)S(1)}, u32[]{:S(2)}, u32[]{:S(2)}) collective-permute-start(f32[68,8,128]{2,1,0:T(8,128)S(1)} %get-tuple-element.20), channel_id=1, source_target_pairs={{16,0},{0,16},{17,1},{1,17},{18,2},{2,18},{19,3},{3,19},{20,4},{4,... | collective-permute-start | bytes 835592 | tf_op jit(solution)/shard_map/ppermute | solution.py:676
  5.6 7.0 %collective-permute-start.3 = (f32[8,8,128]{2,1,0:T(8,128)S(1)}, f32[8,8,128]{2,1,0:T(8,128)S(1)}, u32[]{:S(2)}, u32[]{:S(2)}) collective-permute-start(f32[8,8,128]{2,1,0:T(8,128)S(1)} %get-tuple-element.22), channel_id=1, source_target_pairs={{0,16},{1,2},{2,1},{3,4},{4,3},{5,6},{6,5},{7,8},{8,7},{9,10},{10,... | collective-permute-start | bytes 98312 | tf_op jit(solution)/shard_map/ppermute | solution.py:681
  5.7 12.4 %all-to-all-start = ((f32[32,2,128]{2,1,0:T(2,128)}), f32[32,2,128]{2,1,0:T(2,128)S(1)}, u32[]{:S(2)}, u32[]{:S(2)}) async-start(f32[32,2,128]{2,1,0:T(2,128)} %get-tuple-element.15), calls=%async_computation | async-start | bytes 65536 | tf_op jit(solution)/shard_map/all_to_all | solution.py:683
  12.6 5.5 %collective-permute-start.4 = (f32[8,8,128]{2,1,0:T(8,128)S(1)}, f32[8,8,128]{2,1,0:T(8,128)S(1)}, u32[]{:S(2)}, u32[]{:S(2)}) collective-permute-start(f32[8,8,128]{2,1,0:T(8,128)S(1)} %collective-permute-done.3.refs_8_), channel_id=1, source_target_pairs={{16,0},{0,16},{17,1},{1,17},{18,2},{2,18},{19,3},{3,19},{20,4},{4,... | collective-permute-start | bytes 98312 | tf_op jit(solution)/shard_map/ppermute | solution.py:676
  14.4 1.2 %collective-permute-start.1 = (f32[7,8,128]{2,1,0:T(8,128)S(1)}, f32[7,8,128]{2,1,0:T(8,128)S(1)}, u32[]{:S(2)}, u32[]{:S(2)}) collective-permute-start(f32[7,8,128]{2,1,0:T(8,128)S(1)} %get-tuple-element.21), channel_id=1, source_target_pairs={{0,1},{1,0},{2,3},{3,2},{4,5},{5,4},{6,7},{7,6},{8,9},{9,8},{10,11... | collective-permute-start | bytes 86024 | tf_op jit(solution)/shard_map/ppermute | solution.py:680
  14.4 3.7 %collective-permute-start.2 = (f32[5,8,128]{2,1,0:T(8,128)S(1)}, f32[5,8,128]{2,1,0:T(8,128)S(1)}, u32[]{:S(2)}, u32[]{:S(2)}) collective-permute-start(f32[5,8,128]{2,1,0:T(8,128)S(1)} %slice.4), channel_id=1, source_target_pairs={{0,1},{1,0},{2,3},{3,2},{4,5},{5,4},{6,7},{7,6},{8,9},{9,8},{10,11... | collective-permute-start | bytes 61448 | tf_op jit(solution)/shard_map/ppermute | solution.py:684

commit v6 on v5

--- a/solution.py
+++ b/solution.py
@@ -12,7 +12,6 @@
 
 viscosity = (1.0, 2.0, 0.2)
 vertical_ratio = 0.1
-highest = lax.Precision.HIGHEST
 f32 = jnp.float32
 
 PRESS, MOB, PERM, PART, INV, COEF = 0, 1, 4, 5, 8, 9
@@ -89,7 +88,7 @@
     cell_ref, well_ref, index_ref, rate_ref, wells_out, sems = refs[24:]
     targets = (*refs[19:24], diag_ref, off_ref, *refs[24:28])
     copies = []
-    for i in (7, 8, 9, 10, 0, 1, 4, 2, 3, 5, 6):
+    for i in (1, 0, 7, 9, 8, 10, 4, 2, 3, 5, 6):
         copies.append(pltpu.make_async_copy(sources[i], targets[i], sems.at[i]))
         copies[-1].start()
     for copy in copies[:6]:
@@ -119,11 +118,10 @@
     parts = [index_vals * at_perf[i] for i in range(3)]
     strength = index_vals * (at_perf[0] + at_perf[1] + at_perf[2])
     weighted = strength * at_perf[3]
-    row = iota((8, perfs), 0)
+    row = iota((16, perfs), 0)
     both = jnp.where(row == 0, strength, jnp.where(row == 1, weighted, 0.0))
     wells = wells_out.shape[2]
-    member = jnp.where(iota((wells, perfs), 0) == well_ref[...], 1.0, 0.0)
-    sums = lax.dot_general(both, member, NT, precision=highest, preferred_element_type=f32)
+    sums = split_dot(both, hot_of(iota((wells, perfs), 0) == well_ref[...]), NT)
     owned = rate_ref.shape[1]
     square = jnp.broadcast_to(rate_ref[...], (owned, owned))
     column = jnp.sum(
@@ -180,89 +178,104 @@
             flow = jnp.where(inside, flows[c], 0.0)
             part[c] = part[c] + flow - pltpu.roll(flow, 1, axis)
 
-    for copy in copies[9:]:
-        copy.wait()
-    columns = [[off_ref[q, c, 0] for c in range(3)] for q in range(6)]
-    columns[4] = [jnp.where(layer_at > 0, v, 0.0) for v in columns[4]]
-    columns[5] = [jnp.where(layer_at < nz - 1, v, 0.0) for v in columns[5]]
-    diag = [[diag_ref[a, b] for b in range(3)] for a in range(3)]
-    inverse = 1.0 / (diag[0][0] + diag[1][0] + diag[2][0])
-    coefs = [(columns[q][0] + columns[q][1] + columns[q][2]) * inverse for q in range(6)]
-    bulk = [press, *mobile, perm, *part, inverse, *coefs]
-
-    def cofactor(a, b):
-        return (
-            diag[(a + 1) % 3][(b + 1) % 3] * diag[(a + 2) % 3][(b + 2) % 3]
-            - diag[(a + 1) % 3][(b + 2) % 3] * diag[(a + 2) % 3][(b + 1) % 3]
-        )
-
-    cofactors = [[cofactor(a, b) for b in range(3)] for a in range(3)]
-    over = 1.0 / (
-        diag[0][0] * cofactors[0][0] + diag[0][1] * cofactors[0][1] + diag[0][2] * cofactors[0][2]
-    )
-    solve = [cofactors[b][a] * over for a in range(3) for b in range(3)]
-    for i in range(9):
-        dinv_out[i] = solve[i]
-    edge = solve + [diag[c][0] for c in range(3)] + [columns[q][c] for q in range(6) for c in range(3)]
-
-    for f in range(BULK):
-        own_out[f * cx : (f + 1) * cx] = bulk[f]
-    inner = [*coefs, inverse, part[0] + part[1] + part[2]]
-    for i in range(INNER):
-        for x in range(cx - layers):
-            at = i * (cx - layers) + x
-            if layers == 1:
-                block_out[at] = jnp.where(at_x == 0, inner[i][x], inner[i][x + 1])
-            else:
-                block_out[at] = inner[i][x + 1]
-    for e, values in enumerate([*edge, *part, press, perm, water, gas]):
+    lane = iota((nz, cy), 1)
+    to_left = [jnp.zeros((nz, cy), f32) for _ in range(cx)]
+    to_right = [jnp.zeros((nz, cy), f32) for _ in range(cx)]
+    beside = [jnp.zeros((nz, cy), f32) for _ in range(0, SEAM, cy // (2 * cx))]
+
+    def put_bulk(f, values):
+        own_out[f * cx : (f + 1) * cx] = values
+        shift = f * WIDE
+        on_left = (lane >= shift) & (lane < shift + WIDE)
+        start = (shift - WIDE) % cy
+        on_right = (lane >= start) & (lane < start + WIDE)
+        for x in range(cx):
+            turned = pltpu.roll(values[x], shift, 1) if shift else values[x]
+            to_left[x] = jnp.where(on_left, turned, to_left[x])
+            to_right[x] = jnp.where(on_right, turned, to_right[x])
+
+    def put_edge(e, values):
         if layers == 1:
             block_out[edge_at + e] = jnp.where(at_x == 0, values[cx - 1], values[0])
         else:
             block_out[edge_at + e] = values[0]
             block_out[edge_at + EDGE + e] = values[cx - 1]
-
-    lane = iota((nz, cy), 1)
+        if e < SEAM:
+            group, place = divmod(e, cy // (2 * cx))
+            for x in range(cx):
+                at = 2 * (place * cx + x) + 1
+                here = (lane == at - 1) | (lane == at)
+                beside[group] = jnp.where(here, pltpu.roll(values[x], at, 1), beside[group])
+
+    def put_inner(i, values):
+        for x in range(cx - layers):
+            at = i * (cx - layers) + x
+            if layers == 1:
+                block_out[at] = jnp.where(at_x == 0, values[x], values[x + 1])
+            else:
+                block_out[at] = values[x + 1]
+
     border = jnp.zeros((nz, cy), f32)
     for f in range(FACE):
         for x in range(cx):
             at = BORDER_AT + 2 * (f * cx + x) + 1
-            first = pltpu.roll(bulk[f][x], at - 1, 1)
-            second = pltpu.roll(bulk[f][x], at + 1, 1)
+            first = pltpu.roll(cells_here[f][x], at - 1, 1)
+            second = pltpu.roll(cells_here[f][x], at + 1, 1)
             border = jnp.where(lane == at - 1, first, jnp.where(lane == at, second, border))
     block_out[border_at] = border
     own_out[BULK * cx + 1] = border
-
-    to_left = [jnp.zeros((nz, cy), f32) for _ in range(cx)]
-    to_right = [jnp.zeros((nz, cy), f32) for _ in range(cx)]
     to_left[0] = to_right[0] = border
-    for f in range(BULK):
-        shift = f * WIDE
-        on_left = (lane >= shift) & (lane < shift + WIDE)
-        start = (shift - WIDE) % cy
-        on_right = (lane >= start) & (lane < start + WIDE)
-        for x in range(cx):
-            turned = pltpu.roll(bulk[f][x], shift, 1) if shift else bulk[f][x]
-            to_left[x] = jnp.where(on_left, turned, to_left[x])
-            to_right[x] = jnp.where(on_right, turned, to_right[x])
-    for group in range(0, SEAM, cy // (2 * cx)):
-        left, right = jnp.zeros((nz, cy), f32), jnp.zeros((nz, cy), f32)
-        for e in range(group, min(group + cy // (2 * cx), SEAM)):
-            for x in range(cx):
-                at = 2 * ((e - group) * cx + x) + 1
-                turned = pltpu.roll(edge[e][x], at, 1)
-                left = jnp.where(lane == at, turned, left)
-                right = jnp.where(lane == at - 1, turned, right)
-        to_left.append(left)
-        to_right.append(right)
+    for f, values in enumerate([*cells_here, *part]):
+        put_bulk(f, values)
+    for e, values in enumerate([*part, press, perm, water, gas]):
+        put_edge(EPART + e, values)
+    put_inner(SUM, part[0] + part[1] + part[2])
+
+    copies[9].wait()
+    diag = [[diag_ref[a, b] for b in range(3)] for a in range(3)]
+    inverse = 1.0 / (diag[0][0] + diag[1][0] + diag[2][0])
+    put_bulk(INV, inverse)
+    put_inner(6, inverse)
+
+    def cofactor(a, b):
+        return (
+            diag[(a + 1) % 3][(b + 1) % 3] * diag[(a + 2) % 3][(b + 2) % 3]
+            - diag[(a + 1) % 3][(b + 2) % 3] * diag[(a + 2) % 3][(b + 1) % 3]
+        )
+
+    cofactors = [[cofactor(a, b) for b in range(3)] for a in range(3)]
+    over = 1.0 / (
+        diag[0][0] * cofactors[0][0] + diag[0][1] * cofactors[0][1] + diag[0][2] * cofactors[0][2]
+    )
+    for a in range(3):
+        put_edge(DCOL + a, diag[a][0])
+        for b in range(3):
+            solve = cofactors[b][a] * over
+            dinv_out[3 * a + b] = solve
+            put_edge(DINV + 3 * a + b, solve)
+
+    copies[10].wait()
+    for q in range(6):
+        columns = [off_ref[q, c, 0] for c in range(3)]
+        if q == 4:
+            columns = [jnp.where(layer_at > 0, v, 0.0) for v in columns]
+        if q == 5:
+            columns = [jnp.where(layer_at < nz - 1, v, 0.0) for v in columns]
+        coef = (columns[0] + columns[1] + columns[2]) * inverse
+        put_bulk(COEF + q, coef)
+        put_inner(q, coef)
+        for c in range(3):
+            put_edge(OFFC + 3 * q + c, columns[c])
+
     even = lax.rem(at_y, 2) == 0
     for x in range(cx):
-        block_out[columns_at + x] = jnp.where(even, to_right[x], to_left[x])
-    for t, (left, right) in enumerate(zip(to_left, to_right)):
-        at = t if t < cx else t + 1
-        ya_out[at] = jnp.where(even, right, left)
-        yb_out[at] = jnp.where(even, left, right)
-    for spare in range(len(to_left) + 1, yb_out.shape[0]):
+        ya_out[x] = jnp.where(even, to_right[x], to_left[x])
+        yb_out[x] = jnp.where(even, to_left[x], to_right[x])
+        block_out[columns_at + x] = ya_out[x]
+    for t, values in enumerate(beside):
+        ya_out[cx + 1 + t] = values
+        yb_out[cx + 1 + t] = values
+    for spare in range(cx + 1 + len(beside), yb_out.shape[0]):
         yb_out[spare] = jnp.zeros((nz, cy), f32)
     wells_copy.wait()
 
@@ -297,12 +310,22 @@
         from_left.append(jnp.where(even, second, first) * has_left)
     lane = iota((nz, cy), 1)
 
-    def halo(tiles_l, tiles_r, x, shift, wide):
-        back = (cy - shift) % cy
-        left, right = tiles_l[x], tiles_r[x]
-        if back:
-            left, right = pltpu.roll(left, back, 1), pltpu.roll(right, back, 1)
-        return jnp.where(lane < wide, right, jnp.where(lane >= cy - wide, left, 0.0))
+    merged = []
+    for parity in range(2):
+        of_right = lane < 0
+        for f in range(parity, BULK, 2):
+            of_right = of_right | ((lane >= f * WIDE) & (lane < (f + 1) * WIDE))
+        merged.append(
+            [
+                jnp.where(of_right, from_right[j][x], from_left[j][x])
+                for j in range(width)
+                for x in range(cx)
+            ]
+        )
+
+    def halo(f, x):
+        tile = merged[f % 2][x]
+        return pltpu.roll(tile, cy - f * WIDE, 1) if f else tile
 
     def arranged(edges, inner):
         if layers == 2:
@@ -345,13 +368,7 @@
         own = jnp.concatenate(
             [own_ref[f * cx : (f + 1) * cx], *[other[f] for other in others]], axis=0
         )
-        side = jnp.stack(
-            [
-                halo(from_left[j], from_right[j], x, f * WIDE, WIDE)
-                for j in range(width)
-                for x in range(cx)
-            ]
-        )
+        side = jnp.stack([halo(f, x) for x in range(total)])
         return jnp.concatenate([own, side], axis=2)
 
     lanes = 2 * cy
@@ -394,8 +411,7 @@
 
     def side_of(f, x):
         if (f, x) not in sides:
-            j = x // cx
-            sides[f, x] = halo(from_left[j], from_right[j], x % cx, f * WIDE, WIDE)
+            sides[f, x] = halo(f, x)
         return sides[f, x]
 
     even_lane = lane % 2 == 0

time: 30 us -> 29.8 us (level)
  no operation moved by 1% of the time
where the time goes in v6:
time: 29.8 us; the launch traced here: 29.6 us
  starting transfers between devices  10.6 us (36%)
  blocking collectives  9.7 us (33%)
  waiting for transfers between devices  4.95 us (17%)
  Pallas kernels  3.76 us (13%)
  between operations  0.67 us (2%)
    all_to_all x1, blocking collectives, body(): sums_all = lax.all_to_all(sums, ('gx', 'gy'), 0, 0)  9.7 us
    all_to_all x1, starting transfers between devices, body(): wells_all = lax.all_to_all(wells_part, ('gx', 'gy'), 0, 0)  5.19 us
    ppermute x2, starting transfers between devices, from_x(): lax.ppermute(values, 'gx', [((i + offset) % count_x, i) for i in range(co...  4.79 us
    all_to_all x1, waiting for transfers between devices, body(): wells_all = lax.all_to_all(wells_part, ('gx', 'gy'), 0, 0)  2.53 us
    pallas_call x1, Pallas kernels, body(): pl.pallas_call(functools.partial(before_kernel, count_x, count_y), in_spe...  1.83 us
    ppermute x1, waiting for transfers between devices, body(): yb_got = lax.ppermute(yb, ('gx', 'gy'), others)  1.73 us
    pallas_call x1, Pallas kernels, body(): pl.pallas_call(functools.partial(main_kernel, count_x, count_y, tuple(off...  1.13 us
    pallas_call x1, Pallas kernels, body(): pl.pallas_call(after_kernel, in_specs=[whole] * 3, out_specs=[anywhere] *...  0.8 us
  transfers between devices with their start and end apart: 6, of which 3 were waited for; matrix products, arithmetic and copies ran while one was open for 0% of the time, Pallas kernels for 0%

profile of v6, /device:TPU:0, one launch (start us, length us, event | category | flops | bytes accessed | tf_op | source)
XLA Modules:
  0.0 29.6 jit_solution(11063392819170286814)
XLA Ops:
  0.6 1.8 %before.1 = (f32[32,2,128]{2,1,0:T(2,128)}, f32[68,8,128]{2,1,0:T(8,128)S(1)}, f32[62,8,128]{2,1,0:T(8,128)S(1)}, f32[7,8,128]{2,1,0:T(8,128)S(1)}, f32[8,8,128]...) custom-call(f32[4,8,128]{2,1,0:T(8,128)} %refs_0_.1, ...), custom_call_target="tpu_custom_call" | custom-call | tf_op jit(solution)/shard_map/before/pallas_call | solution.py:664
  2.5 3.0 %collective-permute-start = (f32[68,8,128]{2,1,0:T(8,128)S(1)}, f32[68,8,128]{2,1,0:T(8,128)S(1)}, u32[]{:S(2)}, u32[]{:S(2)}) collective-permute-start(f32[68,8,128]{2,1,0:T(8,128)S(1)} %get-tuple-element.20), channel_id=1, source_target_pairs={{16,0},{0,16},{17,1},{1,17},{18,2},{2,18},{19,3},{3,19},{20,4},{4,... | collective-permute-start | bytes 835592 | tf_op jit(solution)/shard_map/ppermute | solution.py:692
  5.5 0.1 collective-permute-start.3
  5.6 5.2 %all-to-all-start = ((f32[32,2,128]{2,1,0:T(2,128)}), f32[32,2,128]{2,1,0:T(2,128)S(1)}, u32[]{:S(2)}, u32[]{:S(2)}) async-start(f32[32,2,128]{2,1,0:T(2,128)} %get-tuple-element.15), calls=%async_computation | async-start | bytes 65536 | tf_op jit(solution)/shard_map/all_to_all | solution.py:699
  10.7 1.7 %collective-permute-done.3.refs_8_ = f32[8,8,128]{2,1,0:T(8,128)S(1)} collective-permute-done((f32[8,8,128]{2,1,0:T(8,128)S(1)}, f32[8,8,128]{2,1,0:T(8,128)S(1)}, u32[]{:S(2)}, u32[]{:S(2)}) %collective-permute-start.3) | collective-permute-done | bytes 32800 | tf_op jit(solution)/shard_map/ppermute | solution.py:697
  12.5 1.8 %collective-permute-start.4 = (f32[8,8,128]{2,1,0:T(8,128)S(1)}, f32[8,8,128]{2,1,0:T(8,128)S(1)}, u32[]{:S(2)}, u32[]{:S(2)}) collective-permute-start(f32[8,8,128]{2,1,0:T(8,128)S(1)} %collective-permute-done.3.refs_8_), channel_id=1, source_target_pairs={{16,0},{0,16},{17,1},{1,17},{18,2},{2,18},{19,3},{3,19},{20,4},{4,... | collective-permute-start | bytes 98312 | tf_op jit(solution)/shard_map/ppermute | solution.py:692
  14.3 0.0 collective-permute-start.1
  14.3 0.0 collective-permute-done.refs_5_
  14.3 0.5 %collective-permute-start.2 = (f32[5,8,128]{2,1,0:T(8,128)S(1)}, f32[5,8,128]{2,1,0:T(8,128)S(1)}, u32[]{:S(2)}, u32[]{:S(2)}) collective-permute-start(f32[5,8,128]{2,1,0:T(8,128)S(1)} %slice.4), channel_id=1, source_target_pairs={{0,1},{1,0},{2,3},{3,2},{4,5},{5,4},{6,7},{7,6},{8,9},{9,8},{10,11... | collective-permute-start | bytes 61448 | tf_op jit(solution)/shard_map/ppermute | solution.py:700
  14.8 0.7 %collective-permute-done.1.refs_6_ = f32[7,8,128]{2,1,0:T(8,128)S(1)} collective-permute-done((f32[7,8,128]{2,1,0:T(8,128)S(1)}, f32[7,8,128]{2,1,0:T(8,128)S(1)}, u32[]{:S(2)}, u32[]{:S(2)}) %collective-permute-start.1) | collective-permute-done | bytes 28704 | tf_op jit(solution)/shard_map/ppermute | solution.py:696
  15.5 2.5 %all-to-all-done.refs_0_ = f32[32,2,128]{2,1,0:T(2,128)S(1)} async-done(((f32[32,2,128]{2,1,0:T(2,128)}), f32[32,2,128]{2,1,0:T(2,128)S(1)}, u32[]{:S(2)}, u32[]{:S(2)}) %all-to-all-start) | async-done | bytes 32800 | tf_op jit(solution)/shard_map/all_to_all | solution.py:699
  18.0 0.0 collective-permute-done.4.refs_9_
  18.0 0.0 collective-permute-done.2.refs_7_
  18.0 1.1 %main.1 = (f32[3,4,8,128]{3,2,1,0:T(8,128)S(1)}, f32[3,4,8,128]{3,2,1,0:T(8,128)S(1)}, f32[32,2,128]{2,1,0:T(2,128)S(1)}) custom-call(f32[32,2,128]{2,1,0:T(2,128)S(1)} %all-to-all-done.refs_0_, f32[3,3,4,8,128]{4,3,2,1,0:T(8,128)S(1)} %get-tuple-element.16.refs_1_, f32[6,3,3,4,8,128]{5,4,3,2,1,0:T(8,128)S(1)} %get-tuple-element.17.refs_2_, ...), custom_call_target="tpu_custom_call" | custom-call | tf_op jit(solution)/shard_map/main/pallas_call | solution.py:703
  19.1 9.7 %all_to_all.10.sums_ref = f32[32,2,128]{2,1,0:T(2,128)S(1)} all-to-all(f32[32,2,128]{2,1,0:T(2,128)S(1)} %get-tuple-element.23), channel_id=1, replica_groups=mesh['gx'=2,'gy'=16] {'gx','gy'}, dimensions={0} | all-to-all | bytes 65536 | tf_op jit(solution)/shard_map/all_to_all | solution.py:716
  28.8 0.8 %after.1 = (f32[3,4,8,128]{3,2,1,0:T(8,128)}, f32[3,4,8,128]{3,2,1,0:T(8,128)}) custom-call(f32[32,2,128]{2,1,0:T(2,128)S(1)} %all_to_all.10.sums_ref, f32[3,4,8,128]{3,2,1,0:T(8,128)S(1)} %get-tuple-element.24.z_ref, f32[3,4,8,128]{3,2,1,0:T(8,128)S(1)} %get-tuple-element.25.residual_ref), custom_call_target="tpu_custom_call" | custom-call | tf_op jit(solution)/shard_map/after/pallas_call | solution.py:717
  (1 shorter events, 0.0 us)
Async XLA Ops:
  2.5 11.8 %collective-permute-start = (f32[68,8,128]{2,1,0:T(8,128)S(1)}, f32[68,8,128]{2,1,0:T(8,128)S(1)}, u32[]{:S(2)}, u32[]{:S(2)}) collective-permute-start(f32[68,8,128]{2,1,0:T(8,128)S(1)} %get-tuple-element.20), channel_id=1, source_target_pairs={{16,0},{0,16},{17,1},{1,17},{18,2},{2,18},{19,3},{3,19},{20,4},{4,... | collective-permute-start | bytes 835592 | tf_op jit(solution)/shard_map/ppermute | solution.py:692
  5.5 7.0 %collective-permute-start.3 = (f32[8,8,128]{2,1,0:T(8,128)S(1)}, f32[8,8,128]{2,1,0:T(8,128)S(1)}, u32[]{:S(2)}, u32[]{:S(2)}) collective-permute-start(f32[8,8,128]{2,1,0:T(8,128)S(1)} %get-tuple-element.22), channel_id=1, source_target_pairs={{0,16},{1,2},{2,1},{3,4},{4,3},{5,6},{6,5},{7,8},{8,7},{9,10},{10,... | collective-permute-start | bytes 98312 | tf_op jit(solution)/shard_map/ppermute | solution.py:697
  5.6 12.4 %all-to-all-start = ((f32[32,2,128]{2,1,0:T(2,128)}), f32[32,2,128]{2,1,0:T(2,128)S(1)}, u32[]{:S(2)}, u32[]{:S(2)}) async-start(f32[32,2,128]{2,1,0:T(2,128)} %get-tuple-element.15), calls=%async_computation | async-start | bytes 65536 | tf_op jit(solution)/shard_map/all_to_all | solution.py:699
  12.5 5.5 %collective-permute-start.4 = (f32[8,8,128]{2,1,0:T(8,128)S(1)}, f32[8,8,128]{2,1,0:T(8,128)S(1)}, u32[]{:S(2)}, u32[]{:S(2)}) collective-permute-start(f32[8,8,128]{2,1,0:T(8,128)S(1)} %collective-permute-done.3.refs_8_), channel_id=1, source_target_pairs={{16,0},{0,16},{17,1},{1,17},{18,2},{2,18},{19,3},{3,19},{20,4},{4,... | collective-permute-start | bytes 98312 | tf_op jit(solution)/shard_map/ppermute | solution.py:692
  14.3 1.2 %collective-permute-start.1 = (f32[7,8,128]{2,1,0:T(8,128)S(1)}, f32[7,8,128]{2,1,0:T(8,128)S(1)}, u32[]{:S(2)}, u32[]{:S(2)}) collective-permute-start(f32[7,8,128]{2,1,0:T(8,128)S(1)} %get-tuple-element.21), channel_id=1, source_target_pairs={{0,1},{1,0},{2,3},{3,2},{4,5},{5,4},{6,7},{7,6},{8,9},{9,8},{10,11... | collective-permute-start | bytes 86024 | tf_op jit(solution)/shard_map/ppermute | solution.py:696
  14.3 3.7 %collective-permute-start.2 = (f32[5,8,128]{2,1,0:T(8,128)S(1)}, f32[5,8,128]{2,1,0:T(8,128)S(1)}, u32[]{:S(2)}, u32[]{:S(2)}) collective-permute-start(f32[5,8,128]{2,1,0:T(8,128)S(1)} %slice.4), channel_id=1, source_target_pairs={{0,1},{1,0},{2,3},{3,2},{4,5},{5,4},{6,7},{7,6},{8,9},{9,8},{10,11... | collective-permute-start | bytes 61448 | tf_op jit(solution)/shard_map/ppermute | solution.py:700

commit v7 on v6

--- a/solution.py
+++ b/solution.py
@@ -507,10 +507,10 @@
     steps = (last_x, next_x, last_y, next_y, last_z, next_z)
     part = scaled
     for _ in range(1, SWEEPS):
-        gathered = coefs[0] * steps[0](part)
-        for q in range(1, 6):
-            gathered = gathered + coefs[q] * steps[q](part)
-        part = scaled - gathered
+        along_x, along_y, along_z = (
+            coefs[q] * steps[q](part) + coefs[q + 1] * steps[q + 1](part) for q in (0, 2, 4)
+        )
+        part = (scaled - along_x) - (along_z + along_y)
 
     near = [step(part) for step in steps]
     near[0] = seam_before(near[0])
@@ -544,7 +544,7 @@
     beside = []
     for t in range(cx + 1, cx + 1 - (-SEAM * 2 * cx // cy)):
         one, two = ya_refs[0][t], yb_refs[0][t]
-        left, right = jnp.where(even, two, one), jnp.where(even, one, two)
+        left, right = jnp.where(even, two, one) * has_left, jnp.where(even, one, two) * has_right
         beside.append(jnp.where(even_lane, left, right))
 
     def edge_side(e):

time: 29.8 us -> 29.8 us (level)
  no operation moved by 1% of the time
where the time goes in v7:
time: 29.8 us; the launch traced here: 29.7 us
  starting transfers between devices  10.6 us (36%)
  blocking collectives  9.71 us (33%)
  waiting for transfers between devices  4.95 us (17%)
  Pallas kernels  3.77 us (13%)
  between operations  0.67 us (2%)
    all_to_all x1, blocking collectives, body(): sums_all = lax.all_to_all(sums, ('gx', 'gy'), 0, 0)  9.71 us
    all_to_all x1, starting transfers between devices, body(): wells_all = lax.all_to_all(wells_part, ('gx', 'gy'), 0, 0)  5.19 us
    ppermute x2, starting transfers between devices, from_x(): lax.ppermute(values, 'gx', [((i + offset) % count_x, i) for i in range(co...  4.79 us
    all_to_all x1, waiting for transfers between devices, body(): wells_all = lax.all_to_all(wells_part, ('gx', 'gy'), 0, 0)  2.53 us
    pallas_call x1, Pallas kernels, body(): pl.pallas_call(functools.partial(before_kernel, count_x, count_y), in_spe...  1.83 us
    ppermute x1, waiting for transfers between devices, body(): yb_got = lax.ppermute(yb, ('gx', 'gy'), others)  1.73 us
    pallas_call x1, Pallas kernels, body(): pl.pallas_call(functools.partial(main_kernel, count_x, count_y, tuple(off...  1.13 us
    pallas_call x1, Pallas kernels, body(): pl.pallas_call(after_kernel, in_specs=[whole] * 3, out_specs=[anywhere] *...  0.8 us
  transfers between devices with their start and end apart: 6, of which 3 were waited for; matrix products, arithmetic and copies ran while one was open for 0% of the time, Pallas kernels for 0%

profile of v7, /device:TPU:0, one launch (start us, length us, event | category | flops | bytes accessed | tf_op | source)
XLA Modules:
  0.0 29.7 jit_solution(4071694884417832472)
XLA Ops:
  0.6 1.8 %before.1 = (f32[32,2,128]{2,1,0:T(2,128)}, f32[68,8,128]{2,1,0:T(8,128)S(1)}, f32[62,8,128]{2,1,0:T(8,128)S(1)}, f32[7,8,128]{2,1,0:T(8,128)S(1)}, f32[8,8,128]...) custom-call(f32[4,8,128]{2,1,0:T(8,128)} %refs_0_.1, ...), custom_call_target="tpu_custom_call" | custom-call | tf_op jit(solution)/shard_map/before/pallas_call | solution.py:664
  2.5 3.0 %collective-permute-start = (f32[68,8,128]{2,1,0:T(8,128)S(1)}, f32[68,8,128]{2,1,0:T(8,128)S(1)}, u32[]{:S(2)}, u32[]{:S(2)}) collective-permute-start(f32[68,8,128]{2,1,0:T(8,128)S(1)} %get-tuple-element.20), channel_id=1, source_target_pairs={{16,0},{0,16},{17,1},{1,17},{18,2},{2,18},{19,3},{3,19},{20,4},{4,... | collective-permute-start | bytes 835592 | tf_op jit(solution)/shard_map/ppermute | solution.py:692
  5.5 0.1 collective-permute-start.3
  5.6 5.2 %all-to-all-start = ((f32[32,2,128]{2,1,0:T(2,128)}), f32[32,2,128]{2,1,0:T(2,128)S(1)}, u32[]{:S(2)}, u32[]{:S(2)}) async-start(f32[32,2,128]{2,1,0:T(2,128)} %get-tuple-element.15), calls=%async_computation | async-start | bytes 65536 | tf_op jit(solution)/shard_map/all_to_all | solution.py:699
  10.7 1.7 %collective-permute-done.3.refs_8_ = f32[8,8,128]{2,1,0:T(8,128)S(1)} collective-permute-done((f32[8,8,128]{2,1,0:T(8,128)S(1)}, f32[8,8,128]{2,1,0:T(8,128)S(1)}, u32[]{:S(2)}, u32[]{:S(2)}) %collective-permute-start.3) | collective-permute-done | bytes 32800 | tf_op jit(solution)/shard_map/ppermute | solution.py:697
  12.5 1.8 %collective-permute-start.4 = (f32[8,8,128]{2,1,0:T(8,128)S(1)}, f32[8,8,128]{2,1,0:T(8,128)S(1)}, u32[]{:S(2)}, u32[]{:S(2)}) collective-permute-start(f32[8,8,128]{2,1,0:T(8,128)S(1)} %collective-permute-done.3.refs_8_), channel_id=1, source_target_pairs={{16,0},{0,16},{17,1},{1,17},{18,2},{2,18},{19,3},{3,19},{20,4},{4,... | collective-permute-start | bytes 98312 | tf_op jit(solution)/shard_map/ppermute | solution.py:692
  14.3 0.0 collective-permute-start.1
  14.3 0.0 collective-permute-done.refs_5_
  14.3 0.5 %collective-permute-start.2 = (f32[5,8,128]{2,1,0:T(8,128)S(1)}, f32[5,8,128]{2,1,0:T(8,128)S(1)}, u32[]{:S(2)}, u32[]{:S(2)}) collective-permute-start(f32[5,8,128]{2,1,0:T(8,128)S(1)} %slice.4), channel_id=1, source_target_pairs={{0,1},{1,0},{2,3},{3,2},{4,5},{5,4},{6,7},{7,6},{8,9},{9,8},{10,11... | collective-permute-start | bytes 61448 | tf_op jit(solution)/shard_map/ppermute | solution.py:700
  14.8 0.7 %collective-permute-done.1.refs_6_ = f32[7,8,128]{2,1,0:T(8,128)S(1)} collective-permute-done((f32[7,8,128]{2,1,0:T(8,128)S(1)}, f32[7,8,128]{2,1,0:T(8,128)S(1)}, u32[]{:S(2)}, u32[]{:S(2)}) %collective-permute-start.1) | collective-permute-done | bytes 28704 | tf_op jit(solution)/shard_map/ppermute | solution.py:696
  15.5 2.5 %all-to-all-done.refs_0_ = f32[32,2,128]{2,1,0:T(2,128)S(1)} async-done(((f32[32,2,128]{2,1,0:T(2,128)}), f32[32,2,128]{2,1,0:T(2,128)S(1)}, u32[]{:S(2)}, u32[]{:S(2)}) %all-to-all-start) | async-done | bytes 32800 | tf_op jit(solution)/shard_map/all_to_all | solution.py:699
  18.0 0.0 collective-permute-done.4.refs_9_
  18.0 0.0 collective-permute-done.2.refs_7_
  18.0 1.1 %main.1 = (f32[3,4,8,128]{3,2,1,0:T(8,128)S(1)}, f32[3,4,8,128]{3,2,1,0:T(8,128)S(1)}, f32[32,2,128]{2,1,0:T(2,128)S(1)}) custom-call(f32[32,2,128]{2,1,0:T(2,128)S(1)} %all-to-all-done.refs_0_, f32[3,3,4,8,128]{4,3,2,1,0:T(8,128)S(1)} %get-tuple-element.16.refs_1_, f32[6,3,3,4,8,128]{5,4,3,2,1,0:T(8,128)S(1)} %get-tuple-element.17.refs_2_, ...), custom_call_target="tpu_custom_call" | custom-call | tf_op jit(solution)/shard_map/main/pallas_call | solution.py:703
  19.1 9.7 %all_to_all.10.sums_ref = f32[32,2,128]{2,1,0:T(2,128)S(1)} all-to-all(f32[32,2,128]{2,1,0:T(2,128)S(1)} %get-tuple-element.23), channel_id=1, replica_groups=mesh['gx'=2,'gy'=16] {'gx','gy'}, dimensions={0} | all-to-all | bytes 65536 | tf_op jit(solution)/shard_map/all_to_all | solution.py:716
  28.9 0.8 %after.1 = (f32[3,4,8,128]{3,2,1,0:T(8,128)}, f32[3,4,8,128]{3,2,1,0:T(8,128)}) custom-call(f32[32,2,128]{2,1,0:T(2,128)S(1)} %all_to_all.10.sums_ref, f32[3,4,8,128]{3,2,1,0:T(8,128)S(1)} %get-tuple-element.24.z_ref, f32[3,4,8,128]{3,2,1,0:T(8,128)S(1)} %get-tuple-element.25.residual_ref), custom_call_target="tpu_custom_call" | custom-call | tf_op jit(solution)/shard_map/after/pallas_call | solution.py:717
  (1 shorter events, 0.0 us)
Async XLA Ops:
  2.5 11.8 %collective-permute-start = (f32[68,8,128]{2,1,0:T(8,128)S(1)}, f32[68,8,128]{2,1,0:T(8,128)S(1)}, u32[]{:S(2)}, u32[]{:S(2)}) collective-permute-start(f32[68,8,128]{2,1,0:T(8,128)S(1)} %get-tuple-element.20), channel_id=1, source_target_pairs={{16,0},{0,16},{17,1},{1,17},{18,2},{2,18},{19,3},{3,19},{20,4},{4,... | collective-permute-start | bytes 835592 | tf_op jit(solution)/shard_map/ppermute | solution.py:692
  5.5 7.0 %collective-permute-start.3 = (f32[8,8,128]{2,1,0:T(8,128)S(1)}, f32[8,8,128]{2,1,0:T(8,128)S(1)}, u32[]{:S(2)}, u32[]{:S(2)}) collective-permute-start(f32[8,8,128]{2,1,0:T(8,128)S(1)} %get-tuple-element.22), channel_id=1, source_target_pairs={{0,16},{1,2},{2,1},{3,4},{4,3},{5,6},{6,5},{7,8},{8,7},{9,10},{10,... | collective-permute-start | bytes 98312 | tf_op jit(solution)/shard_map/ppermute | solution.py:697
  5.6 12.4 %all-to-all-start = ((f32[32,2,128]{2,1,0:T(2,128)}), f32[32,2,128]{2,1,0:T(2,128)S(1)}, u32[]{:S(2)}, u32[]{:S(2)}) async-start(f32[32,2,128]{2,1,0:T(2,128)} %get-tuple-element.15), calls=%async_computation | async-start | bytes 65536 | tf_op jit(solution)/shard_map/all_to_all | solution.py:699
  12.5 5.5 %collective-permute-start.4 = (f32[8,8,128]{2,1,0:T(8,128)S(1)}, f32[8,8,128]{2,1,0:T(8,128)S(1)}, u32[]{:S(2)}, u32[]{:S(2)}) collective-permute-start(f32[8,8,128]{2,1,0:T(8,128)S(1)} %collective-permute-done.3.refs_8_), channel_id=1, source_target_pairs={{16,0},{0,16},{17,1},{1,17},{18,2},{2,18},{19,3},{3,19},{20,4},{4,... | collective-permute-start | bytes 98312 | tf_op jit(solution)/shard_map/ppermute | solution.py:692
  14.3 1.2 %collective-permute-start.1 = (f32[7,8,128]{2,1,0:T(8,128)S(1)}, f32[7,8,128]{2,1,0:T(8,128)S(1)}, u32[]{:S(2)}, u32[]{:S(2)}) collective-permute-start(f32[7,8,128]{2,1,0:T(8,128)S(1)} %get-tuple-element.21), channel_id=1, source_target_pairs={{0,1},{1,0},{2,3},{3,2},{4,5},{5,4},{6,7},{7,6},{8,9},{9,8},{10,11... | collective-permute-start | bytes 86024 | tf_op jit(solution)/shard_map/ppermute | solution.py:696
  14.3 3.7 %collective-permute-start.2 = (f32[5,8,128]{2,1,0:T(8,128)S(1)}, f32[5,8,128]{2,1,0:T(8,128)S(1)}, u32[]{:S(2)}, u32[]{:S(2)}) collective-permute-start(f32[5,8,128]{2,1,0:T(8,128)S(1)} %slice.4), channel_id=1, source_target_pairs={{0,1},{1,0},{2,3},{3,2},{4,5},{5,4},{6,7},{7,6},{8,9},{9,8},{10,11... | collective-permute-start | bytes 61448 | tf_op jit(solution)/shard_map/ppermute | solution.py:700

commit v8 on v7

--- a/solution.py
+++ b/solution.py
@@ -40,6 +40,13 @@
     parts = jnp.concatenate([high, mid, low], axis=0)
     out = lax.dot_general(parts, hot, dims, preferred_element_type=f32)
     return out[:rows] + (out[rows : 2 * rows] + out[2 * rows :])
+
+
+def total_of(terms):
+    while len(terms) > 1:
+        paired = [a + b for a, b in zip(terms[::2], terms[1::2])]
+        terms = paired + terms[len(terms) - len(terms) % 2 :]
+    return terms[0]
 
 
 def hot_of(condition):
@@ -465,21 +472,25 @@
     wells = wells_ref.shape[2]
     perfs = own_ref.shape[2]
     added = [[] for _ in range(3)]
+    holes = jnp.zeros((16, wells), f32)
+    lists = []
     for j in range(width):
         pair = jnp.sum(wells_ref[pl.ds(index_x[j] * count_y, count_y)], axis=0)
-        hole = pair[1:2] / pair[0:1]
-        tiles = jnp.concatenate(
-            [
-                blocks[j][last] if j else own_ref[BULK * cx],
-                from_left[j][cx],
-                from_right[j][cx],
-            ],
-            axis=1,
-        )
-        spot_xz, spot_y, well = tiles[0:1], tiles[1:2], tiles[2:3]
-        member = hot_of(iota((wells, 3 * perfs), 0).astype(f32) == well)
-        hole_at = split_dot(jnp.broadcast_to(hole, (16, wells)), member, NN)[0:1]
-        fall = tiles[6:7] - hole_at
+        holes = jnp.where(iota((16, wells), 0) == j, pair[1:2] / pair[0:1], holes)
+        lists += [
+            blocks[j][last] if j else own_ref[BULK * cx],
+            from_left[j][cx],
+            from_right[j][cx],
+        ]
+    listed = jnp.concatenate(lists, axis=1)
+    number = iota((wells, perfs), 0).astype(f32)
+    holes_at = jnp.concatenate(
+        [split_dot(holes, hot_of(number == v[2:3]), NN) for v in lists], axis=1
+    )
+    for j in range(width):
+        tiles = listed[:, 3 * perfs * j : 3 * perfs * (j + 1)]
+        spot_xz, spot_y = tiles[0:1], tiles[1:2]
+        fall = tiles[6:7] - holes_at[j : j + 1, 3 * perfs * j : 3 * perfs * (j + 1)]
         on_xz = iota((cx * nz, 3 * perfs), 0).astype(f32) == spot_xz
         spread = jnp.concatenate(
             [jnp.where(on_xz, tiles[3 + c : 4 + c] * fall, 0.0) for c in range(3)], axis=0
@@ -492,10 +503,15 @@
         )
         hot_side = hot_of(hot_y & (kept == 1))
         inner = split_dot(spread[:, :perfs], hot_of(hot_y[:, :perfs]), NT)
-        outer = split_dot(spread[:, perfs:], hot_side[:, perfs:], NT)
-        both = jnp.concatenate([inner, outer], axis=1).reshape(3, cx, nz, lanes)
+        inner = inner.reshape(3, cx, nz, cy)
+        aside = spread[:, perfs:]
+        if j:
+            aside = aside.reshape(3, cx * nz, 2 * perfs)
+            aside = aside[0] + aside[1] + aside[2]
+        outer = split_dot(aside, hot_side[:, perfs:], NT).reshape(-1, cx, nz, cy)
         for c in range(3):
-            added[c].append(both[c])
+            side = outer[c] if c < outer.shape[0] else jnp.zeros_like(outer[0])
+            added[c].append(jnp.concatenate([inner[c], side], axis=2))
     start = [-(resid[c] + jnp.concatenate(added[c], axis=0)) for c in range(3)]
     for c in range(3):
         residual_out[c] = -start[c][:cx, :, :cy]
@@ -518,14 +534,11 @@
     near[4] = jnp.where(level > 0, near[4], 0.0)
     near[5] = jnp.where(level < nz - 1, near[5], 0.0)
 
-    def direction(edge_of, where):
-        here = where(part)
+    def direction(edge_of, here, around, initial):
         rest = []
         for c in range(3):
-            coupled = edge_of(DCOL + c) * here
-            for q in range(6):
-                coupled = coupled + edge_of(OFFC + 3 * q + c) * where(near[q])
-            rest.append(where(start[c]) - coupled)
+            coupled = [edge_of(OFFC + 3 * q + c) * beyond for q, beyond in enumerate(around)]
+            rest.append(initial[c] - total_of([edge_of(DCOL + c) * here, *coupled]))
         solved = []
         for a in range(3):
             value = edge_of(DINV + 3 * a) * rest[0]
@@ -551,29 +564,48 @@
         tile, place = divmod(2 * cx * e, cy)
         return pltpu.roll(beside[tile], cy - place, 1) if place else beside[tile]
 
-    def gathered_side(v):
-        packed = jnp.zeros((nz, cy), f32)
+    def packed(tiles, shift):
+        result = jnp.zeros((nz, cy), f32)
         for x in range(cx):
-            turned = pltpu.roll(v[x, :, cy:], 2 * x + 1, 1)
-            packed = jnp.where((lane >= 2 * x) & (lane < 2 * x + 2), turned, packed)
-        return packed
+            turned = pltpu.roll(tiles[x], (2 * x + shift) % cy, 1)
+            result = jnp.where((lane >= 2 * x) & (lane < 2 * x + 2), turned, result)
+        return result
+
+    inside = [part[x, :, :cy] for x in range(cx)]
+    outside = [part[x, :, cy:] for x in range(cx)]
+    here = packed(outside, 1)
+    depth = iota((nz, cy), 0)
+    z_side = direction(
+        edge_side,
+        here,
+        [
+            packed([part[total - 1, :, cy:] * joined[width - 1], *outside[:-1]], 1),
+            packed([*outside[1:], part[cx % total, :, cy:] * joined[0]], 1),
+            packed([jnp.where(lane == cy - 1, a, b) for a, b in zip(inside, outside)], 2),
+            packed([jnp.where(lane == 0, a, b) for a, b in zip(inside, outside)], 0),
+            jnp.where(depth > 0, pltpu.roll(here, 1, 0), 0.0),
+            jnp.where(depth < nz - 1, pltpu.roll(here, nz - 1, 0), 0.0),
+        ],
+        [packed([start[c][x, :, cy:] for x in range(cx)], 1) for c in range(3)],
+    )
+
+    def direction_at(edge_of, where):
+        return direction(
+            edge_of, where(part), [where(v) for v in near], [where(v) for v in start]
+        )
 
     after, before = 1 % width, width - 1
-    z_own = direction(edge_own, lambda v: v[:cx, :, :cy])
-    z_side = [
-        jnp.stack([pltpu.roll(v, cy - 2 * x - 1, 1) for x in range(cx)])
-        for v in direction(edge_side, gathered_side)
-    ]
+    z_own = direction_at(edge_own, lambda v: v[:cx, :, :cy])
     if layers == 1:
-        z_next = z_last = direction(
+        z_next = z_last = direction_at(
             lambda e: blocks[after][edge_at + e],
             lambda v: jnp.where(at_x == 0, v[cx, :, :cy], v[total - 1, :, :cy]),
         )
     else:
-        z_next = direction(
+        z_next = direction_at(
             lambda e: blocks[after][edge_at + e], lambda v: v[after * cx, :, :cy]
         )
-        z_last = direction(
+        z_last = direction_at(
             lambda e: blocks[before][edge_at + EDGE + e],
             lambda v: v[before * cx + cx - 1, :, :cy],
         )
@@ -581,13 +613,20 @@
     around = []
     for k in range(3):
         z_out[k] = z_own[k]
-        ext = jnp.concatenate([z_own[k], z_side[k]], axis=2)
+        before_y, after_y = [], []
+        for x in range(cx):
+            left = pltpu.roll(z_side[k], (cy - 2 * x) % cy, 1) if x else z_side[k]
+            right = pltpu.roll(z_side[k], (cy - 2 - 2 * x) % cy, 1)
+            before_y.append(jnp.where(lane == 0, left, pltpu.roll(z_own[k][x], 1, 1)))
+            after_y.append(
+                jnp.where(lane == cy - 1, right, pltpu.roll(z_own[k][x], cy - 1, 1))
+            )
         around.append(
             [
                 jnp.concatenate([(z_last[k] * joined[width - 1])[None], z_own[k][:-1]], axis=0),
                 jnp.concatenate([z_own[k][1:], (z_next[k] * joined[0])[None]], axis=0),
-                last_y(ext)[:, :, :cy],
-                next_y(ext)[:, :, :cy],
+                jnp.stack(before_y),
+                jnp.stack(after_y),
                 jnp.where(level_own > 0, last_z(z_own[k]), 0.0),
                 jnp.where(level_own < nz - 1, next_z(z_own[k]), 0.0),
             ]
@@ -595,12 +634,9 @@
     along = jnp.zeros((nz, cy), f32)
     square = jnp.zeros((nz, cy), f32)
     for c in range(3):
-        mapped = diag_ref[c, 0] * z_own[0]
-        for k in range(1, 3):
-            mapped = mapped + diag_ref[c, k] * z_own[k]
-        for q in range(6):
-            for k in range(3):
-                mapped = mapped + off_ref[q, c, k] * around[k][q]
+        terms = [diag_ref[c, k] * z_own[k] for k in range(3)]
+        terms += [off_ref[q, c, k] * around[k][q] for q in range(6) for k in range(3)]
+        mapped = total_of(terms)
         along = along + jnp.sum(mapped * start[c][:cx, :, :cy], axis=0)
         square = square + jnp.sum(mapped * mapped, axis=0)
     along = jnp.sum(along, axis=0, keepdims=True)

time: 29.8 us -> 29.6 us (level)
  no operation moved by 1% of the time
where the time goes in v8:
time: 29.6 us; the launch traced here: 29.4 us
  starting transfers between devices  10.6 us (36%)
  blocking collectives  9.71 us (33%)
  waiting for transfers between devices  4.95 us (17%)
  Pallas kernels  3.52 us (12%)
  between operations  0.67 us (2%)
    all_to_all x1, blocking collectives, body(): sums_all = lax.all_to_all(sums, ('gx', 'gy'), 0, 0)  9.71 us
    all_to_all x1, starting transfers between devices, body(): wells_all = lax.all_to_all(wells_part, ('gx', 'gy'), 0, 0)  5.19 us
    ppermute x2, starting transfers between devices, from_x(): lax.ppermute(values, 'gx', [((i + offset) % count_x, i) for i in range(co...  4.79 us
    all_to_all x1, waiting for transfers between devices, body(): wells_all = lax.all_to_all(wells_part, ('gx', 'gy'), 0, 0)  2.53 us
    pallas_call x1, Pallas kernels, body(): pl.pallas_call(functools.partial(before_kernel, count_x, count_y), in_spe...  1.83 us
    ppermute x1, waiting for transfers between devices, body(): yb_got = lax.ppermute(yb, ('gx', 'gy'), others)  1.73 us
    pallas_call x1, Pallas kernels, body(): pl.pallas_call(functools.partial(main_kernel, count_x, count_y, tuple(off...  0.89 us
    pallas_call x1, Pallas kernels, body(): pl.pallas_call(after_kernel, in_specs=[whole] * 3, out_specs=[anywhere] *...  0.8 us
  transfers between devices with their start and end apart: 6, of which 3 were waited for; matrix products, arithmetic and copies ran while one was open for 0% of the time, Pallas kernels for 0%

profile of v8, /device:TPU:0, one launch (start us, length us, event | category | flops | bytes accessed | tf_op | source)
XLA Modules:
  0.0 29.4 jit_solution(2958538823546159856)
XLA Ops:
  0.6 1.8 %before.1 = (f32[32,2,128]{2,1,0:T(2,128)}, f32[68,8,128]{2,1,0:T(8,128)S(1)}, f32[62,8,128]{2,1,0:T(8,128)S(1)}, f32[7,8,128]{2,1,0:T(8,128)S(1)}, f32[8,8,128]...) custom-call(f32[4,8,128]{2,1,0:T(8,128)} %refs_0_.1, ...), custom_call_target="tpu_custom_call" | custom-call | tf_op jit(solution)/shard_map/before/pallas_call | solution.py:700
  2.5 3.0 %collective-permute-start = (f32[68,8,128]{2,1,0:T(8,128)S(1)}, f32[68,8,128]{2,1,0:T(8,128)S(1)}, u32[]{:S(2)}, u32[]{:S(2)}) collective-permute-start(f32[68,8,128]{2,1,0:T(8,128)S(1)} %get-tuple-element.20), channel_id=1, source_target_pairs={{16,0},{0,16},{17,1},{1,17},{18,2},{2,18},{19,3},{3,19},{20,4},{4,... | collective-permute-start | bytes 835592 | tf_op jit(solution)/shard_map/ppermute | solution.py:728
  5.5 0.1 collective-permute-start.3
  5.6 5.2 %all-to-all-start = ((f32[32,2,128]{2,1,0:T(2,128)}), f32[32,2,128]{2,1,0:T(2,128)S(1)}, u32[]{:S(2)}, u32[]{:S(2)}) async-start(f32[32,2,128]{2,1,0:T(2,128)} %get-tuple-element.15), calls=%async_computation | async-start | bytes 65536 | tf_op jit(solution)/shard_map/all_to_all | solution.py:735
  10.7 1.7 %collective-permute-done.3.refs_8_ = f32[8,8,128]{2,1,0:T(8,128)S(1)} collective-permute-done((f32[8,8,128]{2,1,0:T(8,128)S(1)}, f32[8,8,128]{2,1,0:T(8,128)S(1)}, u32[]{:S(2)}, u32[]{:S(2)}) %collective-permute-start.3) | collective-permute-done | bytes 32800 | tf_op jit(solution)/shard_map/ppermute | solution.py:733
  12.5 1.8 %collective-permute-start.4 = (f32[8,8,128]{2,1,0:T(8,128)S(1)}, f32[8,8,128]{2,1,0:T(8,128)S(1)}, u32[]{:S(2)}, u32[]{:S(2)}) collective-permute-start(f32[8,8,128]{2,1,0:T(8,128)S(1)} %collective-permute-done.3.refs_8_), channel_id=1, source_target_pairs={{16,0},{0,16},{17,1},{1,17},{18,2},{2,18},{19,3},{3,19},{20,4},{4,... | collective-permute-start | bytes 98312 | tf_op jit(solution)/shard_map/ppermute | solution.py:728
  14.3 0.0 collective-permute-start.1
  14.3 0.0 collective-permute-done.refs_5_
  14.3 0.5 %collective-permute-start.2 = (f32[5,8,128]{2,1,0:T(8,128)S(1)}, f32[5,8,128]{2,1,0:T(8,128)S(1)}, u32[]{:S(2)}, u32[]{:S(2)}) collective-permute-start(f32[5,8,128]{2,1,0:T(8,128)S(1)} %slice.4), channel_id=1, source_target_pairs={{0,1},{1,0},{2,3},{3,2},{4,5},{5,4},{6,7},{7,6},{8,9},{9,8},{10,11... | collective-permute-start | bytes 61448 | tf_op jit(solution)/shard_map/ppermute | solution.py:736
  14.8 0.7 %collective-permute-done.1.refs_6_ = f32[7,8,128]{2,1,0:T(8,128)S(1)} collective-permute-done((f32[7,8,128]{2,1,0:T(8,128)S(1)}, f32[7,8,128]{2,1,0:T(8,128)S(1)}, u32[]{:S(2)}, u32[]{:S(2)}) %collective-permute-start.1) | collective-permute-done | bytes 28704 | tf_op jit(solution)/shard_map/ppermute | solution.py:732
  15.5 2.5 %all-to-all-done.refs_0_ = f32[32,2,128]{2,1,0:T(2,128)S(1)} async-done(((f32[32,2,128]{2,1,0:T(2,128)}), f32[32,2,128]{2,1,0:T(2,128)S(1)}, u32[]{:S(2)}, u32[]{:S(2)}) %all-to-all-start) | async-done | bytes 32800 | tf_op jit(solution)/shard_map/all_to_all | solution.py:735
  18.0 0.0 collective-permute-done.4.refs_9_
  18.0 0.0 collective-permute-done.2.refs_7_
  18.0 0.9 %main.1 = (f32[3,4,8,128]{3,2,1,0:T(8,128)S(1)}, f32[3,4,8,128]{3,2,1,0:T(8,128)S(1)}, f32[32,2,128]{2,1,0:T(2,128)S(1)}) custom-call(f32[32,2,128]{2,1,0:T(2,128)S(1)} %all-to-all-done.refs_0_, f32[3,3,4,8,128]{4,3,2,1,0:T(8,128)S(1)} %get-tuple-element.16.refs_1_, f32[6,3,3,4,8,128]{5,4,3,2,1,0:T(8,128)S(1)} %get-tuple-element.17.refs_2_, ...), custom_call_target="tpu_custom_call" | custom-call | tf_op jit(solution)/shard_map/main/pallas_call | solution.py:739
  18.9 9.7 %all_to_all.10.sums_ref = f32[32,2,128]{2,1,0:T(2,128)S(1)} all-to-all(f32[32,2,128]{2,1,0:T(2,128)S(1)} %get-tuple-element.23), channel_id=1, replica_groups=mesh['gx'=2,'gy'=16] {'gx','gy'}, dimensions={0} | all-to-all | bytes 65536 | tf_op jit(solution)/shard_map/all_to_all | solution.py:752
  28.6 0.8 %after.1 = (f32[3,4,8,128]{3,2,1,0:T(8,128)}, f32[3,4,8,128]{3,2,1,0:T(8,128)}) custom-call(f32[32,2,128]{2,1,0:T(2,128)S(1)} %all_to_all.10.sums_ref, f32[3,4,8,128]{3,2,1,0:T(8,128)S(1)} %get-tuple-element.24.z_ref, f32[3,4,8,128]{3,2,1,0:T(8,128)S(1)} %get-tuple-element.25.residual_ref), custom_call_target="tpu_custom_call" | custom-call | tf_op jit(solution)/shard_map/after/pallas_call | solution.py:753
  (1 shorter events, 0.0 us)
Async XLA Ops:
  2.5 11.8 %collective-permute-start = (f32[68,8,128]{2,1,0:T(8,128)S(1)}, f32[68,8,128]{2,1,0:T(8,128)S(1)}, u32[]{:S(2)}, u32[]{:S(2)}) collective-permute-start(f32[68,8,128]{2,1,0:T(8,128)S(1)} %get-tuple-element.20), channel_id=1, source_target_pairs={{16,0},{0,16},{17,1},{1,17},{18,2},{2,18},{19,3},{3,19},{20,4},{4,... | collective-permute-start | bytes 835592 | tf_op jit(solution)/shard_map/ppermute | solution.py:728
  5.5 7.0 %collective-permute-start.3 = (f32[8,8,128]{2,1,0:T(8,128)S(1)}, f32[8,8,128]{2,1,0:T(8,128)S(1)}, u32[]{:S(2)}, u32[]{:S(2)}) collective-permute-start(f32[8,8,128]{2,1,0:T(8,128)S(1)} %get-tuple-element.22), channel_id=1, source_target_pairs={{0,16},{1,2},{2,1},{3,4},{4,3},{5,6},{6,5},{7,8},{8,7},{9,10},{10,... | collective-permute-start | bytes 98312 | tf_op jit(solution)/shard_map/ppermute | solution.py:733
  5.6 12.4 %all-to-all-start = ((f32[32,2,128]{2,1,0:T(2,128)}), f32[32,2,128]{2,1,0:T(2,128)S(1)}, u32[]{:S(2)}, u32[]{:S(2)}) async-start(f32[32,2,128]{2,1,0:T(2,128)} %get-tuple-element.15), calls=%async_computation | async-start | bytes 65536 | tf_op jit(solution)/shard_map/all_to_all | solution.py:735
  12.5 5.5 %collective-permute-start.4 = (f32[8,8,128]{2,1,0:T(8,128)S(1)}, f32[8,8,128]{2,1,0:T(8,128)S(1)}, u32[]{:S(2)}, u32[]{:S(2)}) collective-permute-start(f32[8,8,128]{2,1,0:T(8,128)S(1)} %collective-permute-done.3.refs_8_), channel_id=1, source_target_pairs={{16,0},{0,16},{17,1},{1,17},{18,2},{2,18},{19,3},{3,19},{20,4},{4,... | collective-permute-start | bytes 98312 | tf_op jit(solution)/shard_map/ppermute | solution.py:728
  14.3 1.2 %collective-permute-start.1 = (f32[7,8,128]{2,1,0:T(8,128)S(1)}, f32[7,8,128]{2,1,0:T(8,128)S(1)}, u32[]{:S(2)}, u32[]{:S(2)}) collective-permute-start(f32[7,8,128]{2,1,0:T(8,128)S(1)} %get-tuple-element.21), channel_id=1, source_target_pairs={{0,1},{1,0},{2,3},{3,2},{4,5},{5,4},{6,7},{7,6},{8,9},{9,8},{10,11... | collective-permute-start | bytes 86024 | tf_op jit(solution)/shard_map/ppermute | solution.py:732
  14.3 3.7 %collective-permute-start.2 = (f32[5,8,128]{2,1,0:T(8,128)S(1)}, f32[5,8,128]{2,1,0:T(8,128)S(1)}, u32[]{:S(2)}, u32[]{:S(2)}) collective-permute-start(f32[5,8,128]{2,1,0:T(8,128)S(1)} %slice.4), channel_id=1, source_target_pairs={{0,1},{1,0},{2,3},{3,2},{4,5},{5,4},{6,7},{7,6},{8,9},{9,8},{10,11... | collective-permute-start | bytes 61448 | tf_op jit(solution)/shard_map/ppermute | solution.py:736

commit v9 on v8

--- a/solution.py
+++ b/solution.py
@@ -114,13 +114,14 @@
     perfs = cells.shape[1]
     spot_xz = lax.div(cells, cy)
     spot_y = lax.rem(cells, cy)
-    stacked = jnp.concatenate([m.reshape(cx * nz, cy) for m in mobile + [press]], axis=0)
+    stacked = jnp.concatenate([v.reshape(cx * nz, cy) for v in (water, gas, press)], axis=0)
     hot_y = hot_of(iota((cy, perfs), 0) == spot_y)
-    picked = split_dot(stacked, hot_y, NN).reshape(4, cx * nz, perfs)
+    picked = split_dot(stacked, hot_y, NN).reshape(3, cx * nz, perfs)
     on_xz = iota((cx * nz, perfs), 0) == spot_xz
-    at_perf = [
-        jnp.sum(jnp.where(on_xz, picked[i], 0.0), axis=0, keepdims=True) for i in range(4)
-    ]
+    water_at, gas_at, press_at = (
+        jnp.sum(jnp.where(on_xz, picked[i], 0.0), axis=0, keepdims=True) for i in range(3)
+    )
+    at_perf = [*mobilities(water_at, gas_at), press_at]
     index_vals = index_ref[...]
     parts = [index_vals * at_perf[i] for i in range(3)]
     strength = index_vals * (at_perf[0] + at_perf[1] + at_perf[2])
@@ -706,7 +707,7 @@
             shape((tiles, nz, cy), f32),
             shape((BULK * cx + 2, nz, cy), f32),
             shape((cx + 1 + groups, nz, cy), f32),
-            shape((max(cx + 1 + groups, 2 * cx), nz, cy), f32),
+            shape((max(cx + 1 + groups, 3 * cx), nz, cy), f32),
             shape((9, cx, nz, cy), f32),
             shape(jac_diag.shape, f32),
             shape(jac_off.shape, f32),
@@ -734,7 +735,7 @@
     blocks = [from_x(block, o) for o in offsets[1:]]
     wells_all = lax.all_to_all(wells_part, ("gx", "gy"), 0, 0)
     ya_all = [ya_got] + [lax.ppermute(v[columns_at:], "gy", pairs) for v in blocks]
-    yb_all = [yb_got] + [from_x(yb_got, o) for o in offsets[1:]]
+    yb_all = [yb_got] + [from_x(yb_got[: cx + 1], o) for o in offsets[1:]]
 
     residual, direction, sums = pl.pallas_call(
         functools.partial(main_kernel, count_x, count_y, tuple(offsets)),

time: 29.6 us -> 29.5 us (level)
    all_to_all x1, waiting for transfers between devices: 2.53 us -> 3.53 us  [body(): wells_all = lax.all_to_all(wells_part, ('gx', 'gy'), 0, 0)]
    ppermute x1, waiting for transfers between devices: 0.68 us -> 0.01 us  [body(): ya_got = lax.ppermute(ya, 'gy', pairs)]
    ppermute x1, starting transfers between devices: 0.51 us -> 0.01 us  [body(): lax.ppermute(v[columns_at:], 'gy', pairs)]
    ppermute x1, starting transfers between devices: 0.01 us -> 0.32 us  [body(): ya_got = lax.ppermute(ya, 'gy', pairs)]
  transfers between devices with their start and end apart: 6 -> 6, of which waited for: 3 -> 2; matrix products, arithmetic and copies ran while one was open for 0% -> 0% of each run, Pallas kernels for 0% -> 0%
where the time goes in v9:
time: 29.5 us; the launch traced here: 29.3 us
  starting transfers between devices  10.4 us (35%)
  blocking collectives  9.64 us (33%)
  waiting for transfers between devices  5.13 us (17%)
  Pallas kernels  3.52 us (12%)
  between operations  0.68 us (2%)
    all_to_all x1, blocking collectives, body(): sums_all = lax.all_to_all(sums, ('gx', 'gy'), 0, 0)  9.64 us
    all_to_all x1, starting transfers between devices, body(): wells_all = lax.all_to_all(wells_part, ('gx', 'gy'), 0, 0)  5.19 us
    ppermute x2, starting transfers between devices, from_x(): lax.ppermute(values, 'gx', [((i + offset) % count_x, i) for i in range(co...  4.79 us
    all_to_all x1, waiting for transfers between devices, body(): wells_all = lax.all_to_all(wells_part, ('gx', 'gy'), 0, 0)  3.53 us
    pallas_call x1, Pallas kernels, body(): pl.pallas_call(functools.partial(before_kernel, count_x, count_y), in_spe...  1.82 us
    ppermute x1, waiting for transfers between devices, body(): yb_got = lax.ppermute(yb, ('gx', 'gy'), others)  1.59 us
    pallas_call x1, Pallas kernels, body(): pl.pallas_call(functools.partial(main_kernel, count_x, count_y, tuple(off...  0.9 us
    pallas_call x1, Pallas kernels, body(): pl.pallas_call(after_kernel, in_specs=[whole] * 3, out_specs=[anywhere] *...  0.8 us
  transfers between devices with their start and end apart: 6, of which 2 were waited for; matrix products, arithmetic and copies ran while one was open for 0% of the time, Pallas kernels for 0%

profile of v9, /device:TPU:0, one launch (start us, length us, event | category | flops | bytes accessed | tf_op | source)
XLA Modules:
  0.0 29.3 jit_solution(14230011244771774373)
XLA Ops:
  0.6 1.8 %before.1 = (f32[32,2,128]{2,1,0:T(2,128)}, f32[68,8,128]{2,1,0:T(8,128)S(1)}, f32[62,8,128]{2,1,0:T(8,128)S(1)}, f32[7,8,128]{2,1,0:T(8,128)S(1)}, f32[12,8,128...) custom-call(f32[4,8,128]{2,1,0:T(8,128)} %refs_0_.1, ...), custom_call_target="tpu_custom_call" | custom-call | tf_op jit(solution)/shard_map/before/pallas_call | solution.py:701
  2.5 3.0 %collective-permute-start = (f32[68,8,128]{2,1,0:T(8,128)S(1)}, f32[68,8,128]{2,1,0:T(8,128)S(1)}, u32[]{:S(2)}, u32[]{:S(2)}) collective-permute-start(f32[68,8,128]{2,1,0:T(8,128)S(1)} %get-tuple-element.20), channel_id=1, source_target_pairs={{16,0},{0,16},{17,1},{1,17},{18,2},{2,18},{19,3},{3,19},{20,4},{4,... | collective-permute-start | bytes 835592 | tf_op jit(solution)/shard_map/ppermute | solution.py:729
  5.5 0.1 collective-permute-start.3
  5.5 5.2 %all-to-all-start = ((f32[32,2,128]{2,1,0:T(2,128)}), f32[32,2,128]{2,1,0:T(2,128)S(1)}, u32[]{:S(2)}, u32[]{:S(2)}) async-start(f32[32,2,128]{2,1,0:T(2,128)} %get-tuple-element.15), calls=%async_computation | async-start | bytes 65536 | tf_op jit(solution)/shard_map/all_to_all | solution.py:736
  10.7 0.3 %collective-permute-start.1 = (f32[7,8,128]{2,1,0:T(8,128)S(1)}, f32[7,8,128]{2,1,0:T(8,128)S(1)}, u32[]{:S(2)}, u32[]{:S(2)}) collective-permute-start(f32[7,8,128]{2,1,0:T(8,128)S(1)} %get-tuple-element.21), channel_id=1, source_target_pairs={{0,1},{1,0},{2,3},{3,2},{4,5},{5,4},{6,7},{7,6},{8,9},{9,8},{10,11... | collective-permute-start | bytes 86024 | tf_op jit(solution)/shard_map/ppermute | solution.py:733
  11.1 1.6 %collective-permute-done.3.refs_8_ = f32[12,8,128]{2,1,0:T(8,128)S(1)} collective-permute-done((f32[12,8,128]{2,1,0:T(8,128)S(1)}, f32[12,8,128]{2,1,0:T(8,128)S(1)}, u32[]{:S(2)}, u32[]{:S(2)}) %collective-permute-start.3) | collective-permute-done | bytes 49184 | tf_op jit(solution)/shard_map/ppermute | solution.py:734
  12.6 1.8 %collective-permute-start.4 = (f32[5,8,128]{2,1,0:T(8,128)S(1)}, f32[5,8,128]{2,1,0:T(8,128)S(1)}, u32[]{:S(2)}, u32[]{:S(2)}) collective-permute-start(f32[5,8,128]{2,1,0:T(8,128)S(1)} %slice.9), channel_id=1, source_target_pairs={{16,0},{0,16},{17,1},{1,17},{18,2},{2,18},{19,3},{3,19},{20,4},{4,... | collective-permute-start | bytes 61448 | tf_op jit(solution)/shard_map/ppermute | solution.py:729
  14.4 0.0 collective-permute-done.refs_5_
  14.4 0.0 collective-permute-start.2
  14.4 0.0 collective-permute-done.1.refs_6_
  14.5 3.5 %all-to-all-done.refs_0_ = f32[32,2,128]{2,1,0:T(2,128)S(1)} async-done(((f32[32,2,128]{2,1,0:T(2,128)}), f32[32,2,128]{2,1,0:T(2,128)S(1)}, u32[]{:S(2)}, u32[]{:S(2)}) %all-to-all-start) | async-done | bytes 32800 | tf_op jit(solution)/shard_map/all_to_all | solution.py:736
  18.0 0.0 collective-permute-done.4.refs_9_
  18.0 0.0 collective-permute-done.2.refs_7_
  18.0 0.9 %main.1 = (f32[3,4,8,128]{3,2,1,0:T(8,128)S(1)}, f32[3,4,8,128]{3,2,1,0:T(8,128)S(1)}, f32[32,2,128]{2,1,0:T(2,128)S(1)}) custom-call(f32[32,2,128]{2,1,0:T(2,128)S(1)} %all-to-all-done.refs_0_, f32[3,3,4,8,128]{4,3,2,1,0:T(8,128)S(1)} %get-tuple-element.16.refs_1_, f32[6,3,3,4,8,128]{5,4,3,2,1,0:T(8,128)S(1)} %get-tuple-element.17.refs_2_, ...), custom_call_target="tpu_custom_call" | custom-call | tf_op jit(solution)/shard_map/main/pallas_call | solution.py:740
  18.9 9.6 %all_to_all.10.sums_ref = f32[32,2,128]{2,1,0:T(2,128)S(1)} all-to-all(f32[32,2,128]{2,1,0:T(2,128)S(1)} %get-tuple-element.23), channel_id=1, replica_groups=mesh['gx'=2,'gy'=16] {'gx','gy'}, dimensions={0} | all-to-all | bytes 65536 | tf_op jit(solution)/shard_map/all_to_all | solution.py:753
  28.5 0.8 %after.1 = (f32[3,4,8,128]{3,2,1,0:T(8,128)}, f32[3,4,8,128]{3,2,1,0:T(8,128)}) custom-call(f32[32,2,128]{2,1,0:T(2,128)S(1)} %all_to_all.10.sums_ref, f32[3,4,8,128]{3,2,1,0:T(8,128)S(1)} %get-tuple-element.24.z_ref, f32[3,4,8,128]{3,2,1,0:T(8,128)S(1)} %get-tuple-element.25.residual_ref), custom_call_target="tpu_custom_call" | custom-call | tf_op jit(solution)/shard_map/after/pallas_call | solution.py:754
  (2 shorter events, 0.0 us)
Async XLA Ops:
  2.5 12.0 %collective-permute-start = (f32[68,8,128]{2,1,0:T(8,128)S(1)}, f32[68,8,128]{2,1,0:T(8,128)S(1)}, u32[]{:S(2)}, u32[]{:S(2)}) collective-permute-start(f32[68,8,128]{2,1,0:T(8,128)S(1)} %get-tuple-element.20), channel_id=1, source_target_pairs={{16,0},{0,16},{17,1},{1,17},{18,2},{2,18},{19,3},{3,19},{20,4},{4,... | collective-permute-start | bytes 835592 | tf_op jit(solution)/shard_map/ppermute | solution.py:729
  5.5 7.2 %collective-permute-start.3 = (f32[12,8,128]{2,1,0:T(8,128)S(1)}, f32[12,8,128]{2,1,0:T(8,128)S(1)}, u32[]{:S(2)}, u32[]{:S(2)}) collective-permute-start(f32[12,8,128]{2,1,0:T(8,128)S(1)} %get-tuple-element.22), channel_id=1, source_target_pairs={{0,16},{1,2},{2,1},{3,4},{4,3},{5,6},{6,5},{7,8},{8,7},{9,10},{10,... | collective-permute-start | bytes 147464 | tf_op jit(solution)/shard_map/ppermute | solution.py:734
  5.5 12.4 %all-to-all-start = ((f32[32,2,128]{2,1,0:T(2,128)}), f32[32,2,128]{2,1,0:T(2,128)S(1)}, u32[]{:S(2)}, u32[]{:S(2)}) async-start(f32[32,2,128]{2,1,0:T(2,128)} %get-tuple-element.15), calls=%async_computation | async-start | bytes 65536 | tf_op jit(solution)/shard_map/all_to_all | solution.py:736
  10.7 3.7 %collective-permute-start.1 = (f32[7,8,128]{2,1,0:T(8,128)S(1)}, f32[7,8,128]{2,1,0:T(8,128)S(1)}, u32[]{:S(2)}, u32[]{:S(2)}) collective-permute-start(f32[7,8,128]{2,1,0:T(8,128)S(1)} %get-tuple-element.21), channel_id=1, source_target_pairs={{0,1},{1,0},{2,3},{3,2},{4,5},{5,4},{6,7},{7,6},{8,9},{9,8},{10,11... | collective-permute-start | bytes 86024 | tf_op jit(solution)/shard_map/ppermute | solution.py:733
  12.6 5.3 %collective-permute-start.4 = (f32[5,8,128]{2,1,0:T(8,128)S(1)}, f32[5,8,128]{2,1,0:T(8,128)S(1)}, u32[]{:S(2)}, u32[]{:S(2)}) collective-permute-start(f32[5,8,128]{2,1,0:T(8,128)S(1)} %slice.9), channel_id=1, source_target_pairs={{16,0},{0,16},{17,1},{1,17},{18,2},{2,18},{19,3},{3,19},{20,4},{4,... | collective-permute-start | bytes 61448 | tf_op jit(solution)/shard_map/ppermute | solution.py:729
  14.4 3.6 %collective-permute-start.2 = (f32[5,8,128]{2,1,0:T(8,128)S(1)}, f32[5,8,128]{2,1,0:T(8,128)S(1)}, u32[]{:S(2)}, u32[]{:S(2)}) collective-permute-start(f32[5,8,128]{2,1,0:T(8,128)S(1)} %slice.8), channel_id=1, source_target_pairs={{0,1},{1,0},{2,3},{3,2},{4,5},{5,4},{6,7},{7,6},{8,9},{9,8},{10,11... | collective-permute-start | bytes 61448 | tf_op jit(solution)/shard_map/ppermute | solution.py:737

commit v10 on v9

--- a/solution.py
+++ b/solution.py
@@ -141,8 +141,17 @@
     rates = jnp.sum(jnp.where(mine, column, 0.0), axis=0, keepdims=True)
     pair = sums[:2] - jnp.where(iota((2, wells), 0) == 1, rates, 0.0)
     wells_out[...] = jnp.broadcast_to(pair[None], wells_out.shape)
-    wells_copy = pltpu.make_async_copy(wells_out, wells_hbm, sems.at[11])
-    wells_copy.start()
+    part_size = wells_out.shape[0] // 2
+    wells_copies = [
+        pltpu.make_async_copy(
+            wells_out.at[pl.ds(i * part_size, part_size)],
+            wells_hbm.at[pl.ds(i * part_size, part_size)],
+            sems.at[11 + i],
+        )
+        for i in range(2)
+    ]
+    for each in wells_copies:
+        each.start()
 
     perf_rows = [
         spot_xz.astype(f32),
@@ -240,6 +249,7 @@
     put_inner(SUM, part[0] + part[1] + part[2])
 
     copies[9].wait()
+    copies[10].wait()
     diag = [[diag_ref[a, b] for b in range(3)] for a in range(3)]
     inverse = 1.0 / (diag[0][0] + diag[1][0] + diag[2][0])
     put_bulk(INV, inverse)
@@ -262,7 +272,6 @@
             dinv_out[3 * a + b] = solve
             put_edge(DINV + 3 * a + b, solve)
 
-    copies[10].wait()
     for q in range(6):
         columns = [off_ref[q, c, 0] for c in range(3)]
         if q == 4:
@@ -285,7 +294,8 @@
         yb_out[cx + 1 + t] = values
     for spare in range(cx + 1 + len(beside), yb_out.shape[0]):
         yb_out[spare] = jnp.zeros((nz, cy), f32)
-    wells_copy.wait()
+    for each in wells_copies:
+        each.wait()
 
 
 def main_kernel(count_x, count_y, offsets, *refs):
@@ -707,7 +717,7 @@
             shape((tiles, nz, cy), f32),
             shape((BULK * cx + 2, nz, cy), f32),
             shape((cx + 1 + groups, nz, cy), f32),
-            shape((max(cx + 1 + groups, 3 * cx), nz, cy), f32),
+            shape((max(cx + 1 + groups, 2 * cx), nz, cy), f32),
             shape((9, cx, nz, cy), f32),
             shape(jac_diag.shape, f32),
             shape(jac_off.shape, f32),
@@ -716,7 +726,7 @@
             *[pltpu.VMEM(v.shape, v.dtype) for v in fields[:5]],
             *[pltpu.VMEM(v.shape, v.dtype) for v in perforations],
             pltpu.VMEM((devices, 2, wells), f32),
-            pltpu.SemaphoreType.DMA((12,)),
+            pltpu.SemaphoreType.DMA((13,)),
         ],
         compiler_params=params,
         name="before",
@@ -735,7 +745,7 @@
     blocks = [from_x(block, o) for o in offsets[1:]]
     wells_all = lax.all_to_all(wells_part, ("gx", "gy"), 0, 0)
     ya_all = [ya_got] + [lax.ppermute(v[columns_at:], "gy", pairs) for v in blocks]
-    yb_all = [yb_got] + [from_x(yb_got[: cx + 1], o) for o in offsets[1:]]
+    yb_all = [yb_got] + [from_x(yb_got, o) for o in offsets[1:]]
 
     residual, direction, sums = pl.pallas_call(
         functools.partial(main_kernel, count_x, count_y, tuple(offsets)),

time: 29.5 us -> 29.6 us (level)
    all_to_all x1, waiting for transfers between devices: 3.53 us -> 2.53 us  [body(): wells_all = lax.all_to_all(wells_part, ('gx', 'gy'), 0, 0)]
    ppermute x1, waiting for transfers between devices: 0.01 us -> 0.68 us  [body(): ya_got = lax.ppermute(ya, 'gy', pairs)]
    ppermute x1, starting transfers between devices: 0.01 us -> 0.51 us  [body(): lax.ppermute(v[columns_at:], 'gy', pairs)]
    ppermute x1, starting transfers between devices: 0.32 us -> 0.01 us  [body(): ya_got = lax.ppermute(ya, 'gy', pairs)]
  transfers between devices with their start and end apart: 6 -> 6, of which waited for: 2 -> 3; matrix products, arithmetic and copies ran while one was open for 0% -> 0% of each run, Pallas kernels for 0% -> 0%
where the time goes in v10:
time: 29.6 us; the launch traced here: 29.4 us
  starting transfers between devices  10.6 us (36%)
  blocking collectives  9.71 us (33%)
  waiting for transfers between devices  4.95 us (17%)
  Pallas kernels  3.51 us (12%)
  between operations  0.67 us (2%)
    all_to_all x1, blocking collectives, body(): sums_all = lax.all_to_all(sums, ('gx', 'gy'), 0, 0)  9.71 us
    all_to_all x1, starting transfers between devices, body(): wells_all = lax.all_to_all(wells_part, ('gx', 'gy'), 0, 0)  5.19 us
    ppermute x2, starting transfers between devices, from_x(): lax.ppermute(values, 'gx', [((i + offset) % count_x, i) for i in range(co...  4.79 us
    all_to_all x1, waiting for transfers between devices, body(): wells_all = lax.all_to_all(wells_part, ('gx', 'gy'), 0, 0)  2.53 us
    pallas_call x1, Pallas kernels, body(): pl.pallas_call(functools.partial(before_kernel, count_x, count_y), in_spe...  1.82 us
    ppermute x1, waiting for transfers between devices, body(): yb_got = lax.ppermute(yb, ('gx', 'gy'), others)  1.73 us
    pallas_call x1, Pallas kernels, body(): pl.pallas_call(functools.partial(main_kernel, count_x, count_y, tuple(off...  0.88 us
    pallas_call x1, Pallas kernels, body(): pl.pallas_call(after_kernel, in_specs=[whole] * 3, out_specs=[anywhere] *...  0.8 us
  transfers between devices with their start and end apart: 6, of which 3 were waited for; matrix products, arithmetic and copies ran while one was open for 0% of the time, Pallas kernels for 0%

profile of v10, /device:TPU:0, one launch (start us, length us, event | category | flops | bytes accessed | tf_op | source)
XLA Modules:
  0.0 29.4 jit_solution(8124039503793775970)
XLA Ops:
  0.6 1.8 %before.1 = (f32[32,2,128]{2,1,0:T(2,128)}, f32[68,8,128]{2,1,0:T(8,128)S(1)}, f32[62,8,128]{2,1,0:T(8,128)S(1)}, f32[7,8,128]{2,1,0:T(8,128)S(1)}, f32[8,8,128]...) custom-call(f32[4,8,128]{2,1,0:T(8,128)} %refs_0_.1, ...), custom_call_target="tpu_custom_call" | custom-call | tf_op jit(solution)/shard_map/before/pallas_call | solution.py:711
  2.5 3.0 %collective-permute-start = (f32[68,8,128]{2,1,0:T(8,128)S(1)}, f32[68,8,128]{2,1,0:T(8,128)S(1)}, u32[]{:S(2)}, u32[]{:S(2)}) collective-permute-start(f32[68,8,128]{2,1,0:T(8,128)S(1)} %get-tuple-element.20), channel_id=1, source_target_pairs={{16,0},{0,16},{17,1},{1,17},{18,2},{2,18},{19,3},{3,19},{20,4},{4,... | collective-permute-start | bytes 835592 | tf_op jit(solution)/shard_map/ppermute | solution.py:739
  5.5 0.1 collective-permute-start.3
  5.5 5.2 %all-to-all-start = ((f32[32,2,128]{2,1,0:T(2,128)}), f32[32,2,128]{2,1,0:T(2,128)S(1)}, u32[]{:S(2)}, u32[]{:S(2)}) async-start(f32[32,2,128]{2,1,0:T(2,128)} %get-tuple-element.15), calls=%async_computation | async-start | bytes 65536 | tf_op jit(solution)/shard_map/all_to_all | solution.py:746
  10.7 1.7 %collective-permute-done.3.refs_8_ = f32[8,8,128]{2,1,0:T(8,128)S(1)} collective-permute-done((f32[8,8,128]{2,1,0:T(8,128)S(1)}, f32[8,8,128]{2,1,0:T(8,128)S(1)}, u32[]{:S(2)}, u32[]{:S(2)}) %collective-permute-start.3) | collective-permute-done | bytes 32800 | tf_op jit(solution)/shard_map/ppermute | solution.py:744
  12.5 1.8 %collective-permute-start.4 = (f32[8,8,128]{2,1,0:T(8,128)S(1)}, f32[8,8,128]{2,1,0:T(8,128)S(1)}, u32[]{:S(2)}, u32[]{:S(2)}) collective-permute-start(f32[8,8,128]{2,1,0:T(8,128)S(1)} %collective-permute-done.3.refs_8_), channel_id=1, source_target_pairs={{16,0},{0,16},{17,1},{1,17},{18,2},{2,18},{19,3},{3,19},{20,4},{4,... | collective-permute-start | bytes 98312 | tf_op jit(solution)/shard_map/ppermute | solution.py:739
  14.3 0.0 collective-permute-start.1
  14.3 0.0 collective-permute-done.refs_5_
  14.3 0.5 %collective-permute-start.2 = (f32[5,8,128]{2,1,0:T(8,128)S(1)}, f32[5,8,128]{2,1,0:T(8,128)S(1)}, u32[]{:S(2)}, u32[]{:S(2)}) collective-permute-start(f32[5,8,128]{2,1,0:T(8,128)S(1)} %slice.4), channel_id=1, source_target_pairs={{0,1},{1,0},{2,3},{3,2},{4,5},{5,4},{6,7},{7,6},{8,9},{9,8},{10,11... | collective-permute-start | bytes 61448 | tf_op jit(solution)/shard_map/ppermute | solution.py:747
  14.8 0.7 %collective-permute-done.1.refs_6_ = f32[7,8,128]{2,1,0:T(8,128)S(1)} collective-permute-done((f32[7,8,128]{2,1,0:T(8,128)S(1)}, f32[7,8,128]{2,1,0:T(8,128)S(1)}, u32[]{:S(2)}, u32[]{:S(2)}) %collective-permute-start.1) | collective-permute-done | bytes 28704 | tf_op jit(solution)/shard_map/ppermute | solution.py:743
  15.5 2.5 %all-to-all-done.refs_0_ = f32[32,2,128]{2,1,0:T(2,128)S(1)} async-done(((f32[32,2,128]{2,1,0:T(2,128)}), f32[32,2,128]{2,1,0:T(2,128)S(1)}, u32[]{:S(2)}, u32[]{:S(2)}) %all-to-all-start) | async-done | bytes 32800 | tf_op jit(solution)/shard_map/all_to_all | solution.py:746
  18.0 0.0 collective-permute-done.4.refs_9_
  18.0 0.0 collective-permute-done.2.refs_7_
  18.0 0.9 %main.1 = (f32[3,4,8,128]{3,2,1,0:T(8,128)S(1)}, f32[3,4,8,128]{3,2,1,0:T(8,128)S(1)}, f32[32,2,128]{2,1,0:T(2,128)S(1)}) custom-call(f32[32,2,128]{2,1,0:T(2,128)S(1)} %all-to-all-done.refs_0_, f32[3,3,4,8,128]{4,3,2,1,0:T(8,128)S(1)} %get-tuple-element.16.refs_1_, f32[6,3,3,4,8,128]{5,4,3,2,1,0:T(8,128)S(1)} %get-tuple-element.17.refs_2_, ...), custom_call_target="tpu_custom_call" | custom-call | tf_op jit(solution)/shard_map/main/pallas_call | solution.py:750
  18.9 9.7 %all_to_all.10.sums_ref = f32[32,2,128]{2,1,0:T(2,128)S(1)} all-to-all(f32[32,2,128]{2,1,0:T(2,128)S(1)} %get-tuple-element.23), channel_id=1, replica_groups=mesh['gx'=2,'gy'=16] {'gx','gy'}, dimensions={0} | all-to-all | bytes 65536 | tf_op jit(solution)/shard_map/all_to_all | solution.py:763
  28.6 0.8 %after.1 = (f32[3,4,8,128]{3,2,1,0:T(8,128)}, f32[3,4,8,128]{3,2,1,0:T(8,128)}) custom-call(f32[32,2,128]{2,1,0:T(2,128)S(1)} %all_to_all.10.sums_ref, f32[3,4,8,128]{3,2,1,0:T(8,128)S(1)} %get-tuple-element.24.z_ref, f32[3,4,8,128]{3,2,1,0:T(8,128)S(1)} %get-tuple-element.25.residual_ref), custom_call_target="tpu_custom_call" | custom-call | tf_op jit(solution)/shard_map/after/pallas_call | solution.py:764
  (1 shorter events, 0.0 us)
Async XLA Ops:
  2.5 11.8 %collective-permute-start = (f32[68,8,128]{2,1,0:T(8,128)S(1)}, f32[68,8,128]{2,1,0:T(8,128)S(1)}, u32[]{:S(2)}, u32[]{:S(2)}) collective-permute-start(f32[68,8,128]{2,1,0:T(8,128)S(1)} %get-tuple-element.20), channel_id=1, source_target_pairs={{16,0},{0,16},{17,1},{1,17},{18,2},{2,18},{19,3},{3,19},{20,4},{4,... | collective-permute-start | bytes 835592 | tf_op jit(solution)/shard_map/ppermute | solution.py:739
  5.5 7.0 %collective-permute-start.3 = (f32[8,8,128]{2,1,0:T(8,128)S(1)}, f32[8,8,128]{2,1,0:T(8,128)S(1)}, u32[]{:S(2)}, u32[]{:S(2)}) collective-permute-start(f32[8,8,128]{2,1,0:T(8,128)S(1)} %get-tuple-element.22), channel_id=1, source_target_pairs={{0,16},{1,2},{2,1},{3,4},{4,3},{5,6},{6,5},{7,8},{8,7},{9,10},{10,... | collective-permute-start | bytes 98312 | tf_op jit(solution)/shard_map/ppermute | solution.py:744
  5.5 12.4 %all-to-all-start = ((f32[32,2,128]{2,1,0:T(2,128)}), f32[32,2,128]{2,1,0:T(2,128)S(1)}, u32[]{:S(2)}, u32[]{:S(2)}) async-start(f32[32,2,128]{2,1,0:T(2,128)} %get-tuple-element.15), calls=%async_computation | async-start | bytes 65536 | tf_op jit(solution)/shard_map/all_to_all | solution.py:746
  12.5 5.5 %collective-permute-start.4 = (f32[8,8,128]{2,1,0:T(8,128)S(1)}, f32[8,8,128]{2,1,0:T(8,128)S(1)}, u32[]{:S(2)}, u32[]{:S(2)}) collective-permute-start(f32[8,8,128]{2,1,0:T(8,128)S(1)} %collective-permute-done.3.refs_8_), channel_id=1, source_target_pairs={{16,0},{0,16},{17,1},{1,17},{18,2},{2,18},{19,3},{3,19},{20,4},{4,... | collective-permute-start | bytes 98312 | tf_op jit(solution)/shard_map/ppermute | solution.py:739
  14.3 1.2 %collective-permute-start.1 = (f32[7,8,128]{2,1,0:T(8,128)S(1)}, f32[7,8,128]{2,1,0:T(8,128)S(1)}, u32[]{:S(2)}, u32[]{:S(2)}) collective-permute-start(f32[7,8,128]{2,1,0:T(8,128)S(1)} %get-tuple-element.21), channel_id=1, source_target_pairs={{0,1},{1,0},{2,3},{3,2},{4,5},{5,4},{6,7},{7,6},{8,9},{9,8},{10,11... | collective-permute-start | bytes 86024 | tf_op jit(solution)/shard_map/ppermute | solution.py:743
  14.3 3.7 %collective-permute-start.2 = (f32[5,8,128]{2,1,0:T(8,128)S(1)}, f32[5,8,128]{2,1,0:T(8,128)S(1)}, u32[]{:S(2)}, u32[]{:S(2)}) collective-permute-start(f32[5,8,128]{2,1,0:T(8,128)S(1)} %slice.4), channel_id=1, source_target_pairs={{0,1},{1,0},{2,3},{3,2},{4,5},{5,4},{6,7},{7,6},{8,9},{9,8},{10,11... | collective-permute-start | bytes 61448 | tf_op jit(solution)/shard_map/ppermute | solution.py:747

commit v11 on v10

--- a/solution.py
+++ b/solution.py
@@ -658,7 +658,6 @@
 
 def after_kernel(sums_ref, z_ref, residual_ref, update_hbm, residual_hbm, update_out, sem, sems):
     copy = pltpu.make_async_copy(residual_ref, residual_hbm, sem)
-    copy.start()
     pair = jnp.sum(sums_ref[...], axis=0)
     both = jnp.sum(pair, axis=1, keepdims=True)
     step = both[0:1] / both[1:2]
@@ -667,6 +666,7 @@
         update_out[c] = z_ref[c] * step[None]
         copies.append(pltpu.make_async_copy(update_out.at[c], update_hbm.at[c], sems.at[c]))
         copies[-1].start()
+    copy.start()
     for each in [copy, *copies]:
         each.wait()
 

time: 29.6 us -> 29.6 us (level)
  no operation moved by 1% of the time
where the time goes in v11:
time: 29.6 us; the launch traced here: 29.4 us
  starting transfers between devices  10.6 us (36%)
  blocking collectives  9.71 us (33%)
  waiting for transfers between devices  4.95 us (17%)
  Pallas kernels  3.51 us (12%)
  between operations  0.67 us (2%)
    all_to_all x1, blocking collectives, body(): sums_all = lax.all_to_all(sums, ('gx', 'gy'), 0, 0)  9.71 us
    all_to_all x1, starting transfers between devices, body(): wells_all = lax.all_to_all(wells_part, ('gx', 'gy'), 0, 0)  5.19 us
    ppermute x2, starting transfers between devices, from_x(): lax.ppermute(values, 'gx', [((i + offset) % count_x, i) for i in range(co...  4.79 us
    all_to_all x1, waiting for transfers between devices, body(): wells_all = lax.all_to_all(wells_part, ('gx', 'gy'), 0, 0)  2.53 us
    pallas_call x1, Pallas kernels, body(): pl.pallas_call(functools.partial(before_kernel, count_x, count_y), in_spe...  1.82 us
    ppermute x1, waiting for transfers between devices, body(): yb_got = lax.ppermute(yb, ('gx', 'gy'), others)  1.73 us
    pallas_call x1, Pallas kernels, body(): pl.pallas_call(functools.partial(main_kernel, count_x, count_y, tuple(off...  0.88 us
    pallas_call x1, Pallas kernels, body(): pl.pallas_call(after_kernel, in_specs=[whole] * 3, out_specs=[anywhere] *...  0.8 us
  transfers between devices with their start and end apart: 6, of which 3 were waited for; matrix products, arithmetic and copies ran while one was open for 0% of the time, Pallas kernels for 0%

profile of v11, /device:TPU:0, one launch (start us, length us, event | category | flops | bytes accessed | tf_op | source)
XLA Modules:
  0.0 29.4 jit_solution(8124039503793775970)
XLA Ops:
  0.6 1.8 %before.1 = (f32[32,2,128]{2,1,0:T(2,128)}, f32[68,8,128]{2,1,0:T(8,128)S(1)}, f32[62,8,128]{2,1,0:T(8,128)S(1)}, f32[7,8,128]{2,1,0:T(8,128)S(1)}, f32[8,8,128]...) custom-call(f32[4,8,128]{2,1,0:T(8,128)} %refs_0_.1, ...), custom_call_target="tpu_custom_call" | custom-call | tf_op jit(solution)/shard_map/before/pallas_call | solution.py:711
  2.5 3.0 %collective-permute-start = (f32[68,8,128]{2,1,0:T(8,128)S(1)}, f32[68,8,128]{2,1,0:T(8,128)S(1)}, u32[]{:S(2)}, u32[]{:S(2)}) collective-permute-start(f32[68,8,128]{2,1,0:T(8,128)S(1)} %get-tuple-element.20), channel_id=1, source_target_pairs={{16,0},{0,16},{17,1},{1,17},{18,2},{2,18},{19,3},{3,19},{20,4},{4,... | collective-permute-start | bytes 835592 | tf_op jit(solution)/shard_map/ppermute | solution.py:739
  5.5 0.1 collective-permute-start.3
  5.5 5.2 %all-to-all-start = ((f32[32,2,128]{2,1,0:T(2,128)}), f32[32,2,128]{2,1,0:T(2,128)S(1)}, u32[]{:S(2)}, u32[]{:S(2)}) async-start(f32[32,2,128]{2,1,0:T(2,128)} %get-tuple-element.15), calls=%async_computation | async-start | bytes 65536 | tf_op jit(solution)/shard_map/all_to_all | solution.py:746
  10.7 1.7 %collective-permute-done.3.refs_8_ = f32[8,8,128]{2,1,0:T(8,128)S(1)} collective-permute-done((f32[8,8,128]{2,1,0:T(8,128)S(1)}, f32[8,8,128]{2,1,0:T(8,128)S(1)}, u32[]{:S(2)}, u32[]{:S(2)}) %collective-permute-start.3) | collective-permute-done | bytes 32800 | tf_op jit(solution)/shard_map/ppermute | solution.py:744
  12.5 1.8 %collective-permute-start.4 = (f32[8,8,128]{2,1,0:T(8,128)S(1)}, f32[8,8,128]{2,1,0:T(8,128)S(1)}, u32[]{:S(2)}, u32[]{:S(2)}) collective-permute-start(f32[8,8,128]{2,1,0:T(8,128)S(1)} %collective-permute-done.3.refs_8_), channel_id=1, source_target_pairs={{16,0},{0,16},{17,1},{1,17},{18,2},{2,18},{19,3},{3,19},{20,4},{4,... | collective-permute-start | bytes 98312 | tf_op jit(solution)/shard_map/ppermute | solution.py:739
  14.3 0.0 collective-permute-start.1
  14.3 0.0 collective-permute-done.refs_5_
  14.3 0.5 %collective-permute-start.2 = (f32[5,8,128]{2,1,0:T(8,128)S(1)}, f32[5,8,128]{2,1,0:T(8,128)S(1)}, u32[]{:S(2)}, u32[]{:S(2)}) collective-permute-start(f32[5,8,128]{2,1,0:T(8,128)S(1)} %slice.4), channel_id=1, source_target_pairs={{0,1},{1,0},{2,3},{3,2},{4,5},{5,4},{6,7},{7,6},{8,9},{9,8},{10,11... | collective-permute-start | bytes 61448 | tf_op jit(solution)/shard_map/ppermute | solution.py:747
  14.8 0.7 %collective-permute-done.1.refs_6_ = f32[7,8,128]{2,1,0:T(8,128)S(1)} collective-permute-done((f32[7,8,128]{2,1,0:T(8,128)S(1)}, f32[7,8,128]{2,1,0:T(8,128)S(1)}, u32[]{:S(2)}, u32[]{:S(2)}) %collective-permute-start.1) | collective-permute-done | bytes 28704 | tf_op jit(solution)/shard_map/ppermute | solution.py:743
  15.5 2.5 %all-to-all-done.refs_0_ = f32[32,2,128]{2,1,0:T(2,128)S(1)} async-done(((f32[32,2,128]{2,1,0:T(2,128)}), f32[32,2,128]{2,1,0:T(2,128)S(1)}, u32[]{:S(2)}, u32[]{:S(2)}) %all-to-all-start) | async-done | bytes 32800 | tf_op jit(solution)/shard_map/all_to_all | solution.py:746
  18.0 0.0 collective-permute-done.4.refs_9_
  18.0 0.0 collective-permute-done.2.refs_7_
  18.0 0.9 %main.1 = (f32[3,4,8,128]{3,2,1,0:T(8,128)S(1)}, f32[3,4,8,128]{3,2,1,0:T(8,128)S(1)}, f32[32,2,128]{2,1,0:T(2,128)S(1)}) custom-call(f32[32,2,128]{2,1,0:T(2,128)S(1)} %all-to-all-done.refs_0_, f32[3,3,4,8,128]{4,3,2,1,0:T(8,128)S(1)} %get-tuple-element.16.refs_1_, f32[6,3,3,4,8,128]{5,4,3,2,1,0:T(8,128)S(1)} %get-tuple-element.17.refs_2_, ...), custom_call_target="tpu_custom_call" | custom-call | tf_op jit(solution)/shard_map/main/pallas_call | solution.py:750
  18.9 9.7 %all_to_all.10.sums_ref = f32[32,2,128]{2,1,0:T(2,128)S(1)} all-to-all(f32[32,2,128]{2,1,0:T(2,128)S(1)} %get-tuple-element.23), channel_id=1, replica_groups=mesh['gx'=2,'gy'=16] {'gx','gy'}, dimensions={0} | all-to-all | bytes 65536 | tf_op jit(solution)/shard_map/all_to_all | solution.py:763
  28.6 0.8 %after.1 = (f32[3,4,8,128]{3,2,1,0:T(8,128)}, f32[3,4,8,128]{3,2,1,0:T(8,128)}) custom-call(f32[32,2,128]{2,1,0:T(2,128)S(1)} %all_to_all.10.sums_ref, f32[3,4,8,128]{3,2,1,0:T(8,128)S(1)} %get-tuple-element.24.z_ref, f32[3,4,8,128]{3,2,1,0:T(8,128)S(1)} %get-tuple-element.25.residual_ref), custom_call_target="tpu_custom_call" | custom-call | tf_op jit(solution)/shard_map/after/pallas_call | solution.py:764
  (1 shorter events, 0.0 us)
Async XLA Ops:
  2.5 11.8 %collective-permute-start = (f32[68,8,128]{2,1,0:T(8,128)S(1)}, f32[68,8,128]{2,1,0:T(8,128)S(1)}, u32[]{:S(2)}, u32[]{:S(2)}) collective-permute-start(f32[68,8,128]{2,1,0:T(8,128)S(1)} %get-tuple-element.20), channel_id=1, source_target_pairs={{16,0},{0,16},{17,1},{1,17},{18,2},{2,18},{19,3},{3,19},{20,4},{4,... | collective-permute-start | bytes 835592 | tf_op jit(solution)/shard_map/ppermute | solution.py:739
  5.5 7.0 %collective-permute-start.3 = (f32[8,8,128]{2,1,0:T(8,128)S(1)}, f32[8,8,128]{2,1,0:T(8,128)S(1)}, u32[]{:S(2)}, u32[]{:S(2)}) collective-permute-start(f32[8,8,128]{2,1,0:T(8,128)S(1)} %get-tuple-element.22), channel_id=1, source_target_pairs={{0,16},{1,2},{2,1},{3,4},{4,3},{5,6},{6,5},{7,8},{8,7},{9,10},{10,... | collective-permute-start | bytes 98312 | tf_op jit(solution)/shard_map/ppermute | solution.py:744
  5.5 12.4 %all-to-all-start = ((f32[32,2,128]{2,1,0:T(2,128)}), f32[32,2,128]{2,1,0:T(2,128)S(1)}, u32[]{:S(2)}, u32[]{:S(2)}) async-start(f32[32,2,128]{2,1,0:T(2,128)} %get-tuple-element.15), calls=%async_computation | async-start | bytes 65536 | tf_op jit(solution)/shard_map/all_to_all | solution.py:746
  12.5 5.5 %collective-permute-start.4 = (f32[8,8,128]{2,1,0:T(8,128)S(1)}, f32[8,8,128]{2,1,0:T(8,128)S(1)}, u32[]{:S(2)}, u32[]{:S(2)}) collective-permute-start(f32[8,8,128]{2,1,0:T(8,128)S(1)} %collective-permute-done.3.refs_8_), channel_id=1, source_target_pairs={{16,0},{0,16},{17,1},{1,17},{18,2},{2,18},{19,3},{3,19},{20,4},{4,... | collective-permute-start | bytes 98312 | tf_op jit(solution)/shard_map/ppermute | solution.py:739
  14.3 1.2 %collective-permute-start.1 = (f32[7,8,128]{2,1,0:T(8,128)S(1)}, f32[7,8,128]{2,1,0:T(8,128)S(1)}, u32[]{:S(2)}, u32[]{:S(2)}) collective-permute-start(f32[7,8,128]{2,1,0:T(8,128)S(1)} %get-tuple-element.21), channel_id=1, source_target_pairs={{0,1},{1,0},{2,3},{3,2},{4,5},{5,4},{6,7},{7,6},{8,9},{9,8},{10,11... | collective-permute-start | bytes 86024 | tf_op jit(solution)/shard_map/ppermute | solution.py:743
  14.3 3.7 %collective-permute-start.2 = (f32[5,8,128]{2,1,0:T(8,128)S(1)}, f32[5,8,128]{2,1,0:T(8,128)S(1)}, u32[]{:S(2)}, u32[]{:S(2)}) collective-permute-start(f32[5,8,128]{2,1,0:T(8,128)S(1)} %slice.4), channel_id=1, source_target_pairs={{0,1},{1,0},{2,3},{3,2},{4,5},{5,4},{6,7},{7,6},{8,9},{9,8},{10,11... | collective-permute-start | bytes 61448 | tf_op jit(solution)/shard_map/ppermute | solution.py:747
